TPU v7x, 256 devices: a whole 4x4x8 slice. The times are simulated.
256 devices in a mesh: gz: 8 (over y, core), xy: 32 (over z, x).
Axes of the slice: x: 4, y: 4, z: 8, core: 2. Of those that a mesh axis runs over, the one named last changes fastest.
Arguments:
- velocity: float32 [8192, 8, 8, 128], P(('gz', 'xy')), may hold values from -6 to 6
- offset: int32 [8192], P(('gz', 'xy')), may hold values from 0 to 3
- interp_weight: float32 [8192], P(('gz', 'xy')), may hold values from 0.5 to 2
- route: int32 [8192, 1], replicated, may hold values from 0 to 31; in each aligned block of 32 rows (0 to 31, 32 to 63, ...) at most 4 rows name the same one
- dest_slot: int32 [8192], replicated, may hold values from 0 to 15
- conductivity: float32 [128, 2048, 128], P('gz', 'xy'), may hold values from -20 to 20
Outputs:
- update: bfloat16 [128, 2048, 128], P(None, 'xy')
Inputs may be any that keep to these rules, and one draw needn't show every extreme that they name: `route`: in the records of one device (aligned blocks of 32 rows), no xy index is named more than 4 times, a bound that some block reaches.
All inputs are finite; a program needn't handle non-finite values.
Results may differ from a plain program's by a relative error of at most 0.0039.
Values may be sent and summed in bfloat16 or wider, within the bound.
No kernel may reach another device: no remote copies, remote signals or barrier semaphores. Data moves between devices by JAX's collectives and lax.ppermute only.
A program may use at most 64 MiB of HBM per device.

v0:
```python
import jax
import jax.numpy as jnp
from jax import lax
from jax.sharding import PartitionSpec as P

BZ = 8
BY = 8


smooth_taps = (1.0 / 16.0, 4.0 / 16.0, 6.0 / 16.0, 4.0 / 16.0, 1.0 / 16.0)
deriv_taps = (1.0 / 12.0, -8.0 / 12.0, 0.0, 8.0 / 12.0, -1.0 / 12.0)


def with_halo(array, sides, width):
    for axis, dim in sides:
        size, length = (lax.axis_size(axis), array.shape[dim])
        up = [(i, (i + 1) % size) for i in range(size - 1)]
        down = [(j, i) for i, j in up]
        last = lax.slice_in_dim(array, length - width, length, axis=dim)
        first = lax.slice_in_dim(array, 0, width, axis=dim)
        before = lax.ppermute(last, axis, up)
        after = lax.ppermute(first, axis, down)
        array = jnp.concatenate([before, array, after], axis=dim)
    return array


def taps_last(field, kernel):
    width = field.shape[-1]
    padded = jnp.pad(field, [(0, 0)] * (field.ndim - 1) + [(2, 2)])
    total = kernel[0] * padded[..., 0:width]
    for place in range(1, 5):
        if kernel[place] != 0.0:
            total = total + kernel[place] * padded[..., place : place + width]
    return total


def taps_along(field, kernel, axis):
    length = field.shape[axis] - 4
    total = kernel[0] * lax.slice_in_dim(field, 0, length, axis=axis)
    for place in range(1, 5):
        if kernel[place] != 0.0:
            total = total + kernel[place] * lax.slice_in_dim(
                field, place, place + length, axis=axis
            )
    return total


def grads(padded):
    axis_y = padded.ndim - 2
    axis_z = padded.ndim - 3
    smooth_x = taps_last(padded, smooth_taps)
    deriv_x = taps_last(padded, deriv_taps)
    grad_x = taps_along(taps_along(deriv_x, smooth_taps, axis_y), smooth_taps, axis_z)
    grad_y = taps_along(taps_along(smooth_x, deriv_taps, axis_y), smooth_taps, axis_z)
    grad_z = taps_along(taps_along(smooth_x, smooth_taps, axis_y), deriv_taps, axis_z)
    return (grad_x, grad_y, grad_z)


def cross_adjoint(grad_x, grad_y, grad_z):
    model_x, model_y, model_z = (grad_x[0], grad_y[0], grad_z[0])
    speed_x, speed_y, speed_z = (grad_x[1], grad_y[1], grad_z[1])
    cross_x = model_y * speed_z - model_z * speed_y
    cross_y = model_z * speed_x - model_x * speed_z
    cross_z = model_x * speed_y - model_y * speed_x
    adj_x = speed_y * cross_z - speed_z * cross_y
    adj_y = speed_z * cross_x - speed_x * cross_z
    adj_z = speed_x * cross_y - speed_y * cross_x
    return jnp.stack([adj_x, adj_y, adj_z])


def adjoint(padded):
    smooth_x = taps_last(padded[1:3], smooth_taps)
    deriv_x = taps_last(padded[0], deriv_taps)
    part_z = taps_along(smooth_x[1], smooth_taps, 1)
    part_rest = taps_along(smooth_x[0], deriv_taps, 1) + taps_along(deriv_x, smooth_taps, 1)
    return taps_along(part_z, deriv_taps, 0) + taps_along(part_rest, smooth_taps, 0)


def shifted_contrib(velocity, offset, interp_weight):
    width = velocity.shape[-1]
    padded = jnp.pad(velocity, ((0, 0), (0, 0), (0, 0), (0, 3)))
    moved = jnp.zeros_like(velocity)
    for step in range(4):
        moved = moved + jnp.where(
            (offset == step)[:, None, None, None], padded[..., step : step + width], 0.0
        )
    return (interp_weight[:, None, None, None] * moved).astype(jnp.bfloat16)


def local(velocity, offset, interp_weight, route, dest_slot, conductivity):
    sources = velocity.shape[0]
    depth, lateral_rows, width = conductivity.shape
    lateral_count = lax.axis_size("xy")
    column_count = lax.axis_size("gz")
    lateral = lax.axis_index("xy")
    column = lax.axis_index("gz")
    bricks = depth // BZ * (lateral_rows // BY)
    brick_cells = BZ * BY * width
    contrib = shifted_contrib(velocity, offset, interp_weight).reshape(sources, brick_cells)
    group_size = lateral_count * sources
    first_record = column * group_size
    group_route = lax.dynamic_slice_in_dim(route[:, 0], first_record, group_size)
    group_slot = lax.dynamic_slice_in_dim(dest_slot, first_record, group_size)
    brick_ids = jnp.arange(bricks, dtype=jnp.int32)
    select = (
        (group_route == lateral)[None, :] & (group_slot[None, :] == brick_ids[:, None])
    ).astype(jnp.bfloat16)
    blocks = jnp.dot(
        select,
        lax.all_gather(contrib, "xy", axis=0, tiled=True),
        preferred_element_type=jnp.float32,
    )
    vgrid = blocks.reshape(depth // BZ, lateral_rows // BY, BZ, BY, width)
    vgrid = vgrid.transpose(0, 2, 1, 3, 4).reshape(depth, lateral_rows, width)
    fields = jnp.stack([conductivity, vgrid])
    padded = with_halo(fields, (("gz", 1), ("xy", 2)), 2)
    adj = cross_adjoint(*grads(padded))
    adj_pad = with_halo(adj, (("gz", 1), ("xy", 2)), 2)
    gradient = -adjoint(adj_pad)
    total_cells = depth * column_count * lateral_rows * lateral_count * width
    local_sq = jnp.sum(gradient * gradient)
    total_sq = lax.psum(local_sq, ("gz", "xy"))
    scale = 1.0 / jnp.sqrt(total_sq / total_cells + 1e-06)
    slab = (-gradient * scale).astype(jnp.bfloat16)
    return lax.all_gather(slab, "gz", axis=0, tiled=True)


def solution(mesh):
    in_specs = (
        P(("gz", "xy"), None, None, None),
        P(("gz", "xy")),
        P(("gz", "xy")),
        P(),
        P(),
        P("gz", "xy", None),
    )
    out_specs = P(None, "xy", None)
    return jax.shard_map(local, mesh=mesh, in_specs=in_specs, out_specs=out_specs, check_vma=False)
```

profile of v0, /device:TPU:1, one launch (start us, length us, event | category | flops | bytes accessed | tf_op | source)
XLA Modules:
  0.0 328.4 jit_solution(12327179885347599746)
XLA Ops:
  6.5 0.7 broadcast_compare_fusion.3
  7.2 3.7 %fusion.20 = bf16[32,8,8,128]{3,2,1,0:T(8,128)(2,1)S(1)} fusion(f32[32,8,8,128]{3,2,1,0:T(8,128)} %param.6, f32[32]{0:T(128)} %param.8, pred[32]{0:T(512)(128)(4,1)S(1)} %get-tuple-element.28, pred[32]{0:T(512)(128)(4,1)S(1)} %get-tuple-element.29, pred[32]{0:T(512)(128)(4,1)S(1)} %get-tuple-element.27, pred[32]{0:T(512)(128)(4,1)S(1)} %get-tuple-element.26), kind=kLoop, calls=%fused_computation.46 | loop fusion | flops 2359296 | bytes 1573120 | tf_op jit(solution)/shard_map/convert_element_type | solution.py:87
  10.9 1.1 copy.11
  12.1 0.7 dynamic_slice.7
  12.8 0.7 compare_reduce_fusion
  13.5 142.7 %all-gather.3.cloned.1.call-done = bf16[1024,8192]{1,0:T(8,128)(2,1)} async-done(((bf16[32,8192]{1,0:T(8,128)(2,1)}), bf16[1024,8192]{1,0:T(8,128)(2,1)}) %all-gather.3.cloned.1.call-update) | async-done | bytes 16777232 | tf_op jit(solution)/shard_map/all_gather | solution.py:110
  156.2 8.0 %fusion.62 = f32[16,8192]{1,0:T(8,128)S(1)} fusion(bf16[1024,8192]{1,0:T(8,128)(2,1)} %all-gather.3.cloned.1.call-done, s32[1024]{0:T(1024)S(1)} %dynamic_slice.7, pred[1024]{0:T(1024)(128)(4,1)S(1)} %compare_reduce_fusion), kind=kOutput, calls=%fused_computation.143 | convolution fusion | flops 268468224 | bytes 17306624 | tf_op jit(solution)/shard_map/dot_general | solution.py:108
  164.4 4.0 %collective-permute-start = (f32[2,2,64,128]{3,2,1,0:T(8,128)S(1)}, f32[2,2,64,128]{3,2,1,0:T(8,128)S(1)}, u32[]{:S(2)}, u32[]{:S(2)}) collective-permute-start(f32[2,2,64,128]{3,2,1,0:T(8,128)S(1)} %get-tuple-element.24), channel_id=1, source_target_pairs={{0,32},{32,64},{64,96},{96,128},{128,160},{160,192},{192,224},{1,3... | collective-permute-start | bytes 393224 | tf_op jit(solution)/shard_map/ppermute | solution.py:21
  168.4 1.9 collective-permute-start.1
  170.4 4.3 %collective-permute-done.1 = f32[2,2,64,128]{3,2,1,0:T(8,128)S(1)} collective-permute-done((f32[2,2,64,128]{3,2,1,0:T(8,128)S(1)}, f32[2,2,64,128]{3,2,1,0:T(8,128)S(1)}, u32[]{:S(2)}, u32[]{:S(2)}) %collective-permute-start.1) | collective-permute-done | bytes 131104 | tf_op jit(solution)/shard_map/ppermute | solution.py:22
  174.8 1.9 collective-permute-start.2
  176.6 1.3 collective-permute-start.3
  177.9 3.4 %collective-permute-done.3 = f32[2,20,2,128]{3,2,1,0:T(2,128)S(1)} collective-permute-done((f32[2,20,2,128]{3,2,1,0:T(2,128)S(1)}, f32[2,20,2,128]{3,2,1,0:T(2,128)S(1)}, u32[]{:S(2)}, u32[]{:S(2)}) %collective-permute-start.3) | collective-permute-done | bytes 40992 | tf_op jit(solution)/shard_map/ppermute | solution.py:22
  181.5 3.1 multiply_add_fusion
  184.6 1.8 multiply_add_fusion.2
  188.1 3.2 collective-permute-start.4
  191.3 1.9 collective-permute-start.5
  193.2 0.7 collective-permute-done.4
  193.9 4.4 %collective-permute-done.5 = f32[3,2,64,128]{3,2,1,0:T(8,128)S(1)} collective-permute-done((f32[3,2,64,128]{3,2,1,0:T(8,128)S(1)}, f32[3,2,64,128]{3,2,1,0:T(8,128)S(1)}, u32[]{:S(2)}, u32[]{:S(2)}) %collective-permute-start.5) | collective-permute-done | bytes 196640 | tf_op jit(solution)/shard_map/ppermute | solution.py:22
  198.3 2.8 collective-permute-start.6
  201.1 1.5 collective-permute-start.7
  202.6 3.5 %collective-permute-done.7 = f32[3,20,2,128]{3,2,1,0:T(2,128)S(1)} collective-permute-done((f32[3,20,2,128]{3,2,1,0:T(2,128)S(1)}, f32[3,20,2,128]{3,2,1,0:T(2,128)S(1)}, u32[]{:S(2)}, u32[]{:S(2)}) %collective-permute-start.7) | collective-permute-done | bytes 61472 | tf_op jit(solution)/shard_map/ppermute | solution.py:22
  206.1 0.3 pad_maximum_fusion
  206.5 1.6 fusion.4
  208.3 0.8 fusion.37
  209.1 0.4 fusion.49
  209.5 0.7 fusion.42
  210.2 0.9 multiply_reduce_fusion
  211.1 81.6 %psum.7 = f32[]{:T(128)} all-reduce(f32[]{:T(128)} %get-tuple-element.5), channel_id=1, replica_groups=mesh['gz'=8,'xy'=32] {'gz','xy'}, use_global_device_ids=true, to_apply=%region_1.2 | all-reduce | flops 1 | bytes 8 | tf_op jit(solution)/shard_map/psum | solution.py:122
  293.3 0.8 multiply_convert_fusion
  294.1 24.4 %all-gather.5.cloned.1.call-done = bf16[128,64,128]{2,1,0:T(8,128)(2,1)} async-done(((bf16[16,64,128]{2,1,0:T(8,128)(2,1)}), bf16[128,64,128]{2,1,0:T(8,128)(2,1)}) %all-gather.5.cloned.1.call-update) | async-done | bytes 2097168 | tf_op jit(solution)/shard_map/all_gather | solution.py:125
  318.5 3.1 copy.13
  (24 shorter events, 2.3 us)
Async XLA Ops:
  6.5 149.7 %all-gather.3.cloned.1.call-start = ((), (), s32[]{:S(2)}) async-start(), calls=%async_computation | async-start | bytes 17301504 | tf_op jit(solution)/shard_map/all_gather | solution.py:110
  12.1 306.4 %all-gather.5.cloned.1.call-start = ((), (), s32[]{:S(2)}) async-start(), calls=%async_computation.1 | async-start | bytes 2359296 | tf_op jit(solution)/shard_map/all_gather | solution.py:125
  13.5 150.8 %copy-start = (f32[16,64,128]{2,1,0:T(8,128)S(1)}, f32[16,64,128]{2,1,0:T(8,128)}, u32[]{:S(2)}) copy-start(f32[16,64,128]{2,1,0:T(8,128)} %param.11) | copy-start | bytes 1572868
  164.4 6.0 %collective-permute-start = (f32[2,2,64,128]{3,2,1,0:T(8,128)S(1)}, f32[2,2,64,128]{3,2,1,0:T(8,128)S(1)}, u32[]{:S(2)}, u32[]{:S(2)}) collective-permute-start(f32[2,2,64,128]{3,2,1,0:T(8,128)S(1)} %get-tuple-element.24), channel_id=1, source_target_pairs={{0,32},{32,64},{64,96},{96,128},{128,160},{160,192},{192,224},{1,3... | collective-permute-start | bytes 393224 | tf_op jit(solution)/shard_map/ppermute | solution.py:21
  168.4 6.3 %collective-permute-start.1 = (f32[2,2,64,128]{3,2,1,0:T(8,128)S(1)}, f32[2,2,64,128]{3,2,1,0:T(8,128)S(1)}, u32[]{:S(2)}, u32[]{:S(2)}) collective-permute-start(f32[2,2,64,128]{3,2,1,0:T(8,128)S(1)} %get-tuple-element.25), channel_id=1, source_target_pairs={{32,0},{64,32},{96,64},{128,96},{160,128},{192,160},{224,192},{33,... | collective-permute-start | bytes 393224 | tf_op jit(solution)/shard_map/ppermute | solution.py:22
  174.8 3.2 collective-permute-start.2
  176.6 4.7 %collective-permute-start.3 = (f32[2,20,2,128]{3,2,1,0:T(2,128)S(1)}, f32[2,20,2,128]{3,2,1,0:T(2,128)S(1)}, u32[]{:S(2)}, u32[]{:S(2)}) collective-permute-start(f32[2,20,2,128]{3,2,1,0:T(2,128)S(1)} %get-tuple-element.23), channel_id=1, source_target_pairs={{1,0},{2,1},{3,2},{4,3},{5,4},{6,5},{7,6},{8,7},{9,8},{10,9},{11,1... | collective-permute-start | bytes 122888 | tf_op jit(solution)/shard_map/ppermute | solution.py:22
  188.1 5.8 %collective-permute-start.4 = (f32[3,2,64,128]{3,2,1,0:T(8,128)S(1)}, f32[3,2,64,128]{3,2,1,0:T(8,128)S(1)}, u32[]{:S(2)}, u32[]{:S(2)}) collective-permute-start(f32[3,2,64,128]{3,2,1,0:T(8,128)S(1)} %get-tuple-element.14), channel_id=1, source_target_pairs={{0,32},{32,64},{64,96},{96,128},{128,160},{160,192},{192,224},{1,3... | collective-permute-start | bytes 589832 | tf_op jit(solution)/shard_map/ppermute | solution.py:21
  191.3 7.0 %collective-permute-start.5 = (f32[3,2,64,128]{3,2,1,0:T(8,128)S(1)}, f32[3,2,64,128]{3,2,1,0:T(8,128)S(1)}, u32[]{:S(2)}, u32[]{:S(2)}) collective-permute-start(f32[3,2,64,128]{3,2,1,0:T(8,128)S(1)} %get-tuple-element.15), channel_id=1, source_target_pairs={{32,0},{64,32},{96,64},{128,96},{160,128},{192,160},{224,192},{33,... | collective-permute-start | bytes 589832 | tf_op jit(solution)/shard_map/ppermute | solution.py:22
  198.3 4.3 %collective-permute-start.6 = (f32[3,20,2,128]{3,2,1,0:T(2,128)S(1)}, f32[3,20,2,128]{3,2,1,0:T(2,128)S(1)}, u32[]{:S(2)}, u32[]{:S(2)}) collective-permute-start(f32[3,20,2,128]{3,2,1,0:T(2,128)S(1)} %get-tuple-element.12), channel_id=1, source_target_pairs={{0,1},{1,2},{2,3},{3,4},{4,5},{5,6},{6,7},{7,8},{8,9},{9,10},{10,1... | collective-permute-start | bytes 184328 | tf_op jit(solution)/shard_map/ppermute | solution.py:21
  201.1 5.0 %collective-permute-start.7 = (f32[3,20,2,128]{3,2,1,0:T(2,128)S(1)}, f32[3,20,2,128]{3,2,1,0:T(2,128)S(1)}, u32[]{:S(2)}, u32[]{:S(2)}) collective-permute-start(f32[3,20,2,128]{3,2,1,0:T(2,128)S(1)} %get-tuple-element.13), channel_id=1, source_target_pairs={{1,0},{2,1},{3,2},{4,3},{5,4},{6,5},{7,6},{8,7},{9,8},{10,9},{11,1... | collective-permute-start | bytes 184328 | tf_op jit(solution)/shard_map/ppermute | solution.py:22
Sparse Core Ops, SparseCore 0:
  12.2 143.9 all-gather.2
  294.2 24.2 all-gather.4
where the time goes:
time: 329 us; the launch traced here: 328 us
  waiting for transfers between devices  183 us (56%)
  blocking collectives  81.6 us (25%)
  starting transfers between devices  18.6 us (6%)
  other arithmetic  17.3 us (5%)
  between operations  14.3 us (4%)
  matrix products  8.04 us (2%)
  local copies, waits for them, and re-layouts  5.2 us (2%)
    all_gather x1, waiting for transfers between devices, local(): lax.all_gather(contrib, 'xy', axis=0, tiled=True)  143 us
    psum x1, blocking collectives, local(): total_sq = lax.psum(local_sq, ('gz', 'xy'))  81.6 us
    all_gather x1, waiting for transfers between devices, local(): return lax.all_gather(slab, 'gz', axis=0, tiled=True)  24.4 us
    ppermute x4, waiting for transfers between devices, with_halo(): after = lax.ppermute(first, axis, down)  15.7 us
    ppermute x4, starting transfers between devices, with_halo(): before = lax.ppermute(last, axis, up)  11.9 us
    dot_general x1, matrix products, local(): jnp.dot(select, lax.all_gather(contrib, 'xy', axis=0, tiled=True), prefer...  8.04 us
    ppermute x4, starting transfers between devices, with_halo(): after = lax.ppermute(first, axis, down)  6.61 us
  transfers between devices with their start and end apart: 10, of which 7 were waited for; matrix products, arithmetic and copies ran while one was open for 0% of the time, Pallas kernels for 0%

commit v1 on v0

v1 whole, which is shorter than its diff:
```python
import functools

import jax
import jax.numpy as jnp
from jax import lax
from jax.experimental import pallas as pl
from jax.experimental.pallas import tpu as pltpu
from jax.sharding import PartitionSpec as P

F32 = jnp.float32
BF16 = jnp.bfloat16
VMEM_LIMIT = 40 * 1024 * 1024
CAP = 4


def params():
    return pltpu.CompilerParams(vmem_limit_bytes=VMEM_LIMIT)


def vspec():
    return pl.BlockSpec(memory_space=pltpu.VMEM)


def sspec():
    return pl.BlockSpec(memory_space=pltpu.SMEM)


def sds(shape, dtype):
    return jax.ShapeDtypeStruct(shape, dtype)


def pack_kernel(vel, off, wt, route_any, route, slot, send, code, route_s, count, sem):
    g = lax.axis_index("gz")
    d = lax.axis_index("xy")
    rows = pl.ds(pl.multiple_of(g * 8, 8), 8)
    copy = pltpu.make_async_copy(route_any.at[rows], route_s, sem)
    copy.start()
    lane = lax.broadcasted_iota(jnp.int32, (8, 128), 1) % 32
    mine = (route[rows, :] == d).astype(jnp.int32)
    upto = mine
    for step in (1, 2, 4, 8, 16):
        upto = upto + jnp.where(lane >= step, pltpu.roll(upto, step, 1), 0)
    rank = upto - mine
    word = jnp.where(mine > 0, (slot[rows, :] + 1) << (5 * rank), 0)
    for step in (1, 2, 4, 8, 16):
        word = word + jnp.where(lane >= step, pltpu.roll(word, step, 1), 0)
    code[...] = word
    for i in range(32):
        count[i] = 0
    copy.wait()
    row = d // 4
    first = (d % 4) * 32
    x = lax.broadcasted_iota(jnp.int32, (64, 128), 1)

    def one(r, carry):
        dest = route_s[row, first + r]
        k = count[dest]
        count[dest] = k + 1
        o = off[r]
        v = vel[r].reshape(64, 128)
        moved = jnp.where(x < 128 - o, pltpu.roll(v, (128 - o) % 128, 1), 0.0)
        send[dest * CAP + k] = (moved * wt[r]).astype(BF16)
        return carry

    lax.fori_loop(0, 32, one, 0)


def pack(velocity, offset, weight, route, slot):
    return pl.pallas_call(
        pack_kernel,
        out_shape=(sds((32 * CAP, 64, 128), BF16), sds((8, 128), jnp.int32)),
        in_specs=[vspec(), sspec(), sspec(), pl.BlockSpec(memory_space=pl.ANY), vspec(), vspec()],
        out_specs=(vspec(), vspec()),
        scratch_shapes=[
            pltpu.SMEM((8, 128), jnp.int32),
            pltpu.SMEM((32,), jnp.int32),
            pltpu.SemaphoreType.DMA,
        ],
        compiler_params=params(),
        name="pack",
    )(velocity, offset, weight, route, route, slot)


def pair_rows(block):
    n = block.shape[0] // 2
    return jnp.stack(
        [jnp.concatenate([block[2 * i], block[2 * i + 1]], axis=0) for i in range(n)]
    )


def combine_kernel(recv, code, cond, v, z_a, z_b, y_own):
    g = lax.axis_index("gz")
    d = lax.axis_index("xy")
    v[...] = jnp.zeros_like(v)

    def source(s, carry):
        word = code[s // 4, (s % 4) * 32 + 31]
        for k in range(CAP):
            j = ((word >> (5 * k)) & 31) - 1

            @pl.when(j >= 0)
            def _():
                z0 = pl.multiple_of((j // 8) * 8, 8)
                y0 = pl.multiple_of((j % 8) * 8, 8)
                block = recv[s * CAP + k].astype(F32).reshape(8, 8, 128)
                v[pl.ds(z0, 8), pl.ds(y0, 8), :] += block

        return carry

    lax.fori_loop(0, 32, source, 0)
    even = g % 2 == 0
    z_hi = jnp.where(even, 12, 0)
    z_lo = 12 - z_hi
    y_even = d % 2 == 0
    for f, field in enumerate((cond, v)):
        z_a[f] = field[pl.ds(z_hi, 4)]
        z_b[f] = field[pl.ds(z_lo, 4)]
        lo = pair_rows(field[:, 0:8, :][:, 0:4])
        hi = pair_rows(field[:, 56:64, :][:, 4:8])
        y_own[0, f] = jnp.where(y_even, hi, lo)
        y_own[1, f] = jnp.where(y_even, lo, hi)


def combine(recv, code, cond):
    return pl.pallas_call(
        combine_kernel,
        out_shape=(
            sds((16, 64, 128), F32),
            sds((2, 4, 64, 128), F32),
            sds((2, 4, 64, 128), F32),
            sds((2, 2, 8, 8, 128), F32),
        ),
        in_specs=[vspec(), sspec(), vspec()],
        out_specs=(vspec(),) * 4,
        compiler_params=params(),
        name="combine",
    )(recv, code, cond)


def strips_kernel(y_own, r_a, r_b, y_c, y_d):
    d = lax.axis_index("xy")
    y_even = d % 2 == 0
    for f in range(2):
        y_c[f, 0:8] = y_own[0, f]
        y_d[f, 0:8] = y_own[1, f]
        for i, r in enumerate((r_a, r_b)):
            lo = pair_rows(r[f, :, 0:8, :][:, 0:4])
            hi = pair_rows(r[f, :, 56:64, :][:, 4:8])
            at = slice(8 + 2 * i, 10 + 2 * i)
            y_c[f, at] = jnp.where(y_even, hi, lo)
            y_d[f, at] = jnp.where(y_even, lo, hi)


def strips(y_own, r_a, r_b):
    return pl.pallas_call(
        strips_kernel,
        out_shape=(sds((2, 12, 8, 128), F32),) * 2,
        in_specs=[vspec()] * 3,
        out_specs=(vspec(),) * 2,
        compiler_params=params(),
        name="strips",
    )(y_own, r_a, r_b)


def split3(x):
    hi = x.astype(BF16)
    rest = x - hi.astype(F32)
    mid = rest.astype(BF16)
    lo = (rest - mid.astype(F32)).astype(BF16)
    return hi, mid, lo


def band(taps):
    i = lax.broadcasted_iota(jnp.int32, (128, 128), 0)
    j = lax.broadcasted_iota(jnp.int32, (128, 128), 1)
    m = jnp.zeros((128, 128), F32)
    for place, tap in enumerate(taps):
        if tap:
            m = jnp.where(i - j == place - 2, F32(tap), m)
    return m.astype(BF16)


S_TAPS = (1.0, 4.0, 6.0, 4.0, 1.0)
D_TAPS = (1.0, -8.0, 0.0, 8.0, -1.0)
NORM = 1.0 / (16.0 * 16.0 * 12.0)


def smooth5(a):
    return (a[0] + a[4]) + 4.0 * (a[1] + a[3]) + 6.0 * a[2]


def deriv5(a):
    return (a[0] - a[4]) + 8.0 * (a[3] - a[1])


def dot(a, b):
    return jnp.dot(a, b, preferred_element_type=F32)


def stencil_kernel(cond, v, r_a, r_b, q_c, q_d, out, total, ext, sx, dx, adj, mid_u, mid_t):
    g = lax.axis_index("gz")
    d = lax.axis_index("xy")
    even = g % 2 == 0
    y_even = d % 2 == 0
    at_a = jnp.where(even, 20, 0)
    at_b = 20 - at_a
    low_in = (g > 0).astype(F32)
    high_in = (g < 7).astype(F32)
    keep_a = jnp.where(even, high_in, low_in)
    keep_b = jnp.where(even, low_in, high_in)
    left_in = (d > 0).astype(F32)
    right_in = (d < 31).astype(F32)
    zeros4 = jnp.zeros((4, 128), F32)
    for f, field in enumerate((cond, v)):
        ext[f, 4:20, 8:72, :] = field[...]
        ext[f, pl.ds(at_a, 4), 8:72, :] = r_a[f] * keep_a
        ext[f, pl.ds(at_b, 4), 8:72, :] = r_b[f] * keep_b
        for z in range(24):
            c = q_c[f, z // 2]
            e = q_d[f, z // 2]
            lo = jnp.where(y_even, e, c)[4 * (z % 2) : 4 * (z % 2) + 4] * left_in
            hi = jnp.where(y_even, c, e)[4 * (z % 2) : 4 * (z % 2) + 4] * right_in
            if z < 16:
                place, keep = z + 4, 1.0
            elif z < 20:
                place, keep = at_a + (z - 16), keep_a
            else:
                place, keep = at_b + (z - 20), keep_b
            ext[f, place, 0:8, :] = jnp.concatenate([zeros4, lo * keep], axis=0)
            ext[f, place, 72:80, :] = jnp.concatenate([hi * keep, zeros4], axis=0)

    weights = jnp.concatenate([band(S_TAPS), band(D_TAPS)], axis=1)

    def along_x(i, carry):
        f = i // 24
        z = i % 24
        h, m, l = split3(ext[f, z])
        both = dot(h, weights) + dot(m, weights) + dot(l, weights)
        sx[f, z] = both[:, 0:128]
        dx[f, z] = both[:, 128:256]
        return carry

    lax.fori_loop(0, 48, along_x, 0)

    def along_y(i, carry):
        f = i // 24
        z = i % 24
        s = sx[f, z]
        t = dx[f, z]
        ss = [pltpu.roll(s, sh % 80, 0) for sh in (2, 1, 0, -1, -2)]
        tt = [pltpu.roll(t, sh % 80, 0) for sh in (2, 1, 0, -1, -2)]
        dx[f, z] = smooth5(tt)
        sx[f, z] = deriv5(ss)
        ext[f, z] = smooth5(ss)
        return carry

    lax.fori_loop(0, 48, along_y, 0)

    row = lax.broadcasted_iota(jnp.int32, (8, 128), 0)

    def cross(t, carry):
        y0 = pl.multiple_of(t * 8, 8)
        y = row + (y0 - 8)
        inside = jnp.where((y >= 0) | (d > 0), NORM, 0.0)
        inside = jnp.where((y < 64) | (d < 31), inside, 0.0)
        tile = pl.ds(y0, 8)
        for z in range(20):
            scale = inside
            if z < 2:
                scale = inside * low_in
            if z >= 18:
                scale = inside * high_in
            grad = []
            for f in range(2):
                gx = smooth5([dx[f, z + i, tile, :] for i in range(5)]) * scale
                gy = smooth5([sx[f, z + i, tile, :] for i in range(5)]) * scale
                gz = deriv5([ext[f, z + i, tile, :] for i in range(5)]) * scale
                grad.append((gx, gy, gz))
            (mx, my, mz), (vx, vy, vz) = grad
            cx = my * vz - mz * vy
            cy = mz * vx - mx * vz
            cz = mx * vy - my * vx
            adj[0, z, tile, :] = vy * cz - vz * cy
            adj[1, z, tile, :] = vz * cx - vx * cz
            adj[2, z, tile, :] = vx * cy - vy * cx
        return carry

    lax.fori_loop(0, 10, cross, 0)

    def back_yz(z, carry):
        p = smooth5([adj[0, z + i] for i in range(5)])
        q = smooth5([adj[1, z + i] for i in range(5)])
        r = deriv5([adj[2, z + i] for i in range(5)])
        sh = lambda a: [pltpu.roll(a, s % 80, 0) for s in (2, 1, 0, -1, -2)]
        mid_u[z] = smooth5(sh(p))[8:72]
        mid_t[z] = (deriv5(sh(q)) + smooth5(sh(r)))[8:72]
        return carry

    lax.fori_loop(0, 16, back_yz, 0)

    w_s = band(S_TAPS)
    w_d = band(D_TAPS)
    w = jnp.concatenate([w_d, w_s], axis=0)
    total[...] = jnp.zeros_like(total)

    def back_x(z, carry):
        us = split3(mid_u[z])
        ts = split3(mid_t[z])
        acc = sum(dot(jnp.concatenate([a, b], axis=1), w) for a, b in zip(us, ts))
        acc = acc * NORM
        out[z] = acc.astype(BF16)
        total[...] += jnp.sum((acc * acc).reshape(8, 8, 128), axis=0)
        return carry

    lax.fori_loop(0, 16, back_x, 0)
    total[...] = jnp.broadcast_to(jnp.sum(total[...], axis=0, keepdims=True), (8, 128))


def stencil(cond, v, r_a, r_b, q_c, q_d):
    return pl.pallas_call(
        stencil_kernel,
        out_shape=(sds((16, 64, 128), BF16), sds((8, 128), F32)),
        in_specs=[vspec()] * 6,
        out_specs=(vspec(),) * 2,
        scratch_shapes=[
            pltpu.VMEM((2, 24, 80, 128), F32),
            pltpu.VMEM((2, 24, 80, 128), F32),
            pltpu.VMEM((2, 24, 80, 128), F32),
            pltpu.VMEM((3, 20, 80, 128), F32),
            pltpu.VMEM((16, 64, 128), F32),
            pltpu.VMEM((16, 64, 128), F32),
        ],
        compiler_params=params(),
        name="stencil",
    )(cond, v, r_a, r_b, q_c, q_d)


def scale_kernel(cells, sums, *refs):
    pieces, out = refs[:-1], refs[-1]
    g = lax.axis_index("gz")
    total = jnp.sum(sums[...], axis=0, keepdims=True)
    total = jnp.sum(total, axis=1, keepdims=True)
    scale = 1.0 / jnp.sqrt(total / cells + 1e-06)
    scale = jnp.broadcast_to(scale, (64, 128))
    for k, piece in enumerate(pieces):
        base = (g ^ k) * 16
        for z in range(16):
            out[base + z] = (piece[z].astype(F32) * scale).astype(BF16)


def scaled(cells, sums, pieces):
    return pl.pallas_call(
        functools.partial(scale_kernel, cells),
        out_shape=sds((128, 64, 128), BF16),
        in_specs=[vspec()] * (1 + len(pieces)),
        out_specs=vspec(),
        compiler_params=params(),
        name="scale",
    )(sums, *pieces)


def swap_odd(count):
    return [(i, (i + 1) % count if i % 2 else (i - 1) % count) for i in range(count)]


def swap_even(count):
    return [(i, i ^ 1) for i in range(count)]


def local(velocity, offset, interp_weight, route, dest_slot, conductivity):
    n_g = lax.axis_size("gz")
    n_x = lax.axis_size("xy")
    send, code = pack(
        velocity, offset, interp_weight, route.reshape(64, 128), dest_slot.reshape(64, 128)
    )
    recv = lax.all_to_all(
        send.reshape(n_x, CAP * 64, 128), "xy", split_axis=0, concat_axis=0, tiled=True
    )
    v, z_a, z_b, y_own = combine(recv.reshape(n_x * CAP, 64, 128), code, conductivity)
    r_a = lax.ppermute(z_a, "gz", swap_even(n_g))
    r_b = lax.ppermute(z_b, "gz", swap_odd(n_g))
    y_c, y_d = strips(y_own, r_a, r_b)
    q_c = lax.ppermute(y_c, "xy", swap_even(n_x))
    q_d = lax.ppermute(y_d, "xy", swap_odd(n_x))
    grad, total = stencil(conductivity, v, r_a, r_b, q_c, q_d)
    pieces = [grad]
    for k in range(1, n_g):
        pieces.append(lax.ppermute(grad, "gz", [(i, i ^ k) for i in range(n_g)]))
    part = jnp.broadcast_to(total[0:1], (n_x, 128))
    part = lax.all_to_all(part, "xy", 0, 0, tiled=True)
    part = jnp.broadcast_to(jnp.sum(part, axis=0, keepdims=True), (n_g, 128))
    part = lax.all_to_all(part, "gz", 0, 0, tiled=True)
    cells = float(n_g * n_x * 16 * 64 * 128)
    return scaled(cells, part, pieces)


def solution(mesh):
    in_specs = (
        P(("gz", "xy"), None, None, None),
        P(("gz", "xy")),
        P(("gz", "xy")),
        P(),
        P(),
        P("gz", "xy", None),
    )
    out_specs = P(None, "xy", None)
    return jax.shard_map(local, mesh=mesh, in_specs=in_specs, out_specs=out_specs, check_vma=False)
```

time: 329 us -> 159 us (0.48)
  waiting for transfers between devices: 183 us -> 31.2 us
  Pallas kernels: 0 us -> 24.9 us
  other arithmetic: 17.3 us -> 0.02 us
  between operations: 14.3 us -> 0.07 us
  matrix products: 8.04 us -> 0 us
  starting transfers between devices: 18.6 us -> 15.1 us
    all_gather x2 -> x0, waiting for transfers between devices: 167 us -> none  [the longest x1 143 us: local(): lax.all_gather(contrib, 'xy', axis=0, tiled=True)]
    all_to_all x0 -> x3, blocking collectives: none -> 83 us  [the longest x1 60.5 us: local(): lax.all_to_all(send.reshape(n_x, CAP * 64, 128), 'xy', split_axis=0, conc...]
    psum x1 -> x0, blocking collectives: 81.6 us -> none  [local(): total_sq = lax.psum(local_sq, ('gz', 'xy'))]
    pallas_call x0 -> x5, Pallas kernels: none -> 24.9 us  [the longest x1 16.9 us: stencil(): pl.pallas_call(stencil_kernel, out_shape=(sds((16, 64, 128), BF16), sds((...]
    ppermute x8 -> x11, waiting for transfers between devices: 16.3 us -> 31.2 us  [the longest x7 20 us: local(): pieces.append(lax.ppermute(grad, 'gz', [(i, i ^ k) for i in range(n_g)]))]
    add x9 -> x0, other arithmetic: 9.1 us -> none  [the longest x3 5.51 us: taps_last(): total = total + kernel[place] * padded[..., place:place + width]]
    dot_general x1 -> x0, matrix products: 8.04 us -> none  [local(): jnp.dot(select, lax.all_gather(contrib, 'xy', axis=0, tiled=True), prefer...]
    convert_element_type x2 -> x0, other arithmetic: 4.46 us -> none  [the longest x1 3.69 us: shifted_contrib(): return (interp_weight[:, None, None, None] * moved).astype(jnp.bfloat16)]
  transfers between devices with their start and end apart: 10 -> 11, of which waited for: 7 -> 5; matrix products, arithmetic and copies ran while one was open for 0% -> 0% of each run, Pallas kernels for 0% -> 0%
where the time goes in v1:
time: 159 us; the launch traced here: 158 us
  blocking collectives  83 us (52%)
  waiting for transfers between devices  31.2 us (20%)
  Pallas kernels  24.9 us (16%)
  starting transfers between devices  15.1 us (9%)
  local copies, waits for them, and re-layouts  4.08 us (3%)
    all_to_all x1, blocking collectives, local(): lax.all_to_all(send.reshape(n_x, CAP * 64, 128), 'xy', split_axis=0, conc...  60.5 us
    ppermute x7, waiting for transfers between devices, local(): pieces.append(lax.ppermute(grad, 'gz', [(i, i ^ k) for i in range(n_g)]))  20 us
    pallas_call x1, Pallas kernels, stencil(): pl.pallas_call(stencil_kernel, out_shape=(sds((16, 64, 128), BF16), sds((...  16.9 us
    all_to_all x1, blocking collectives, local(): part = lax.all_to_all(part, 'xy', 0, 0, tiled=True)  12.6 us
    all_to_all x1, blocking collectives, local(): part = lax.all_to_all(part, 'gz', 0, 0, tiled=True)  9.89 us
    ppermute x7, starting transfers between devices, local(): pieces.append(lax.ppermute(grad, 'gz', [(i, i ^ k) for i in range(n_g)]))  8.96 us
    ppermute x1, waiting for transfers between devices, local(): r_b = lax.ppermute(z_b, 'gz', swap_odd(n_g))  4.82 us
    ppermute x1, waiting for transfers between devices, local(): q_d = lax.ppermute(y_d, 'xy', swap_odd(n_x))  4.78 us
  transfers between devices with their start and end apart: 11, of which 5 were waited for; matrix products, arithmetic and copies ran while one was open for 0% of the time, Pallas kernels for 0%

profile of v1, /device:TPU:1, one launch (start us, length us, event | category | flops | bytes accessed | tf_op | source)
XLA Modules:
  0.0 158.4 jit_solution(12552127316583617775)
XLA Ops:
  0.0 1.2 copy-done.1
  1.2 0.8 copy-done.2
  2.0 0.8 copy-done.3
  2.7 0.7 copy-done.4
  3.4 0.7 copy-done.5
  4.1 3.8 %pack.1 = (bf16[128,64,128]{2,1,0:T(8,128)(2,1)S(1)}, s32[8,128]{1,0:T(8,128)S(1)}) custom-call(f32[32,8,8,128]{3,2,1,0:T(8,128)S(1)} %copy-done.1, s32[32]{0:T(128)S(1)} %copy-done.4, f32[32]{0:T(128)S(1)} %copy-done.5, s32[64,128]{1,0:T(8,128)S(1)} %bitcast.10, s32[64,128]{1,0:T(8,128)S(1)} %bitcast.11, s32[64,128]{1,0:T(8,128)S(1)} %bitcast.12), custom_call_target="tpu_custom_call" | custom-call | tf_op jit(solution)/shard_map/pack/pallas_call | solution.py:69
  7.9 0.0 copy-start
  7.9 60.5 %all_to_all.19 = bf16[32,256,128]{2,1,0:T(8,128)(2,1)S(1)} all-to-all(bf16[32,256,128]{2,1,0:T(8,128)(2,1)S(1)} %bitcast.9), channel_id=1, replica_groups=mesh['gz'=8,'xy'=32] {'xy'}, dimensions={0} | all-to-all | bytes 4194304 | tf_op jit(solution)/shard_map/all_to_all | solution.py:376
  68.4 2.3 %combine.1 = (f32[16,64,128]{2,1,0:T(8,128)S(1)}, f32[2,4,64,128]{3,2,1,0:T(8,128)S(1)}, f32[2,4,64,128]{3,2,1,0:T(8,128)S(1)}, f32[2,2,8,8,128]{4,3,2,1,0:T(8,128)S(1)}) custom-call(bf16[128,64,128]{2,1,0:T(8,128)(2,1)S(1)} %bitcast.8, s32[8,128]{1,0:T(8,128)S(1)} %get-tuple-element.16.code, f32[16,64,128]{2,1,0:T(8,128)S(1)} %copy-done), custom_call_target="tpu_custom_call" | custom-call | tf_op jit(solution)/shard_map/combine/pallas_call | solution.py:125
  70.7 2.9 %collective-permute-start = (f32[2,4,64,128]{3,2,1,0:T(8,128)S(1)}, f32[2,4,64,128]{3,2,1,0:T(8,128)S(1)}, u32[]{:S(2)}, u32[]{:S(2)}) collective-permute-start(f32[2,4,64,128]{3,2,1,0:T(8,128)S(1)} %get-tuple-element.18), channel_id=1, source_target_pairs={{0,32},{32,0},{64,96},{96,64},{128,160},{160,128},{192,224},{224,1... | collective-permute-start | bytes 786440 | tf_op jit(solution)/shard_map/ppermute | solution.py:380
  73.6 1.3 collective-permute-start.1
  74.9 0.0 collective-permute-done.r_a
  74.9 4.8 %collective-permute-done.1.r_b = f32[2,4,64,128]{3,2,1,0:T(8,128)S(1)} collective-permute-done((f32[2,4,64,128]{3,2,1,0:T(8,128)S(1)}, f32[2,4,64,128]{3,2,1,0:T(8,128)S(1)}, u32[]{:S(2)}, u32[]{:S(2)}) %collective-permute-start.1) | collective-permute-done | bytes 262176 | tf_op jit(solution)/shard_map/ppermute | solution.py:381
  79.8 1.6 collective-permute-start.2
  81.3 0.4 collective-permute-start.3
  81.7 1.7 %collective-permute-done.2.q_c = f32[2,12,8,128]{3,2,1,0:T(8,128)S(1)} collective-permute-done((f32[2,12,8,128]{3,2,1,0:T(8,128)S(1)}, f32[2,12,8,128]{3,2,1,0:T(8,128)S(1)}, u32[]{:S(2)}, u32[]{:S(2)}) %collective-permute-start.2) | collective-permute-done | bytes 98336 | tf_op jit(solution)/shard_map/ppermute | solution.py:383
  83.3 4.8 %collective-permute-done.3.q_d = f32[2,12,8,128]{3,2,1,0:T(8,128)S(1)} collective-permute-done((f32[2,12,8,128]{3,2,1,0:T(8,128)S(1)}, f32[2,12,8,128]{3,2,1,0:T(8,128)S(1)}, u32[]{:S(2)}, u32[]{:S(2)}) %collective-permute-start.3) | collective-permute-done | bytes 98336 | tf_op jit(solution)/shard_map/ppermute | solution.py:384
  88.1 16.9 %stencil.1 = (bf16[16,64,128]{2,1,0:T(8,128)(2,1)S(1)}, f32[8,128]{1,0:T(8,128)S(1)}) custom-call(f32[16,64,128]{2,1,0:T(8,128)S(1)} %copy-done, f32[16,64,128]{2,1,0:T(8,128)S(1)} %get-tuple-element.17.v, f32[2,4,64,128]{3,2,1,0:T(8,128)S(1)} %collective-permute-done.r_a, f32[2,4,64,128]{3,2,1,0:T(8,128)S(1)} %collective-permute-done.1.r_b, ...), custom_call_target="tpu_custom_call" | custom-call | tf_op jit(solution)/shard_map/stencil/pallas_call | solution.py:320
  105.1 4.7 %collective-permute-start.10 = (bf16[16,64,128]{2,1,0:T(8,128)(2,1)S(1)}, bf16[16,64,128]{2,1,0:T(8,128)(2,1)S(1)}, u32[]{:S(2)}, u32[]{:S(2)}) collective-permute-start(bf16[16,64,128]{2,1,0:T(8,128)(2,1)S(1)} %get-tuple-element.24.refs_0_), channel_id=1, source_target_pairs={{0,224},{32,192},{64,160},{96,128},{128,96},{160,64},{192,32},{224... | collective-permute-start | bytes 786440 | tf_op jit(solution)/shard_map/ppermute | solution.py:388
  109.8 0.5 collective-permute-start.9
  110.2 0.2 collective-permute-start.8
  110.4 2.7 %collective-permute-start.7 = (bf16[16,64,128]{2,1,0:T(8,128)(2,1)S(1)}, bf16[16,64,128]{2,1,0:T(8,128)(2,1)S(1)}, u32[]{:S(2)}, u32[]{:S(2)}) collective-permute-start(bf16[16,64,128]{2,1,0:T(8,128)(2,1)S(1)} %get-tuple-element.24.refs_0_), channel_id=1, source_target_pairs={{0,128},{32,160},{64,192},{96,224},{128,0},{160,32},{192,64},{224,... | collective-permute-start | bytes 786440 | tf_op jit(solution)/shard_map/ppermute | solution.py:388
  113.1 0.5 collective-permute-start.6
  113.6 14.3 %collective-permute-done.10.refs_7_ = bf16[16,64,128]{2,1,0:T(8,128)(2,1)S(1)} collective-permute-done((bf16[16,64,128]{2,1,0:T(8,128)(2,1)S(1)}, bf16[16,64,128]{2,1,0:T(8,128)(2,1)S(1)}, u32[]{:S(2)}, u32[]{:S(2)}) %collective-permute-start.10) | collective-permute-done | bytes 262176 | tf_op jit(solution)/shard_map/ppermute | solution.py:388
  128.0 0.0 collective-permute-start.5
  128.0 5.6 %collective-permute-done.9.refs_6_ = bf16[16,64,128]{2,1,0:T(8,128)(2,1)S(1)} collective-permute-done((bf16[16,64,128]{2,1,0:T(8,128)(2,1)S(1)}, bf16[16,64,128]{2,1,0:T(8,128)(2,1)S(1)}, u32[]{:S(2)}, u32[]{:S(2)}) %collective-permute-start.9) | collective-permute-done | bytes 262176 | tf_op jit(solution)/shard_map/ppermute | solution.py:388
  133.6 0.4 collective-permute-start.4
  134.0 12.6 %all_to_all.20 = f32[32,1,128]{2,1,0:T(1,128)S(1)} all-to-all(f32[32,1,128]{2,1,0:T(1,128)S(1)} %broadcast_in_dim.4), channel_id=1, replica_groups=mesh['gz'=8,'xy'=32] {'xy'}, dimensions={0} | all-to-all | bytes 32768 | tf_op jit(solution)/shard_map/all_to_all | solution.py:390
  146.7 9.9 %all_to_all.21 = f32[8,1,128]{2,1,0:T(1,128)S(1)} all-to-all(f32[8,1,128]{2,1,0:T(1,128)S(1)} %broadcast_in_dim.5), channel_id=1, replica_groups=mesh['gz'=8,'xy'=32] {'gz'}, dimensions={0} | all-to-all | bytes 8192 | tf_op jit(solution)/shard_map/all_to_all | solution.py:392
  156.6 0.0 collective-permute-done.8.refs_5_
  156.6 0.0 collective-permute-done.5.refs_2_
  156.6 1.8 %scale.1 = bf16[128,64,128]{2,1,0:T(8,128)(2,1)} custom-call(f32[8,128]{1,0:T(8,128)S(1)} %bitcast.13, bf16[16,64,128]{2,1,0:T(8,128)(2,1)S(1)} %get-tuple-element.24.refs_0_, bf16[16,64,128]{2,1,0:T(8,128)(2,1)S(1)} %collective-permute-done.4.refs_1_, bf16[16,64,128]{2,1,0:T(8,128)(2,1)S(1)} %collective-permute-done.5.refs_2_, ...), custom_call_target="tpu_custom_call" | custom-call | tf_op jit(solution)/shard_map/scale/pallas_call | solution.py:352
  (14 shorter events, 0.1 us)
Async XLA Ops:
  0.0 1.2 copy-start.1
  1.2 0.8 copy-start.2
  2.0 0.8 copy-start.3
  2.7 0.7 copy-start.4
  3.4 0.7 copy-start.5
  7.9 60.5 %copy-start = (f32[16,64,128]{2,1,0:T(8,128)S(1)}, f32[16,64,128]{2,1,0:T(8,128)}, u32[]{:S(2)}) copy-start(f32[16,64,128]{2,1,0:T(8,128)} %cond.3) | copy-start | bytes 1572868
  70.7 4.2 %collective-permute-start = (f32[2,4,64,128]{3,2,1,0:T(8,128)S(1)}, f32[2,4,64,128]{3,2,1,0:T(8,128)S(1)}, u32[]{:S(2)}, u32[]{:S(2)}) collective-permute-start(f32[2,4,64,128]{3,2,1,0:T(8,128)S(1)} %get-tuple-element.18), channel_id=1, source_target_pairs={{0,32},{32,0},{64,96},{96,64},{128,160},{160,128},{192,224},{224,1... | collective-permute-start | bytes 786440 | tf_op jit(solution)/shard_map/ppermute | solution.py:380
  73.6 6.1 %collective-permute-start.1 = (f32[2,4,64,128]{3,2,1,0:T(8,128)S(1)}, f32[2,4,64,128]{3,2,1,0:T(8,128)S(1)}, u32[]{:S(2)}, u32[]{:S(2)}) collective-permute-start(f32[2,4,64,128]{3,2,1,0:T(8,128)S(1)} %get-tuple-element.19), channel_id=1, source_target_pairs={{0,224},{32,64},{64,32},{96,128},{128,96},{160,192},{192,160},{224... | collective-permute-start | bytes 786440 | tf_op jit(solution)/shard_map/ppermute | solution.py:381
  79.8 3.6 %collective-permute-start.2 = (f32[2,12,8,128]{3,2,1,0:T(8,128)S(1)}, f32[2,12,8,128]{3,2,1,0:T(8,128)S(1)}, u32[]{:S(2)}, u32[]{:S(2)}) collective-permute-start(f32[2,12,8,128]{3,2,1,0:T(8,128)S(1)} %get-tuple-element.21), channel_id=1, source_target_pairs={{0,1},{1,0},{2,3},{3,2},{4,5},{5,4},{6,7},{7,6},{8,9},{9,8},{10,11... | collective-permute-start | bytes 294920 | tf_op jit(solution)/shard_map/ppermute | solution.py:383
  81.3 6.8 %collective-permute-start.3 = (f32[2,12,8,128]{3,2,1,0:T(8,128)S(1)}, f32[2,12,8,128]{3,2,1,0:T(8,128)S(1)}, u32[]{:S(2)}, u32[]{:S(2)}) collective-permute-start(f32[2,12,8,128]{3,2,1,0:T(8,128)S(1)} %get-tuple-element.22), channel_id=1, source_target_pairs={{0,31},{1,2},{2,1},{3,4},{4,3},{5,6},{6,5},{7,8},{8,7},{9,10},{10,... | collective-permute-start | bytes 294920 | tf_op jit(solution)/shard_map/ppermute | solution.py:384
  105.1 22.9 %collective-permute-start.10 = (bf16[16,64,128]{2,1,0:T(8,128)(2,1)S(1)}, bf16[16,64,128]{2,1,0:T(8,128)(2,1)S(1)}, u32[]{:S(2)}, u32[]{:S(2)}) collective-permute-start(bf16[16,64,128]{2,1,0:T(8,128)(2,1)S(1)} %get-tuple-element.24.refs_0_), channel_id=1, source_target_pairs={{0,224},{32,192},{64,160},{96,128},{128,96},{160,64},{192,32},{224... | collective-permute-start | bytes 786440 | tf_op jit(solution)/shard_map/ppermute | solution.py:388
  109.8 23.8 %collective-permute-start.9 = (bf16[16,64,128]{2,1,0:T(8,128)(2,1)S(1)}, bf16[16,64,128]{2,1,0:T(8,128)(2,1)S(1)}, u32[]{:S(2)}, u32[]{:S(2)}) collective-permute-start(bf16[16,64,128]{2,1,0:T(8,128)(2,1)S(1)} %get-tuple-element.24.refs_0_), channel_id=1, source_target_pairs={{0,192},{32,224},{64,128},{96,160},{128,64},{160,96},{192,0},{224,... | collective-permute-start | bytes 786440 | tf_op jit(solution)/shard_map/ppermute | solution.py:388
  110.2 46.4 %collective-permute-start.8 = (bf16[16,64,128]{2,1,0:T(8,128)(2,1)S(1)}, bf16[16,64,128]{2,1,0:T(8,128)(2,1)S(1)}, u32[]{:S(2)}, u32[]{:S(2)}) collective-permute-start(bf16[16,64,128]{2,1,0:T(8,128)(2,1)S(1)} %get-tuple-element.24.refs_0_), channel_id=1, source_target_pairs={{0,160},{32,128},{64,224},{96,192},{128,32},{160,0},{192,96},{224,... | collective-permute-start | bytes 786440 | tf_op jit(solution)/shard_map/ppermute | solution.py:388
  110.4 46.2 %collective-permute-start.7 = (bf16[16,64,128]{2,1,0:T(8,128)(2,1)S(1)}, bf16[16,64,128]{2,1,0:T(8,128)(2,1)S(1)}, u32[]{:S(2)}, u32[]{:S(2)}) collective-permute-start(bf16[16,64,128]{2,1,0:T(8,128)(2,1)S(1)} %get-tuple-element.24.refs_0_), channel_id=1, source_target_pairs={{0,128},{32,160},{64,192},{96,224},{128,0},{160,32},{192,64},{224,... | collective-permute-start | bytes 786440 | tf_op jit(solution)/shard_map/ppermute | solution.py:388
  113.1 43.5 %collective-permute-start.6 = (bf16[16,64,128]{2,1,0:T(8,128)(2,1)S(1)}, bf16[16,64,128]{2,1,0:T(8,128)(2,1)S(1)}, u32[]{:S(2)}, u32[]{:S(2)}) collective-permute-start(bf16[16,64,128]{2,1,0:T(8,128)(2,1)S(1)} %get-tuple-element.24.refs_0_), channel_id=1, source_target_pairs={{0,96},{32,64},{64,32},{96,0},{128,224},{160,192},{192,160},{224,1... | collective-permute-start | bytes 786440 | tf_op jit(solution)/shard_map/ppermute | solution.py:388
  128.0 28.6 %collective-permute-start.5 = (bf16[16,64,128]{2,1,0:T(8,128)(2,1)S(1)}, bf16[16,64,128]{2,1,0:T(8,128)(2,1)S(1)}, u32[]{:S(2)}, u32[]{:S(2)}) collective-permute-start(bf16[16,64,128]{2,1,0:T(8,128)(2,1)S(1)} %get-tuple-element.24.refs_0_), channel_id=1, source_target_pairs={{0,64},{32,96},{64,0},{96,32},{128,192},{160,224},{192,128},{224,1... | collective-permute-start | bytes 786440 | tf_op jit(solution)/shard_map/ppermute | solution.py:388
  133.6 23.0 %collective-permute-start.4 = (bf16[16,64,128]{2,1,0:T(8,128)(2,1)S(1)}, bf16[16,64,128]{2,1,0:T(8,128)(2,1)S(1)}, u32[]{:S(2)}, u32[]{:S(2)}) collective-permute-start(bf16[16,64,128]{2,1,0:T(8,128)(2,1)S(1)} %get-tuple-element.24.refs_0_), channel_id=1, source_target_pairs={{0,32},{32,0},{64,96},{96,64},{128,160},{160,128},{192,224},{224,1... | collective-permute-start | bytes 786440 | tf_op jit(solution)/shard_map/ppermute | solution.py:388

commit v2 on v1

--- a/solution.py
+++ b/solution.py
@@ -9,12 +9,13 @@
 
 F32 = jnp.float32
 BF16 = jnp.bfloat16
-VMEM_LIMIT = 40 * 1024 * 1024
+VMEM_LIMIT = 24 * 1024 * 1024
+VMEM_ALL = 60 * 1024 * 1024
 CAP = 4
 
 
-def params():
-    return pltpu.CompilerParams(vmem_limit_bytes=VMEM_LIMIT)
+def params(limit=VMEM_LIMIT):
+    return pltpu.CompilerParams(vmem_limit_bytes=limit)
 
 
 def vspec():
@@ -29,56 +30,71 @@
     return jax.ShapeDtypeStruct(shape, dtype)
 
 
-def pack_kernel(vel, off, wt, route_any, route, slot, send, code, route_s, count, sem):
+def pack_kernel(vel_any, off, wt, route_any, slot_any, send, code, vel, out, route, slot, route_s, count, sems):
     g = lax.axis_index("gz")
     d = lax.axis_index("xy")
     rows = pl.ds(pl.multiple_of(g * 8, 8), 8)
-    copy = pltpu.make_async_copy(route_any.at[rows], route_s, sem)
-    copy.start()
+    loads = [
+        pltpu.make_async_copy(route_any.at[rows], route_s, sems.at[0]),
+        pltpu.make_async_copy(route_any.at[rows], route, sems.at[1]),
+        pltpu.make_async_copy(slot_any.at[rows], slot, sems.at[2]),
+    ]
+    bricks = [
+        pltpu.make_async_copy(vel_any.at[pl.ds(8 * i, 8)], vel.at[pl.ds(8 * i, 8)], sems.at[3 + i])
+        for i in range(4)
+    ]
+    for copy in loads + bricks:
+        copy.start()
+    for i in range(32):
+        count[i] = 0
+    for copy in loads:
+        copy.wait()
     lane = lax.broadcasted_iota(jnp.int32, (8, 128), 1) % 32
-    mine = (route[rows, :] == d).astype(jnp.int32)
+    mine = (route[...] == d).astype(jnp.int32)
     upto = mine
     for step in (1, 2, 4, 8, 16):
         upto = upto + jnp.where(lane >= step, pltpu.roll(upto, step, 1), 0)
     rank = upto - mine
-    word = jnp.where(mine > 0, (slot[rows, :] + 1) << (5 * rank), 0)
+    word = jnp.where(mine > 0, (slot[...] + 1) << (5 * rank), 0)
     for step in (1, 2, 4, 8, 16):
         word = word + jnp.where(lane >= step, pltpu.roll(word, step, 1), 0)
     code[...] = word
-    for i in range(32):
-        count[i] = 0
-    copy.wait()
     row = d // 4
     first = (d % 4) * 32
     x = lax.broadcasted_iota(jnp.int32, (64, 128), 1)
-
-    def one(r, carry):
+    for r in range(32):
+        if r % 8 == 0:
+            bricks[r // 8].wait()
         dest = route_s[row, first + r]
         k = count[dest]
         count[dest] = k + 1
         o = off[r]
         v = vel[r].reshape(64, 128)
         moved = jnp.where(x < 128 - o, pltpu.roll(v, (128 - o) % 128, 1), 0.0)
-        send[dest * CAP + k] = (moved * wt[r]).astype(BF16)
-        return carry
-
-    lax.fori_loop(0, 32, one, 0)
+        out[r] = (moved * wt[r]).astype(BF16)
+        pltpu.make_async_copy(out.at[r], send.at[dest * CAP + k], sems.at[7]).start()
+    pltpu.make_async_copy(out, send.at[pl.ds(0, 32)], sems.at[7]).wait()
 
 
 def pack(velocity, offset, weight, route, slot):
+    anywhere = pl.BlockSpec(memory_space=pl.ANY)
     return pl.pallas_call(
         pack_kernel,
         out_shape=(sds((32 * CAP, 64, 128), BF16), sds((8, 128), jnp.int32)),
-        in_specs=[vspec(), sspec(), sspec(), pl.BlockSpec(memory_space=pl.ANY), vspec(), vspec()],
-        out_specs=(vspec(), vspec()),
+        in_specs=[anywhere, sspec(), sspec(), anywhere, anywhere],
+        out_specs=(anywhere, vspec()),
         scratch_shapes=[
+            pltpu.VMEM((32, 8, 8, 128), F32),
+            pltpu.VMEM((32, 64, 128), BF16),
+            pltpu.VMEM((8, 128), jnp.int32),
+            pltpu.VMEM((8, 128), jnp.int32),
             pltpu.SMEM((8, 128), jnp.int32),
             pltpu.SMEM((32,), jnp.int32),
-            pltpu.SemaphoreType.DMA,
+            pltpu.SemaphoreType.DMA((8,)),
         ],
-        compiler_params=params(),
+        compiler_params=params(VMEM_ALL),
         name="pack",
-    )(velocity, offset, weight, route, route, slot)
+    )(velocity, offset, weight, route, slot)
 
 
 def pair_rows(block):
@@ -231,16 +247,18 @@
 
     weights = jnp.concatenate([band(S_TAPS), band(D_TAPS)], axis=1)
 
+    twice = jnp.concatenate([weights, weights], axis=0)
+
     def along_x(i, carry):
-        f = i // 24
-        z = i % 24
-        h, m, l = split3(ext[f, z])
-        both = dot(h, weights) + dot(m, weights) + dot(l, weights)
-        sx[f, z] = both[:, 0:128]
-        dx[f, z] = both[:, 128:256]
-        return carry
-
-    lax.fori_loop(0, 48, along_x, 0)
+        f = i // 2
+        part = pl.ds((i % 2) * 12, 12)
+        h, m, l = split3(ext[f, part].reshape(12 * 80, 128))
+        both = dot(jnp.concatenate([h, m], axis=1), twice) + dot(l, weights)
+        sx[f, part] = both[:, 0:128].reshape(12, 80, 128)
+        dx[f, part] = both[:, 128:256].reshape(12, 80, 128)
+        return carry
+
+    lax.fori_loop(0, 4, along_x, 0)
 
     def along_y(i, carry):
         f = i // 24
@@ -254,7 +272,7 @@
         ext[f, z] = smooth5(ss)
         return carry
 
-    lax.fori_loop(0, 48, along_y, 0)
+    lax.fori_loop(0, 48, along_y, 0, unroll=2)
 
     row = lax.broadcasted_iota(jnp.int32, (8, 128), 0)
 
@@ -301,25 +319,26 @@
     w_s = band(S_TAPS)
     w_d = band(D_TAPS)
     w = jnp.concatenate([w_d, w_s], axis=0)
-    total[...] = jnp.zeros_like(total)
-
-    def back_x(z, carry):
-        us = split3(mid_u[z])
-        ts = split3(mid_t[z])
+    total[0:8, :] = jnp.zeros((8, 128), F32)
+
+    def back_x(i, carry):
+        part = pl.ds(i * 8, 8)
+        us = split3(mid_u[part].reshape(512, 128))
+        ts = split3(mid_t[part].reshape(512, 128))
         acc = sum(dot(jnp.concatenate([a, b], axis=1), w) for a, b in zip(us, ts))
         acc = acc * NORM
-        out[z] = acc.astype(BF16)
-        total[...] += jnp.sum((acc * acc).reshape(8, 8, 128), axis=0)
-        return carry
-
-    lax.fori_loop(0, 16, back_x, 0)
-    total[...] = jnp.broadcast_to(jnp.sum(total[...], axis=0, keepdims=True), (8, 128))
+        out[part] = acc.reshape(8, 64, 128).astype(BF16)
+        total[0:8, :] += jnp.sum((acc * acc).reshape(64, 8, 128), axis=0)
+        return carry
+
+    lax.fori_loop(0, 2, back_x, 0, unroll=2)
+    total[...] = jnp.broadcast_to(jnp.sum(total[0:8, :], axis=0, keepdims=True), (32, 128))
 
 
 def stencil(cond, v, r_a, r_b, q_c, q_d):
     return pl.pallas_call(
         stencil_kernel,
-        out_shape=(sds((16, 64, 128), BF16), sds((8, 128), F32)),
+        out_shape=(sds((16, 64, 128), BF16), sds((32, 128), F32)),
         in_specs=[vspec()] * 6,
         out_specs=(vspec(),) * 2,
         scratch_shapes=[
@@ -335,17 +354,20 @@
     )(cond, v, r_a, r_b, q_c, q_d)
 
 
-def scale_kernel(cells, sums, *refs):
-    pieces, out = refs[:-1], refs[-1]
+def scale_kernel(cells, sums, pair, before, after, far_own, far_twin, out):
     g = lax.axis_index("gz")
     total = jnp.sum(sums[...], axis=0, keepdims=True)
     total = jnp.sum(total, axis=1, keepdims=True)
     scale = 1.0 / jnp.sqrt(total / cells + 1e-06)
     scale = jnp.broadcast_to(scale, (64, 128))
-    for k, piece in enumerate(pieces):
-        base = (g ^ k) * 16
+    left, right, across = lax.rem(g + 6, 8), lax.rem(g + 2, 8), lax.rem(g + 4, 8)
+    places = [(pair.at[0], g), (pair.at[1], g ^ 1)]
+    places += [(before.at[0], left), (before.at[1], left ^ 1)]
+    places += [(after.at[0], right), (after.at[1], right ^ 1)]
+    places += [(far_own, across), (far_twin, across ^ 1)]
+    for piece, owner in places:
         for z in range(16):
-            out[base + z] = (piece[z].astype(F32) * scale).astype(BF16)
+            out[owner * 16 + z] = (piece[z].astype(F32) * scale).astype(BF16)
 
 
 def scaled(cells, sums, pieces):
@@ -365,6 +387,10 @@
 
 def swap_even(count):
     return [(i, i ^ 1) for i in range(count)]
+
+
+def row_sum(rows, size):
+    return jnp.broadcast_to(jnp.sum(rows, axis=0, keepdims=True), (size, 128))
 
 
 def local(velocity, offset, interp_weight, route, dest_slot, conductivity):
@@ -383,15 +409,20 @@
     q_c = lax.ppermute(y_c, "xy", swap_even(n_x))
     q_d = lax.ppermute(y_d, "xy", swap_odd(n_x))
     grad, total = stencil(conductivity, v, r_a, r_b, q_c, q_d)
-    pieces = [grad]
-    for k in range(1, n_g):
-        pieces.append(lax.ppermute(grad, "gz", [(i, i ^ k) for i in range(n_g)]))
-    part = jnp.broadcast_to(total[0:1], (n_x, 128))
-    part = lax.all_to_all(part, "xy", 0, 0, tiled=True)
-    part = jnp.broadcast_to(jnp.sum(part, axis=0, keepdims=True), (n_g, 128))
-    part = lax.all_to_all(part, "gz", 0, 0, tiled=True)
+    up = [(i, (i + 2) % n_g) for i in range(n_g)]
+    down = [(i, (i - 2) % n_g) for i in range(n_g)]
+    pair = jnp.stack([grad, lax.ppermute(grad, "gz", swap_even(n_g))])
+    pair, total = lax.optimization_barrier((pair, total))
+    before = lax.ppermute(pair, "gz", up)
+    after = lax.ppermute(pair, "gz", down)
+    rows = lax.all_to_all(total, "xy", 0, 0, tiled=True)
+    before, after, rows = lax.optimization_barrier((before, after, rows))
+    far_own = lax.ppermute(before[0], "gz", up)
+    far_twin = lax.ppermute(after[1], "gz", down)
+    sums = lax.all_to_all(row_sum(rows, n_g), "gz", 0, 0, tiled=True)
+    pieces = [pair, before, after, far_own, far_twin]
     cells = float(n_g * n_x * 16 * 64 * 128)
-    return scaled(cells, part, pieces)
+    return scaled(cells, sums, pieces)
 
 
 def solution(mesh):

time: 159 us -> 126 us (0.79)
  waiting for transfers between devices: 31.2 us -> 15.3 us
  Pallas kernels: 24.9 us -> 15.6 us
  local copies, waits for them, and re-layouts: 4.08 us -> 0.05 us
  starting transfers between devices: 15.1 us -> 12.2 us
    ppermute x7 -> x5, waiting for transfers between devices: 20 us -> 3.65 us  [the longest x1 2.48 us: local(): before = lax.ppermute(pair, 'gz', up)]
    pallas_call x1, Pallas kernels: 16.9 us -> 7.62 us  [stencil(): pl.pallas_call(stencil_kernel, out_shape=(sds((16, 64, 128), BF16), sds((...]
    unnamed x12 -> x4, local copies, waits for them, and re-layouts: 4.05 us -> 0.01 us
    ppermute x7 -> x5, starting transfers between devices: 8.96 us -> 6.45 us  [the longest x1 2.61 us: local(): pair = jnp.stack([grad, lax.ppermute(grad, 'gz', swap_even(n_g))])]
  transfers between devices with their start and end apart: 11 -> 9, of which waited for: 5 -> 5; matrix products, arithmetic and copies ran while one was open for 0% -> 0% of each run, Pallas kernels for 0% -> 0%
where the time goes in v2:
time: 126 us
  blocking collectives  82.4 us (65%)
  Pallas kernels  15.6 us (12%)
  waiting for transfers between devices  15.3 us (12%)
  starting transfers between devices  12.2 us (10%)
    all_to_all x1, blocking collectives, local(): lax.all_to_all(send.reshape(n_x, CAP * 64, 128), 'xy', split_axis=0, conc...  60.7 us
    all_to_all x1, blocking collectives, local(): rows = lax.all_to_all(total, 'xy', 0, 0, tiled=True)  11.5 us
    all_to_all x1, blocking collectives, local(): sums = lax.all_to_all(row_sum(rows, n_g), 'gz', 0, 0, tiled=True)  10.2 us
    pallas_call x1, Pallas kernels, stencil(): pl.pallas_call(stencil_kernel, out_shape=(sds((16, 64, 128), BF16), sds((...  7.62 us
    ppermute x1, waiting for transfers between devices, local(): r_b = lax.ppermute(z_b, 'gz', swap_odd(n_g))  4.83 us
    ppermute x1, waiting for transfers between devices, local(): q_d = lax.ppermute(y_d, 'xy', swap_odd(n_x))  4.78 us
    pallas_call x1, Pallas kernels, pack(): pl.pallas_call(pack_kernel, out_shape=(sds((32 * CAP, 64, 128), BF16), sd...  3.94 us
    ppermute x1, starting transfers between devices, local(): r_a = lax.ppermute(z_a, 'gz', swap_even(n_g))  2.96 us
  transfers between devices with their start and end apart: 9, of which 5 were waited for; matrix products, arithmetic and copies ran while one was open for 0% of the time, Pallas kernels for 0%

profile of v2, /device:TPU:1, one launch (start us, length us, event | category | flops | bytes accessed | tf_op | source)
XLA Modules:
  0.0 125.7 jit_solution(8131307186084369245)
XLA Ops:
  0.0 3.9 %pack.1 = (bf16[128,64,128]{2,1,0:T(8,128)(2,1)}, s32[8,128]{1,0:T(8,128)}) custom-call(f32[32,8,8,128]{3,2,1,0:T(8,128)} %vel_any.1, s32[32]{0:T(128)} %off.1, f32[32]{0:T(128)} %wt.1, s32[64,128]{1,0:T(8,128)} %bitcast.22, s32[64,128]{1,0:T(8,128)} %bitcast.23), custom_call_target="tpu_custom_call" | custom-call | tf_op jit(solution)/shard_map/pack/pallas_call | solution.py:81
  4.0 0.0 copy-start
  4.0 0.0 copy-start.1
  4.0 60.7 %all_to_all.25 = bf16[32,256,128]{2,1,0:T(8,128)(2,1)S(1)} all-to-all(bf16[32,256,128]{2,1,0:T(8,128)(2,1)} %bitcast.19), channel_id=1, replica_groups=mesh['gz'=8,'xy'=32] {'xy'}, dimensions={0} | all-to-all | bytes 4194304 | tf_op jit(solution)/shard_map/all_to_all | solution.py:402
  64.7 0.0 copy-done
  64.7 0.0 copy-done.1
  64.7 2.3 %combine.1 = (f32[16,64,128]{2,1,0:T(8,128)S(1)}, f32[2,4,64,128]{3,2,1,0:T(8,128)S(1)}, f32[2,4,64,128]{3,2,1,0:T(8,128)S(1)}, f32[2,2,8,8,128]{4,3,2,1,0:T(8,128)S(1)}) custom-call(bf16[128,64,128]{2,1,0:T(8,128)(2,1)S(1)} %bitcast.15, s32[8,128]{1,0:T(8,128)S(1)} %copy-done.1, f32[16,64,128]{2,1,0:T(8,128)S(1)} %copy-done), custom_call_target="tpu_custom_call" | custom-call | tf_op jit(solution)/shard_map/combine/pallas_call | solution.py:141
  67.0 3.0 %collective-permute-start = (f32[2,4,64,128]{3,2,1,0:T(8,128)S(1)}, f32[2,4,64,128]{3,2,1,0:T(8,128)S(1)}, u32[]{:S(2)}, u32[]{:S(2)}) collective-permute-start(f32[2,4,64,128]{3,2,1,0:T(8,128)S(1)} %get-tuple-element.23), channel_id=1, source_target_pairs={{0,32},{32,0},{64,96},{96,64},{128,160},{160,128},{192,224},{224,1... | collective-permute-start | bytes 786440 | tf_op jit(solution)/shard_map/ppermute | solution.py:406
  69.9 1.3 %collective-permute-start.1 = (f32[2,4,64,128]{3,2,1,0:T(8,128)S(1)}, f32[2,4,64,128]{3,2,1,0:T(8,128)S(1)}, u32[]{:S(2)}, u32[]{:S(2)}) collective-permute-start(f32[2,4,64,128]{3,2,1,0:T(8,128)S(1)} %get-tuple-element.24), channel_id=1, source_target_pairs={{0,224},{32,64},{64,32},{96,128},{128,96},{160,192},{192,160},{224... | collective-permute-start | bytes 786440 | tf_op jit(solution)/shard_map/ppermute | solution.py:407
  71.2 0.0 collective-permute-done.r_a
  71.2 4.8 %collective-permute-done.1.r_b = f32[2,4,64,128]{3,2,1,0:T(8,128)S(1)} collective-permute-done((f32[2,4,64,128]{3,2,1,0:T(8,128)S(1)}, f32[2,4,64,128]{3,2,1,0:T(8,128)S(1)}, u32[]{:S(2)}, u32[]{:S(2)}) %collective-permute-start.1) | collective-permute-done | bytes 262176 | tf_op jit(solution)/shard_map/ppermute | solution.py:407
  76.0 1.6 %collective-permute-start.2 = (f32[2,12,8,128]{3,2,1,0:T(8,128)S(1)}, f32[2,12,8,128]{3,2,1,0:T(8,128)S(1)}, u32[]{:S(2)}, u32[]{:S(2)}) collective-permute-start(f32[2,12,8,128]{3,2,1,0:T(8,128)S(1)} %get-tuple-element.26), channel_id=1, source_target_pairs={{0,1},{1,0},{2,3},{3,2},{4,5},{5,4},{6,7},{7,6},{8,9},{9,8},{10,11... | collective-permute-start | bytes 294920 | tf_op jit(solution)/shard_map/ppermute | solution.py:409
  77.6 0.0 collective-permute-start.3
  77.6 2.0 %collective-permute-done.2.q_c = f32[2,12,8,128]{3,2,1,0:T(8,128)S(1)} collective-permute-done((f32[2,12,8,128]{3,2,1,0:T(8,128)S(1)}, f32[2,12,8,128]{3,2,1,0:T(8,128)S(1)}, u32[]{:S(2)}, u32[]{:S(2)}) %collective-permute-start.2) | collective-permute-done | bytes 98336 | tf_op jit(solution)/shard_map/ppermute | solution.py:409
  79.6 4.8 %collective-permute-done.3.q_d = f32[2,12,8,128]{3,2,1,0:T(8,128)S(1)} collective-permute-done((f32[2,12,8,128]{3,2,1,0:T(8,128)S(1)}, f32[2,12,8,128]{3,2,1,0:T(8,128)S(1)}, u32[]{:S(2)}, u32[]{:S(2)}) %collective-permute-start.3) | collective-permute-done | bytes 98336 | tf_op jit(solution)/shard_map/ppermute | solution.py:410
  84.4 7.6 %stencil.1 = (bf16[16,64,128]{2,1,0:T(8,128)(2,1)S(1)}, f32[32,128]{1,0:T(8,128)S(1)}) custom-call(f32[16,64,128]{2,1,0:T(8,128)S(1)} %copy-done, f32[16,64,128]{2,1,0:T(8,128)S(1)} %get-tuple-element.22.v, f32[2,4,64,128]{3,2,1,0:T(8,128)S(1)} %collective-permute-done.r_a, f32[2,4,64,128]{3,2,1,0:T(8,128)S(1)} %collective-permute-done.1.r_b, ...), custom_call_target="tpu_custom_call" | custom-call | tf_op jit(solution)/shard_map/stencil/pallas_call | solution.py:339
  92.0 2.6 %collective-permute-start.4 = (bf16[16,64,128]{2,1,0:T(8,128)(2,1)S(1)}, bf16[16,64,128]{2,1,0:T(8,128)(2,1)S(1)}, u32[]{:S(2)}, u32[]{:S(2)}) collective-permute-start(bf16[16,64,128]{2,1,0:T(8,128)(2,1)S(1)} %get-tuple-element.28), channel_id=1, source_target_pairs={{0,32},{32,0},{64,96},{96,64},{128,160},{160,128},{192,224},{224,1... | collective-permute-start | bytes 786440 | tf_op jit(solution)/shard_map/ppermute | solution.py:414
  94.6 1.2 collective-permute-done.4
  95.8 0.1 pad_maximum_fusion.pair
  95.9 2.3 %collective-permute-start.6 = (bf16[2,16,64,128]{3,2,1,0:T(8,128)(2,1)S(1)}, bf16[2,16,64,128]{3,2,1,0:T(8,128)(2,1)S(1)}, u32[]{:S(2)}, u32[]{:S(2)}) collective-permute-start(bf16[2,16,64,128]{3,2,1,0:T(8,128)(2,1)S(1)} %pad_maximum_fusion.pair), channel_id=1, source_target_pairs={{0,192},{32,224},{64,0},{96,32},{128,64},{160,96},{192,128},{224,1... | collective-permute-start | bytes 1572872 | tf_op jit(solution)/shard_map/ppermute | solution.py:417
  98.1 0.0 collective-permute-start.5
  98.2 11.5 %all_to_all.26 = f32[32,1,128]{2,1,0:T(1,128)S(1)} all-to-all(f32[32,1,128]{2,1,0:T(1,128)S(1)} %bitcast.18), channel_id=1, replica_groups=mesh['gz'=8,'xy'=32] {'xy'}, dimensions={0} | all-to-all | bytes 32768 | tf_op jit(solution)/shard_map/all_to_all | solution.py:418
  109.7 0.0 collective-permute-done.6.after
  109.7 2.5 %collective-permute-done.5.before = bf16[2,16,64,128]{3,2,1,0:T(8,128)(2,1)S(1)} collective-permute-done((bf16[2,16,64,128]{3,2,1,0:T(8,128)(2,1)S(1)}, bf16[2,16,64,128]{3,2,1,0:T(8,128)(2,1)S(1)}, u32[]{:S(2)}, u32[]{:S(2)}) %collective-permute-start.5) | collective-permute-done | bytes 524320 | tf_op jit(solution)/shard_map/ppermute | solution.py:416
  112.2 0.4 collective-permute-start.8
  112.6 1.1 collective-permute-start.7
  113.8 10.2 %all_to_all.27 = f32[8,1,128]{2,1,0:T(1,128)S(1)} all-to-all(f32[8,1,128]{2,1,0:T(1,128)S(1)} %broadcast_in_dim.2), channel_id=1, replica_groups=mesh['gz'=8,'xy'=32] {'gz'}, dimensions={0} | all-to-all | bytes 8192 | tf_op jit(solution)/shard_map/all_to_all | solution.py:422
  124.0 0.0 collective-permute-done.8.far_twin
  124.0 0.0 collective-permute-done.7.far_own
  124.0 1.8 %scale.1 = bf16[128,64,128]{2,1,0:T(8,128)(2,1)} custom-call(f32[8,128]{1,0:T(8,128)S(1)} %bitcast.17, bf16[2,16,64,128]{3,2,1,0:T(8,128)(2,1)S(1)} %pad_maximum_fusion.pair, bf16[2,16,64,128]{3,2,1,0:T(8,128)(2,1)S(1)} %collective-permute-done.5.before, bf16[2,16,64,128]{3,2,1,0:T(8,128)(2,1)S(1)} %collective-permute-done.6.after, ...), custom_call_target="tpu_custom_call" | custom-call | tf_op jit(solution)/shard_map/scale/pallas_call | solution.py:374
  (5 shorter events, 0.1 us)
Async XLA Ops:
  4.0 60.7 %copy-start = (f32[16,64,128]{2,1,0:T(8,128)S(1)}, f32[16,64,128]{2,1,0:T(8,128)}, u32[]{:S(2)}) copy-start(f32[16,64,128]{2,1,0:T(8,128)} %cond.3) | copy-start | bytes 1572868
  4.0 60.7 %copy-start.1 = (s32[8,128]{1,0:T(8,128)S(1)}, s32[8,128]{1,0:T(8,128)}, u32[]{:S(2)}) copy-start(s32[8,128]{1,0:T(8,128)} %get-tuple-element.21.code) | copy-start | bytes 12292
  67.0 4.2 %collective-permute-start = (f32[2,4,64,128]{3,2,1,0:T(8,128)S(1)}, f32[2,4,64,128]{3,2,1,0:T(8,128)S(1)}, u32[]{:S(2)}, u32[]{:S(2)}) collective-permute-start(f32[2,4,64,128]{3,2,1,0:T(8,128)S(1)} %get-tuple-element.23), channel_id=1, source_target_pairs={{0,32},{32,0},{64,96},{96,64},{128,160},{160,128},{192,224},{224,1... | collective-permute-start | bytes 786440 | tf_op jit(solution)/shard_map/ppermute | solution.py:406
  69.9 6.1 %collective-permute-start.1 = (f32[2,4,64,128]{3,2,1,0:T(8,128)S(1)}, f32[2,4,64,128]{3,2,1,0:T(8,128)S(1)}, u32[]{:S(2)}, u32[]{:S(2)}) collective-permute-start(f32[2,4,64,128]{3,2,1,0:T(8,128)S(1)} %get-tuple-element.24), channel_id=1, source_target_pairs={{0,224},{32,64},{64,32},{96,128},{128,96},{160,192},{192,160},{224... | collective-permute-start | bytes 786440 | tf_op jit(solution)/shard_map/ppermute | solution.py:407
  76.0 3.6 %collective-permute-start.2 = (f32[2,12,8,128]{3,2,1,0:T(8,128)S(1)}, f32[2,12,8,128]{3,2,1,0:T(8,128)S(1)}, u32[]{:S(2)}, u32[]{:S(2)}) collective-permute-start(f32[2,12,8,128]{3,2,1,0:T(8,128)S(1)} %get-tuple-element.26), channel_id=1, source_target_pairs={{0,1},{1,0},{2,3},{3,2},{4,5},{5,4},{6,7},{7,6},{8,9},{9,8},{10,11... | collective-permute-start | bytes 294920 | tf_op jit(solution)/shard_map/ppermute | solution.py:409
  77.6 6.8 %collective-permute-start.3 = (f32[2,12,8,128]{3,2,1,0:T(8,128)S(1)}, f32[2,12,8,128]{3,2,1,0:T(8,128)S(1)}, u32[]{:S(2)}, u32[]{:S(2)}) collective-permute-start(f32[2,12,8,128]{3,2,1,0:T(8,128)S(1)} %get-tuple-element.27), channel_id=1, source_target_pairs={{0,31},{1,2},{2,1},{3,4},{4,3},{5,6},{6,5},{7,8},{8,7},{9,10},{10,... | collective-permute-start | bytes 294920 | tf_op jit(solution)/shard_map/ppermute | solution.py:410
  92.0 3.8 %collective-permute-start.4 = (bf16[16,64,128]{2,1,0:T(8,128)(2,1)S(1)}, bf16[16,64,128]{2,1,0:T(8,128)(2,1)S(1)}, u32[]{:S(2)}, u32[]{:S(2)}) collective-permute-start(bf16[16,64,128]{2,1,0:T(8,128)(2,1)S(1)} %get-tuple-element.28), channel_id=1, source_target_pairs={{0,32},{32,0},{64,96},{96,64},{128,160},{160,128},{192,224},{224,1... | collective-permute-start | bytes 786440 | tf_op jit(solution)/shard_map/ppermute | solution.py:414
  95.9 13.8 %collective-permute-start.6 = (bf16[2,16,64,128]{3,2,1,0:T(8,128)(2,1)S(1)}, bf16[2,16,64,128]{3,2,1,0:T(8,128)(2,1)S(1)}, u32[]{:S(2)}, u32[]{:S(2)}) collective-permute-start(bf16[2,16,64,128]{3,2,1,0:T(8,128)(2,1)S(1)} %pad_maximum_fusion.pair), channel_id=1, source_target_pairs={{0,192},{32,224},{64,0},{96,32},{128,64},{160,96},{192,128},{224,1... | collective-permute-start | bytes 1572872 | tf_op jit(solution)/shard_map/ppermute | solution.py:417
  98.1 14.0 %collective-permute-start.5 = (bf16[2,16,64,128]{3,2,1,0:T(8,128)(2,1)S(1)}, bf16[2,16,64,128]{3,2,1,0:T(8,128)(2,1)S(1)}, u32[]{:S(2)}, u32[]{:S(2)}) collective-permute-start(bf16[2,16,64,128]{3,2,1,0:T(8,128)(2,1)S(1)} %pad_maximum_fusion.pair), channel_id=1, source_target_pairs={{0,64},{32,96},{64,128},{96,160},{128,192},{160,224},{192,0},{224,... | collective-permute-start | bytes 1572872 | tf_op jit(solution)/shard_map/ppermute | solution.py:416
  112.2 11.8 %collective-permute-start.8 = (bf16[16,64,128]{2,1,0:T(8,128)(2,1)S(1)}, bf16[16,64,128]{2,1,0:T(8,128)(2,1)S(1)}, u32[]{:S(2)}, u32[]{:S(2)}) collective-permute-start(bf16[16,64,128]{2,1,0:T(8,128)(2,1)S(1)} %slice_bitcast_fusion), channel_id=1, source_target_pairs={{0,192},{32,224},{64,0},{96,32},{128,64},{160,96},{192,128},{224,1... | collective-permute-start | bytes 786440 | tf_op jit(solution)/shard_map/ppermute | solution.py:421
  112.6 11.4 %collective-permute-start.7 = (bf16[16,64,128]{2,1,0:T(8,128)(2,1)S(1)}, bf16[16,64,128]{2,1,0:T(8,128)(2,1)S(1)}, u32[]{:S(2)}, u32[]{:S(2)}) collective-permute-start(bf16[16,64,128]{2,1,0:T(8,128)(2,1)S(1)} %slice_bitcast_fusion.1), channel_id=1, source_target_pairs={{0,64},{32,96},{64,128},{96,160},{128,192},{160,224},{192,0},{224,... | collective-permute-start | bytes 786440 | tf_op jit(solution)/shard_map/ppermute | solution.py:420

commit v3 on v2

v3 whole, which is shorter than its diff:
```python
import functools

import jax
import jax.numpy as jnp
from jax import lax
from jax.experimental import pallas as pl
from jax.experimental.pallas import tpu as pltpu
from jax.sharding import PartitionSpec as P

F32 = jnp.float32
BF16 = jnp.bfloat16
VMEM_LIMIT = 24 * 1024 * 1024
VMEM_ALL = 60 * 1024 * 1024
CAP = 4


def params(limit=VMEM_LIMIT):
    return pltpu.CompilerParams(vmem_limit_bytes=limit)


def vspec():
    return pl.BlockSpec(memory_space=pltpu.VMEM)


def sspec():
    return pl.BlockSpec(memory_space=pltpu.SMEM)


def sds(shape, dtype):
    return jax.ShapeDtypeStruct(shape, dtype)


def edge_starts(g):
    first = jnp.where(g % 2 == 0, 12, 0)
    return first, 12 - first


def pack_kernel(
    vel_any, off, wt, route_any, send, vel, out, route_s, count, sems
):
    g = lax.axis_index("gz")
    d = lax.axis_index("xy")
    rows = pl.ds(pl.multiple_of(g * 8, 8), 8)
    load = pltpu.make_async_copy(route_any.at[rows], route_s, sems.at[0])
    bricks = [
        pltpu.make_async_copy(vel_any.at[pl.ds(8 * i, 8)], vel.at[pl.ds(8 * i, 8)], sems.at[1 + i])
        for i in range(4)
    ]
    for copy in [load] + bricks:
        copy.start()
    for i in range(32):
        count[i] = 0
    load.wait()
    row = d // 4
    first = (d % 4) * 32
    x = lax.broadcasted_iota(jnp.int32, (64, 128), 1)
    for r in range(32):
        if r % 8 == 0:
            bricks[r // 8].wait()
        dest = route_s[row, first + r]
        k = count[dest]
        count[dest] = k + 1
        o = off[r]
        v = vel[r].reshape(64, 128)
        moved = jnp.where(x < 128 - o, pltpu.roll(v, (128 - o) % 128, 1), 0.0)
        out[r] = (moved * wt[r]).astype(BF16)
        pltpu.make_async_copy(out.at[r], send.at[dest * CAP + k], sems.at[5]).start()
    pltpu.make_async_copy(out, send.at[pl.ds(0, 32)], sems.at[5]).wait()


def pack(velocity, offset, weight, route):
    anywhere = pl.BlockSpec(memory_space=pl.ANY)
    return pl.pallas_call(
        pack_kernel,
        out_shape=sds((32 * CAP, 64, 128), BF16),
        in_specs=[anywhere, sspec(), sspec(), anywhere],
        out_specs=anywhere,
        scratch_shapes=[
            pltpu.VMEM((32, 8, 8, 128), F32),
            pltpu.VMEM((32, 64, 128), BF16),
            pltpu.SMEM((8, 128), jnp.int32),
            pltpu.SMEM((32,), jnp.int32),
            pltpu.SemaphoreType.DMA((6,)),
        ],
        compiler_params=params(VMEM_ALL),
        name="pack",
    )(velocity, offset, weight, route)


def pair_rows(block):
    n = block.shape[0] // 2
    return jnp.stack(
        [jnp.concatenate([block[2 * i], block[2 * i + 1]], axis=0) for i in range(n)]
    )


def edge_pairs(field, y_even):
    lo = pair_rows(field[:, 0:8, :][:, 0:4])
    hi = pair_rows(field[:, 56:64, :][:, 4:8])
    return jnp.where(y_even, hi, lo), jnp.where(y_even, lo, hi)


def prepare_kernel(route, slot, cond, code, c_a, c_b, m_own):
    g = lax.axis_index("gz")
    d = lax.axis_index("xy")
    rows = pl.ds(pl.multiple_of(g * 8, 8), 8)
    lane = lax.broadcasted_iota(jnp.int32, (8, 128), 1) % 32
    mine = (route[rows, :] == d).astype(jnp.int32)
    upto = mine
    for step in (1, 2, 4, 8, 16):
        upto = upto + jnp.where(lane >= step, pltpu.roll(upto, step, 1), 0)
    rank = upto - mine
    word = jnp.where(mine > 0, (slot[rows, :] + 1) << (5 * rank), 0)
    for step in (1, 2, 4, 8, 16):
        word = word + jnp.where(lane >= step, pltpu.roll(word, step, 1), 0)
    code[...] = word
    z_hi, z_lo = edge_starts(g)
    c_a[...] = cond[pl.ds(z_hi, 4)]
    c_b[...] = cond[pl.ds(z_lo, 4)]
    m_own[0], m_own[1] = edge_pairs(cond, d % 2 == 0)


def prepare(route, slot, cond):
    return pl.pallas_call(
        prepare_kernel,
        out_shape=(
            sds((8, 128), jnp.int32),
            sds((4, 64, 128), F32),
            sds((4, 64, 128), F32),
            sds((2, 8, 8, 128), F32),
        ),
        in_specs=[vspec()] * 3,
        out_specs=(vspec(),) * 4,
        compiler_params=params(),
        name="prepare",
    )(route, slot, cond)


def combine_kernel(recv, code, v, z_a, z_b, y_own):
    g = lax.axis_index("gz")
    d = lax.axis_index("xy")
    v[...] = jnp.zeros_like(v)

    def source(s, carry):
        word = code[s // 4, (s % 4) * 32 + 31]
        for k in range(CAP):
            j = ((word >> (5 * k)) & 31) - 1

            @pl.when(j >= 0)
            def _():
                z0 = pl.multiple_of((j // 8) * 8, 8)
                y0 = pl.multiple_of((j % 8) * 8, 8)
                block = recv[s * CAP + k].astype(F32).reshape(8, 8, 128)
                v[pl.ds(z0, 8), pl.ds(y0, 8), :] += block

        return carry

    lax.fori_loop(0, 32, source, 0, unroll=4)
    z_hi, z_lo = edge_starts(g)
    z_a[...] = v[pl.ds(z_hi, 4)]
    z_b[...] = v[pl.ds(z_lo, 4)]
    y_own[0], y_own[1] = edge_pairs(v, d % 2 == 0)


def combine(recv, code):
    return pl.pallas_call(
        combine_kernel,
        out_shape=(
            sds((16, 64, 128), F32),
            sds((4, 64, 128), F32),
            sds((4, 64, 128), F32),
            sds((2, 8, 8, 128), F32),
        ),
        in_specs=[vspec(), sspec()],
        out_specs=(vspec(),) * 4,
        compiler_params=params(),
        name="combine",
    )(recv, code)


def strips_kernel(y_own, r_a, r_b, y_c, y_d):
    d = lax.axis_index("xy")
    y_even = d % 2 == 0
    y_c[0:8] = y_own[0]
    y_d[0:8] = y_own[1]
    for at, field in ((8, r_a), (10, r_b)):
        y_c[at : at + 2], y_d[at : at + 2] = edge_pairs(field, y_even)


def strips(y_own, r_a, r_b):
    return pl.pallas_call(
        strips_kernel,
        out_shape=(sds((12, 8, 128), F32),) * 2,
        in_specs=[vspec()] * 3,
        out_specs=(vspec(),) * 2,
        compiler_params=params(),
        name="strips",
    )(y_own, r_a, r_b)


def split3(x):
    hi = x.astype(BF16)
    rest = x - hi.astype(F32)
    mid = rest.astype(BF16)
    lo = (rest - mid.astype(F32)).astype(BF16)
    return hi, mid, lo


def band(taps):
    i = lax.broadcasted_iota(jnp.int32, (128, 128), 0)
    j = lax.broadcasted_iota(jnp.int32, (128, 128), 1)
    m = jnp.zeros((128, 128), F32)
    for place, tap in enumerate(taps):
        if tap:
            m = jnp.where(i - j == place - 2, F32(tap), m)
    return m.astype(BF16)


S_TAPS = (1.0, 4.0, 6.0, 4.0, 1.0)
D_TAPS = (1.0, -8.0, 0.0, 8.0, -1.0)
NORM = 1.0 / (16.0 * 16.0 * 12.0)


def smooth5(a):
    return (a[0] + a[4]) + 4.0 * (a[1] + a[3]) + 6.0 * a[2]


def deriv5(a):
    return (a[0] - a[4]) + 8.0 * (a[3] - a[1])


def dot(a, b):
    return jnp.dot(a, b, preferred_element_type=F32)


def fill(ext, field, r_a, r_b, q_c, q_d):
    g = lax.axis_index("gz")
    d = lax.axis_index("xy")
    even = g % 2 == 0
    y_even = d % 2 == 0
    at_a = jnp.where(even, 20, 0)
    at_b = 20 - at_a
    low_in = (g > 0).astype(F32)
    high_in = (g < 7).astype(F32)
    keep_a = jnp.where(even, high_in, low_in)
    keep_b = jnp.where(even, low_in, high_in)
    left_in = (d > 0).astype(F32)
    right_in = (d < 31).astype(F32)
    zeros4 = jnp.zeros((4, 128), F32)
    ext[4:20, 8:72, :] = field[...]
    ext[pl.ds(at_a, 4), 8:72, :] = r_a[...] * keep_a
    ext[pl.ds(at_b, 4), 8:72, :] = r_b[...] * keep_b
    for z in range(24):
        c = q_c[z // 2]
        e = q_d[z // 2]
        lo = jnp.where(y_even, e, c)[4 * (z % 2) : 4 * (z % 2) + 4] * left_in
        hi = jnp.where(y_even, c, e)[4 * (z % 2) : 4 * (z % 2) + 4] * right_in
        if z < 16:
            place, keep = z + 4, 1.0
        elif z < 20:
            place, keep = at_a + (z - 16), keep_a
        else:
            place, keep = at_b + (z - 20), keep_b
        ext[place, 0:8, :] = jnp.concatenate([zeros4, lo * keep], axis=0)
        ext[place, 72:80, :] = jnp.concatenate([hi * keep, zeros4], axis=0)


SHIFTS = (2, 1, 0, -1, -2)


def shifted(a):
    return [pltpu.roll(a, sh % 80, 0) for sh in SHIFTS]


def mix_xy(ext, sx, dx):
    weights = jnp.concatenate([band(S_TAPS), band(D_TAPS)], axis=1)
    twice = jnp.concatenate([weights, weights], axis=0)

    def along_x(i, carry):
        part = pl.ds(i * 12, 12)
        h, m, l = split3(ext[part].reshape(12 * 80, 128))
        both = dot(jnp.concatenate([h, m], axis=1), twice) + dot(l, weights)
        sx[part] = both[:, 0:128].reshape(12, 80, 128)
        dx[part] = both[:, 128:256].reshape(12, 80, 128)
        return carry

    lax.fori_loop(0, 2, along_x, 0)

    def along_y(z, carry):
        ss = shifted(sx[z])
        tt = shifted(dx[z])
        dx[z] = smooth5(tt)
        sx[z] = deriv5(ss)
        ext[z] = smooth5(ss)
        return carry

    lax.fori_loop(0, 24, along_y, 0, unroll=2)


def grad_tile(ext, sx, dx, z, tile):
    gx = smooth5([dx[z + i, tile, :] for i in range(5)])
    gy = smooth5([sx[z + i, tile, :] for i in range(5)])
    gz = deriv5([ext[z + i, tile, :] for i in range(5)])
    return gx, gy, gz


def model_kernel(cond, r_a, r_b, q_c, q_d, gm, ext, sx, dx):
    fill(ext, cond, r_a, r_b, q_c, q_d)
    mix_xy(ext, sx, dx)

    def tiles(t, carry):
        tile = pl.ds(pl.multiple_of(t * 8, 8), 8)
        for z in range(20):
            gx, gy, gz = grad_tile(ext, sx, dx, z, tile)
            gm[0, z, tile, :] = gx
            gm[1, z, tile, :] = gy
            gm[2, z, tile, :] = gz
        return carry

    lax.fori_loop(0, 10, tiles, 0)


def model(cond, r_a, r_b, q_c, q_d):
    return pl.pallas_call(
        model_kernel,
        out_shape=sds((3, 20, 80, 128), F32),
        in_specs=[vspec()] * 5,
        out_specs=vspec(),
        scratch_shapes=[pltpu.VMEM((24, 80, 128), F32)] * 3,
        compiler_params=params(),
        cost_estimate=pl.CostEstimate(flops=200_000_000, bytes_accessed=8_000_000, transcendentals=0),
        name="model",
    )(cond, r_a, r_b, q_c, q_d)


def stencil_kernel(v, r_a, r_b, q_c, q_d, gm, out, total, ext, sx, dx, adj, mid_u, mid_t):
    g = lax.axis_index("gz")
    d = lax.axis_index("xy")
    low_in = (g > 0).astype(F32)
    high_in = (g < 7).astype(F32)
    fill(ext, v, r_a, r_b, q_c, q_d)
    mix_xy(ext, sx, dx)
    row = lax.broadcasted_iota(jnp.int32, (8, 128), 0)

    def cross(t, carry):
        y0 = pl.multiple_of(t * 8, 8)
        y = row + (y0 - 8)
        inside = jnp.where((y >= 0) | (d > 0), NORM, 0.0)
        inside = jnp.where((y < 64) | (d < 31), inside, 0.0)
        tile = pl.ds(y0, 8)
        for z in range(20):
            scale = inside
            if z < 2:
                scale = inside * low_in
            if z >= 18:
                scale = inside * high_in
            mx, my, mz = [gm[i, z, tile, :] * scale for i in range(3)]
            vx, vy, vz = [a * scale for a in grad_tile(ext, sx, dx, z, tile)]
            cx = my * vz - mz * vy
            cy = mz * vx - mx * vz
            cz = mx * vy - my * vx
            adj[0, z, tile, :] = vy * cz - vz * cy
            adj[1, z, tile, :] = vz * cx - vx * cz
            adj[2, z, tile, :] = vx * cy - vy * cx
        return carry

    lax.fori_loop(0, 10, cross, 0)

    def back_yz(z, carry):
        p = smooth5([adj[0, z + i] for i in range(5)])
        q = smooth5([adj[1, z + i] for i in range(5)])
        r = deriv5([adj[2, z + i] for i in range(5)])
        mid_u[z] = smooth5(shifted(p))[8:72]
        mid_t[z] = (deriv5(shifted(q)) + smooth5(shifted(r)))[8:72]
        return carry

    lax.fori_loop(0, 16, back_yz, 0)

    w_s = band(S_TAPS)
    w_d = band(D_TAPS)
    w = jnp.concatenate([w_d, w_s], axis=0)
    total[0:8, :] = jnp.zeros((8, 128), F32)

    def back_x(i, carry):
        part = pl.ds(i * 8, 8)
        us = split3(mid_u[part].reshape(512, 128))
        ts = split3(mid_t[part].reshape(512, 128))
        acc = sum(dot(jnp.concatenate([a, b], axis=1), w) for a, b in zip(us, ts))
        acc = acc * NORM
        out[part] = acc.reshape(8, 64, 128).astype(BF16)
        total[0:8, :] += jnp.sum((acc * acc).reshape(64, 8, 128), axis=0)
        return carry

    lax.fori_loop(0, 2, back_x, 0, unroll=2)
    total[...] = jnp.broadcast_to(jnp.sum(total[0:8, :], axis=0, keepdims=True), (256, 128))


def stencil(v, r_a, r_b, q_c, q_d, gm):
    return pl.pallas_call(
        stencil_kernel,
        out_shape=(sds((16, 64, 128), BF16), sds((256, 128), F32)),
        in_specs=[vspec()] * 6,
        out_specs=(vspec(),) * 2,
        scratch_shapes=[
            pltpu.VMEM((24, 80, 128), F32),
            pltpu.VMEM((24, 80, 128), F32),
            pltpu.VMEM((24, 80, 128), F32),
            pltpu.VMEM((3, 20, 80, 128), F32),
            pltpu.VMEM((16, 64, 128), F32),
            pltpu.VMEM((16, 64, 128), F32),
        ],
        compiler_params=params(),
        name="stencil",
    )(v, r_a, r_b, q_c, q_d, gm)


def scale_kernel(cells, sums, *refs):
    pieces, out = refs[:-1], refs[-1]
    g = lax.axis_index("gz")
    total = jnp.sum(sums[...], axis=0, keepdims=True)
    total = jnp.sum(total, axis=1, keepdims=True)
    scale = 1.0 / jnp.sqrt(total / cells + 1e-06)
    scale = jnp.broadcast_to(scale, (64, 128))
    left, right, across = lax.rem(g + 6, 8), lax.rem(g + 2, 8), lax.rem(g + 4, 8)
    owners = (g, left, right, across, g ^ 1, left ^ 1, right ^ 1, across ^ 1)
    for piece, owner in zip(pieces, owners):
        for z in range(16):
            out[owner * 16 + z] = (piece[z].astype(F32) * scale).astype(BF16)


def scaled(cells, sums, pieces):
    return pl.pallas_call(
        functools.partial(scale_kernel, cells),
        out_shape=sds((128, 64, 128), BF16),
        in_specs=[vspec()] * (1 + len(pieces)),
        out_specs=vspec(),
        compiler_params=params(),
        name="scale",
    )(sums, *pieces)


def swap_odd(count):
    return [(i, (i + 1) % count if i % 2 else (i - 1) % count) for i in range(count)]


def swap_even(count):
    return [(i, i ^ 1) for i in range(count)]


def local(velocity, offset, interp_weight, route, dest_slot, conductivity):
    n_g = lax.axis_size("gz")
    n_x = lax.axis_size("xy")
    z_even, z_odd = swap_even(n_g), swap_odd(n_g)
    y_even, y_odd = swap_even(n_x), swap_odd(n_x)
    route = route.reshape(64, 128)
    send = pack(velocity, offset, interp_weight, route)
    send, route, dest_slot, conductivity = lax.optimization_barrier(
        (send, route, dest_slot, conductivity)
    )
    recv = lax.all_to_all(
        send.reshape(n_x, CAP * 64, 128), "xy", split_axis=0, concat_axis=0, tiled=True
    )
    code, c_a, c_b, m_own = prepare(route, dest_slot.reshape(64, 128), conductivity)
    rc_b = lax.ppermute(c_b, "gz", z_odd)
    rc_a = lax.ppermute(c_a, "gz", z_even)
    m_c, m_d = strips(m_own, rc_a, rc_b)
    qm_c = lax.ppermute(m_c, "xy", y_even)
    qm_d = lax.ppermute(m_d, "xy", y_odd)
    recv, code, qm_c, qm_d = lax.optimization_barrier((recv, code, qm_c, qm_d))
    v, z_a, z_b, y_own = combine(recv.reshape(n_x * CAP, 64, 128), code)
    r_b = lax.ppermute(z_b, "gz", z_odd)
    r_a = lax.ppermute(z_a, "gz", z_even)
    y_c, y_d = strips(y_own, r_a, r_b)
    y_c, y_d, qm_c, qm_d = lax.optimization_barrier((y_c, y_d, qm_c, qm_d))
    q_c = lax.ppermute(y_c, "xy", y_even)
    q_d = lax.ppermute(y_d, "xy", y_odd)
    gm = model(conductivity, rc_a, rc_b, qm_c, qm_d)
    grad, total = stencil(v, r_a, r_b, q_c, q_d, gm)
    core = swap_even(n_g)
    before = lax.ppermute(grad, "gz", [(i, (i + 2) % n_g) for i in range(n_g)])
    after = lax.ppermute(grad, "gz", [(i, (i - 2) % n_g) for i in range(n_g)])
    across = lax.ppermute(grad, "gz", [(i, (i + 4) % n_g) for i in range(n_g)])
    twin = lax.ppermute(grad, "gz", core)
    sums = lax.all_to_all(total, ("gz", "xy"), 0, 0, tiled=True)
    before, after, across, sums = lax.optimization_barrier((before, after, across, sums))
    others = [lax.ppermute(piece, "gz", core) for piece in (before, after, across)]
    pieces = [grad, before, after, across, twin] + others
    cells = float(n_g * n_x * 16 * 64 * 128)
    return scaled(cells, sums, pieces)


def solution(mesh):
    in_specs = (
        P(("gz", "xy"), None, None, None),
        P(("gz", "xy")),
        P(("gz", "xy")),
        P(),
        P(),
        P("gz", "xy", None),
    )
    out_specs = P(None, "xy", None)
    return jax.shard_map(local, mesh=mesh, in_specs=in_specs, out_specs=out_specs, check_vma=False)
```

time: 126 us -> 117 us (0.929)
  blocking collectives: 82.4 us -> 0 us
  waiting for transfers between devices: 15.3 us -> 57.9 us
  starting transfers between devices: 12.2 us -> 43.9 us
    all_to_all x3 -> x0, blocking collectives: 82.4 us -> none  [the longest x1 60.7 us: local(): lax.all_to_all(send.reshape(n_x, CAP * 64, 128), 'xy', split_axis=0, conc...]
    ppermute x9 -> x15, waiting for transfers between devices: 15.3 us -> 47.4 us  [the longest x1 34.5 us: local(): qm_d = lax.ppermute(m_d, 'xy', y_odd)]
    all_to_all x0 -> x2, starting transfers between devices: none -> 22.4 us  [the longest x1 12 us: local(): lax.all_to_all(send.reshape(n_x, CAP * 64, 128), 'xy', split_axis=0, conc...]
    all_to_all x0 -> x2, waiting for transfers between devices: none -> 10.5 us  [the longest x1 10.3 us: local(): sums = lax.all_to_all(total, ('gz', 'xy'), 0, 0, tiled=True)]
    ppermute x9 -> x15, starting transfers between devices: 12.2 us -> 21.5 us  [the longest x1 3.98 us: local(): qm_d = lax.ppermute(m_d, 'xy', y_odd)]
    pallas_call x1, Pallas kernels: 7.62 us -> 5.6 us  [stencil(): pl.pallas_call(stencil_kernel, out_shape=(sds((16, 64, 128), BF16), sds((...]
    pallas_call x3 -> x6, Pallas kernels: 6.26 us -> 8.22 us  [the longest x1 2.87 us: pack(): pl.pallas_call(pack_kernel, out_shape=sds((32 * CAP, 64, 128), BF16), in_...]
  transfers between devices with their start and end apart: 9 -> 17, of which waited for: 5 -> 10; matrix products, arithmetic and copies ran while one was open for 0% -> 0% of each run, Pallas kernels for 0% -> 3%
where the time goes in v3:
time: 117 us; the launch traced here: 118 us
  waiting for transfers between devices  57.9 us (49%)
  starting transfers between devices  43.9 us (38%)
  Pallas kernels  15.6 us (13%)
    ppermute x1, waiting for transfers between devices, local(): qm_d = lax.ppermute(m_d, 'xy', y_odd)  34.5 us
    all_to_all x1, starting transfers between devices, local(): lax.all_to_all(send.reshape(n_x, CAP * 64, 128), 'xy', split_axis=0, conc...  12 us
    all_to_all x1, starting transfers between devices, local(): sums = lax.all_to_all(total, ('gz', 'xy'), 0, 0, tiled=True)  10.4 us
    all_to_all x1, waiting for transfers between devices, local(): sums = lax.all_to_all(total, ('gz', 'xy'), 0, 0, tiled=True)  10.3 us
    pallas_call x1, Pallas kernels, stencil(): pl.pallas_call(stencil_kernel, out_shape=(sds((16, 64, 128), BF16), sds((...  5.6 us
    ppermute x1, starting transfers between devices, local(): qm_d = lax.ppermute(m_d, 'xy', y_odd)  3.98 us
    ppermute x1, waiting for transfers between devices, local(): rc_b = lax.ppermute(c_b, 'gz', z_odd)  3.5 us
    ppermute x1, waiting for transfers between devices, local(): r_b = lax.ppermute(z_b, 'gz', z_odd)  3.38 us
  transfers between devices with their start and end apart: 17, of which 10 were waited for; matrix products, arithmetic and copies ran while one was open for 0% of the time, Pallas kernels for 3%

profile of v3, /device:TPU:1, one launch (start us, length us, event | category | flops | bytes accessed | tf_op | source)
XLA Modules:
  0.0 117.5 jit_solution(2960905635939297582)
XLA Ops:
  0.0 2.9 %pack.1 = bf16[128,64,128]{2,1,0:T(8,128)(2,1)} custom-call(f32[32,8,8,128]{3,2,1,0:T(8,128)} %vel_any.1, s32[32]{0:T(128)} %off.1, f32[32]{0:T(128)} %wt.1, s32[64,128]{1,0:T(8,128)} %bitcast.10), custom_call_target="tpu_custom_call" | custom-call | tf_op jit(solution)/shard_map/pack/pallas_call | solution.py:73
  2.9 12.0 %all-to-all-start = ((bf16[32,256,128]{2,1,0:T(8,128)(2,1)}), bf16[32,256,128]{2,1,0:T(8,128)(2,1)S(1)}, u32[]{:S(2)}, u32[]{:S(2)}) async-start(bf16[32,256,128]{2,1,0:T(8,128)(2,1)} %bitcast.13), calls=%async_computation | async-start | bytes 4194304 | tf_op jit(solution)/shard_map/all_to_all | solution.py:460
  15.0 0.7 prepare.1
  15.7 1.0 collective-permute-start
  16.6 1.2 %collective-permute-start.1 = (f32[4,64,128]{2,1,0:T(8,128)S(1)}, f32[4,64,128]{2,1,0:T(8,128)S(1)}, u32[]{:S(2)}, u32[]{:S(2)}) collective-permute-start(f32[4,64,128]{2,1,0:T(8,128)S(1)} %get-tuple-element.42), channel_id=1, source_target_pairs={{0,224},{32,64},{64,32},{96,128},{128,96},{160,192},{192,160},{224... | collective-permute-start | bytes 393224 | tf_op jit(solution)/shard_map/ppermute | solution.py:464
  17.8 3.5 %collective-permute-done.1.r_b = f32[4,64,128]{2,1,0:T(8,128)S(1)} collective-permute-done((f32[4,64,128]{2,1,0:T(8,128)S(1)}, f32[4,64,128]{2,1,0:T(8,128)S(1)}, u32[]{:S(2)}, u32[]{:S(2)}) %collective-permute-start.1) | collective-permute-done | bytes 131104 | tf_op jit(solution)/shard_map/ppermute | solution.py:464
  21.3 1.6 %collective-permute-start.2 = (f32[12,8,128]{2,1,0:T(8,128)S(1)}, f32[12,8,128]{2,1,0:T(8,128)S(1)}, u32[]{:S(2)}, u32[]{:S(2)}) collective-permute-start(f32[12,8,128]{2,1,0:T(8,128)S(1)} %get-tuple-element.43), channel_id=1, source_target_pairs={{0,1},{1,0},{2,3},{3,2},{4,5},{5,4},{6,7},{7,6},{8,9},{9,8},{10,11... | collective-permute-start | bytes 147464 | tf_op jit(solution)/shard_map/ppermute | solution.py:467
  22.9 4.0 %collective-permute-start.3 = (f32[12,8,128]{2,1,0:T(8,128)S(1)}, f32[12,8,128]{2,1,0:T(8,128)S(1)}, u32[]{:S(2)}, u32[]{:S(2)}) collective-permute-start(f32[12,8,128]{2,1,0:T(8,128)S(1)} %get-tuple-element.44), channel_id=1, source_target_pairs={{0,31},{1,2},{2,1},{3,4},{4,3},{5,6},{6,5},{7,8},{8,7},{9,10},{10,... | collective-permute-start | bytes 147464 | tf_op jit(solution)/shard_map/ppermute | solution.py:468
  26.9 1.8 %collective-permute-done.2.q_c = f32[12,8,128]{2,1,0:T(8,128)S(1)} collective-permute-done((f32[12,8,128]{2,1,0:T(8,128)S(1)}, f32[12,8,128]{2,1,0:T(8,128)S(1)}, u32[]{:S(2)}, u32[]{:S(2)}) %collective-permute-start.2) | collective-permute-done | bytes 49184 | tf_op jit(solution)/shard_map/ppermute | solution.py:467
  28.7 34.5 %collective-permute-done.3.q_d = f32[12,8,128]{2,1,0:T(8,128)S(1)} collective-permute-done((f32[12,8,128]{2,1,0:T(8,128)S(1)}, f32[12,8,128]{2,1,0:T(8,128)S(1)}, u32[]{:S(2)}, u32[]{:S(2)}) %collective-permute-start.3) | collective-permute-done | bytes 49184 | tf_op jit(solution)/shard_map/ppermute | solution.py:468
  63.3 0.2 all-to-all-done
  63.4 2.1 %combine.1 = (f32[16,64,128]{2,1,0:T(8,128)S(1)}, f32[4,64,128]{2,1,0:T(8,128)S(1)}, f32[4,64,128]{2,1,0:T(8,128)S(1)}, f32[2,8,8,128]{3,2,1,0:T(8,128)S(1)}) custom-call(bf16[128,64,128]{2,1,0:T(8,128)(2,1)S(1)} %bitcast.8, s32[8,128]{1,0:T(8,128)S(1)} %get-tuple-element.46.code), custom_call_target="tpu_custom_call" | custom-call | tf_op jit(solution)/shard_map/combine/pallas_call | solution.py:166
  65.6 2.8 %collective-permute-start.4 = (f32[4,64,128]{2,1,0:T(8,128)S(1)}, f32[4,64,128]{2,1,0:T(8,128)S(1)}, u32[]{:S(2)}, u32[]{:S(2)}) collective-permute-start(f32[4,64,128]{2,1,0:T(8,128)S(1)} %get-tuple-element.48), channel_id=1, source_target_pairs={{0,32},{32,0},{64,96},{96,64},{128,160},{160,128},{192,224},{224,1... | collective-permute-start | bytes 393224 | tf_op jit(solution)/shard_map/ppermute | solution.py:472
  68.3 1.3 %collective-permute-start.5 = (f32[4,64,128]{2,1,0:T(8,128)S(1)}, f32[4,64,128]{2,1,0:T(8,128)S(1)}, u32[]{:S(2)}, u32[]{:S(2)}) collective-permute-start(f32[4,64,128]{2,1,0:T(8,128)S(1)} %get-tuple-element.49), channel_id=1, source_target_pairs={{0,224},{32,64},{64,32},{96,128},{128,96},{160,192},{192,160},{224... | collective-permute-start | bytes 393224 | tf_op jit(solution)/shard_map/ppermute | solution.py:471
  69.6 3.4 %collective-permute-done.5.r_b = f32[4,64,128]{2,1,0:T(8,128)S(1)} collective-permute-done((f32[4,64,128]{2,1,0:T(8,128)S(1)}, f32[4,64,128]{2,1,0:T(8,128)S(1)}, u32[]{:S(2)}, u32[]{:S(2)}) %collective-permute-start.5) | collective-permute-done | bytes 131104 | tf_op jit(solution)/shard_map/ppermute | solution.py:471
  73.0 0.7 collective-permute-start.6
  73.7 1.0 collective-permute-start.7
  74.8 2.5 %model.1.gm = f32[3,20,80,128]{3,2,1,0:T(8,128)S(1)} custom-call(f32[16,64,128]{2,1,0:T(8,128)S(1)} %copy-done, f32[4,64,128]{2,1,0:T(8,128)S(1)} %collective-permute-done.r_a, f32[4,64,128]{2,1,0:T(8,128)S(1)} %collective-permute-done.1.r_b, f32[12,8,128]{2,1,0:T(8,128)S(1)} %collective-permute-done.2.q_c, f32[12,8,128]{2,1,0:T(8,128)S(1)} %collective-permute-done.3.q_d), custom_call_target="tpu_custom_call" | custom-call | flops 200000000 | bytes 8000000 | tf_op jit(solution)/shard_map/model/pallas_call | solution.py:324
  77.2 2.7 %collective-permute-done.7.q_d = f32[12,8,128]{2,1,0:T(8,128)S(1)} collective-permute-done((f32[12,8,128]{2,1,0:T(8,128)S(1)}, f32[12,8,128]{2,1,0:T(8,128)S(1)}, u32[]{:S(2)}, u32[]{:S(2)}) %collective-permute-start.7) | collective-permute-done | bytes 49184 | tf_op jit(solution)/shard_map/ppermute | solution.py:476
  80.0 5.6 %stencil.1 = (bf16[16,64,128]{2,1,0:T(8,128)(2,1)S(1)}, f32[256,128]{1,0:T(8,128)}) custom-call(f32[16,64,128]{2,1,0:T(8,128)S(1)} %get-tuple-element.47.v, f32[4,64,128]{2,1,0:T(8,128)S(1)} %collective-permute-done.4.r_a, f32[4,64,128]{2,1,0:T(8,128)S(1)} %collective-permute-done.5.r_b, f32[12,8,128]{2,1,0:T(8,128)S(1)} %collective-permute-done.6.q_c, ...), custom_call_target="tpu_custom_call" | custom-call | tf_op jit(solution)/shard_map/stencil/pallas_call | solution.py:399
  85.6 2.6 %collective-permute-start.10 = (bf16[16,64,128]{2,1,0:T(8,128)(2,1)S(1)}, bf16[16,64,128]{2,1,0:T(8,128)(2,1)S(1)}, u32[]{:S(2)}, u32[]{:S(2)}) collective-permute-start(bf16[16,64,128]{2,1,0:T(8,128)(2,1)S(1)} %get-tuple-element.59.refs_0_), channel_id=1, source_target_pairs={{0,128},{32,160},{64,192},{96,224},{128,0},{160,32},{192,64},{224,... | collective-permute-start | bytes 786440 | tf_op jit(solution)/shard_map/ppermute | solution.py:482
  88.2 1.2 %collective-permute-start.9 = (bf16[16,64,128]{2,1,0:T(8,128)(2,1)S(1)}, bf16[16,64,128]{2,1,0:T(8,128)(2,1)S(1)}, u32[]{:S(2)}, u32[]{:S(2)}) collective-permute-start(bf16[16,64,128]{2,1,0:T(8,128)(2,1)S(1)} %get-tuple-element.59.refs_0_), channel_id=1, source_target_pairs={{0,192},{32,224},{64,0},{96,32},{128,64},{160,96},{192,128},{224,1... | collective-permute-start | bytes 786440 | tf_op jit(solution)/shard_map/ppermute | solution.py:481
  89.4 0.6 collective-permute-start.8
  90.0 10.4 %all-to-all-start.1 = ((f32[256,1,128]{2,1,0:T(1,128)}), f32[256,1,128]{2,1,0:T(1,128)S(1)}, u32[]{:S(2)}, u32[]{:S(2)}) async-start(f32[256,1,128]{2,1,0:T(1,128)} %bitcast.5), calls=%async_computation.1 | async-start | bytes 262144 | tf_op jit(solution)/shard_map/all_to_all | solution.py:484
  100.4 2.2 %collective-permute-start.11 = (bf16[16,64,128]{2,1,0:T(8,128)(2,1)S(1)}, bf16[16,64,128]{2,1,0:T(8,128)(2,1)S(1)}, u32[]{:S(2)}, u32[]{:S(2)}) collective-permute-start(bf16[16,64,128]{2,1,0:T(8,128)(2,1)S(1)} %get-tuple-element.59.refs_0_), channel_id=1, source_target_pairs={{0,32},{32,0},{64,96},{96,64},{128,160},{160,128},{192,224},{224,1... | collective-permute-start | bytes 786440 | tf_op jit(solution)/shard_map/ppermute | solution.py:483
  102.6 10.3 %all-to-all-done.1 = f32[256,1,128]{2,1,0:T(1,128)S(1)} async-done(((f32[256,1,128]{2,1,0:T(1,128)}), f32[256,1,128]{2,1,0:T(1,128)S(1)}, u32[]{:S(2)}, u32[]{:S(2)}) %all-to-all-start.1) | async-done | bytes 131104 | tf_op jit(solution)/shard_map/all_to_all | solution.py:484
  113.0 0.8 collective-permute-start.12
  113.9 0.4 collective-permute-start.14
  114.3 0.6 collective-permute-done.12.refs_5_
  115.0 0.4 collective-permute-done.13.refs_6_
  115.4 0.4 collective-permute-done.14.refs_7_
  115.7 1.8 %scale.1 = bf16[128,64,128]{2,1,0:T(8,128)(2,1)} custom-call(f32[256,128]{1,0:T(8,128)S(1)} %bitcast.9, bf16[16,64,128]{2,1,0:T(8,128)(2,1)S(1)} %get-tuple-element.59.refs_0_, bf16[16,64,128]{2,1,0:T(8,128)(2,1)S(1)} %collective-permute-done.8.refs_1_, bf16[16,64,128]{2,1,0:T(8,128)(2,1)S(1)} %collective-permute-done.9.refs_2_, ...), custom_call_target="tpu_custom_call" | custom-call | tf_op jit(solution)/shard_map/scale/pallas_call | solution.py:432
  (16 shorter events, 0.2 us)
Async XLA Ops:
  2.9 12.1 %copy-start = (f32[16,64,128]{2,1,0:T(8,128)S(1)}, f32[16,64,128]{2,1,0:T(8,128)}, u32[]{:S(2)}) copy-start(f32[16,64,128]{2,1,0:T(8,128)} %cond.1) | copy-start | bytes 1572868
  2.9 12.1 %copy-start.1 = (s32[8192,1]{0,1:T(1,128)S(1)}, s32[8192,1]{0,1:T(1,128)}, u32[]{:S(2)}) copy-start(s32[8192,1]{0,1:T(1,128)} %param.9) | copy-start | bytes 98308
  2.9 12.1 %copy-start.2 = (s32[8192]{0:T(1024)S(1)}, s32[8192]{0:T(1024)}, u32[]{:S(2)}) copy-start(s32[8192]{0:T(1024)} %param.10) | copy-start | bytes 98308
  2.9 60.5 %all-to-all-start = ((bf16[32,256,128]{2,1,0:T(8,128)(2,1)}), bf16[32,256,128]{2,1,0:T(8,128)(2,1)S(1)}, u32[]{:S(2)}, u32[]{:S(2)}) async-start(bf16[32,256,128]{2,1,0:T(8,128)(2,1)} %bitcast.13), calls=%async_computation | async-start | bytes 4194304 | tf_op jit(solution)/shard_map/all_to_all | solution.py:460
  15.7 2.1 %collective-permute-start = (f32[4,64,128]{2,1,0:T(8,128)S(1)}, f32[4,64,128]{2,1,0:T(8,128)S(1)}, u32[]{:S(2)}, u32[]{:S(2)}) collective-permute-start(f32[4,64,128]{2,1,0:T(8,128)S(1)} %get-tuple-element.41), channel_id=1, source_target_pairs={{0,32},{32,0},{64,96},{96,64},{128,160},{160,128},{192,224},{224,1... | collective-permute-start | bytes 393224 | tf_op jit(solution)/shard_map/ppermute | solution.py:465
  16.6 4.7 %collective-permute-start.1 = (f32[4,64,128]{2,1,0:T(8,128)S(1)}, f32[4,64,128]{2,1,0:T(8,128)S(1)}, u32[]{:S(2)}, u32[]{:S(2)}) collective-permute-start(f32[4,64,128]{2,1,0:T(8,128)S(1)} %get-tuple-element.42), channel_id=1, source_target_pairs={{0,224},{32,64},{64,32},{96,128},{128,96},{160,192},{192,160},{224... | collective-permute-start | bytes 393224 | tf_op jit(solution)/shard_map/ppermute | solution.py:464
  21.3 7.4 %collective-permute-start.2 = (f32[12,8,128]{2,1,0:T(8,128)S(1)}, f32[12,8,128]{2,1,0:T(8,128)S(1)}, u32[]{:S(2)}, u32[]{:S(2)}) collective-permute-start(f32[12,8,128]{2,1,0:T(8,128)S(1)} %get-tuple-element.43), channel_id=1, source_target_pairs={{0,1},{1,0},{2,3},{3,2},{4,5},{5,4},{6,7},{7,6},{8,9},{9,8},{10,11... | collective-permute-start | bytes 147464 | tf_op jit(solution)/shard_map/ppermute | solution.py:467
  22.9 40.3 %collective-permute-start.3 = (f32[12,8,128]{2,1,0:T(8,128)S(1)}, f32[12,8,128]{2,1,0:T(8,128)S(1)}, u32[]{:S(2)}, u32[]{:S(2)}) collective-permute-start(f32[12,8,128]{2,1,0:T(8,128)S(1)} %get-tuple-element.44), channel_id=1, source_target_pairs={{0,31},{1,2},{2,1},{3,4},{4,3},{5,6},{6,5},{7,8},{8,7},{9,10},{10,... | collective-permute-start | bytes 147464 | tf_op jit(solution)/shard_map/ppermute | solution.py:468
  65.6 4.1 %collective-permute-start.4 = (f32[4,64,128]{2,1,0:T(8,128)S(1)}, f32[4,64,128]{2,1,0:T(8,128)S(1)}, u32[]{:S(2)}, u32[]{:S(2)}) collective-permute-start(f32[4,64,128]{2,1,0:T(8,128)S(1)} %get-tuple-element.48), channel_id=1, source_target_pairs={{0,32},{32,0},{64,96},{96,64},{128,160},{160,128},{192,224},{224,1... | collective-permute-start | bytes 393224 | tf_op jit(solution)/shard_map/ppermute | solution.py:472
  68.3 4.7 %collective-permute-start.5 = (f32[4,64,128]{2,1,0:T(8,128)S(1)}, f32[4,64,128]{2,1,0:T(8,128)S(1)}, u32[]{:S(2)}, u32[]{:S(2)}) collective-permute-start(f32[4,64,128]{2,1,0:T(8,128)S(1)} %get-tuple-element.49), channel_id=1, source_target_pairs={{0,224},{32,64},{64,32},{96,128},{128,96},{160,192},{192,160},{224... | collective-permute-start | bytes 393224 | tf_op jit(solution)/shard_map/ppermute | solution.py:471
  73.0 4.2 %collective-permute-start.6 = (f32[12,8,128]{2,1,0:T(8,128)S(1)}, f32[12,8,128]{2,1,0:T(8,128)S(1)}, u32[]{:S(2)}, u32[]{:S(2)}) collective-permute-start(f32[12,8,128]{2,1,0:T(8,128)S(1)} %get-tuple-element.55), channel_id=1, source_target_pairs={{0,1},{1,0},{2,3},{3,2},{4,5},{5,4},{6,7},{7,6},{8,9},{9,8},{10,11... | collective-permute-start | bytes 147464 | tf_op jit(solution)/shard_map/ppermute | solution.py:475
  73.7 6.3 %collective-permute-start.7 = (f32[12,8,128]{2,1,0:T(8,128)S(1)}, f32[12,8,128]{2,1,0:T(8,128)S(1)}, u32[]{:S(2)}, u32[]{:S(2)}) collective-permute-start(f32[12,8,128]{2,1,0:T(8,128)S(1)} %get-tuple-element.56), channel_id=1, source_target_pairs={{0,31},{1,2},{2,1},{3,4},{4,3},{5,6},{6,5},{7,8},{8,7},{9,10},{10,... | collective-permute-start | bytes 147464 | tf_op jit(solution)/shard_map/ppermute | solution.py:476
  85.6 27.4 %collective-permute-start.10 = (bf16[16,64,128]{2,1,0:T(8,128)(2,1)S(1)}, bf16[16,64,128]{2,1,0:T(8,128)(2,1)S(1)}, u32[]{:S(2)}, u32[]{:S(2)}) collective-permute-start(bf16[16,64,128]{2,1,0:T(8,128)(2,1)S(1)} %get-tuple-element.59.refs_0_), channel_id=1, source_target_pairs={{0,128},{32,160},{64,192},{96,224},{128,0},{160,32},{192,64},{224,... | collective-permute-start | bytes 786440 | tf_op jit(solution)/shard_map/ppermute | solution.py:482
  88.2 24.8 %collective-permute-start.9 = (bf16[16,64,128]{2,1,0:T(8,128)(2,1)S(1)}, bf16[16,64,128]{2,1,0:T(8,128)(2,1)S(1)}, u32[]{:S(2)}, u32[]{:S(2)}) collective-permute-start(bf16[16,64,128]{2,1,0:T(8,128)(2,1)S(1)} %get-tuple-element.59.refs_0_), channel_id=1, source_target_pairs={{0,192},{32,224},{64,0},{96,32},{128,64},{160,96},{192,128},{224,1... | collective-permute-start | bytes 786440 | tf_op jit(solution)/shard_map/ppermute | solution.py:481
  89.4 23.6 %collective-permute-start.8 = (bf16[16,64,128]{2,1,0:T(8,128)(2,1)S(1)}, bf16[16,64,128]{2,1,0:T(8,128)(2,1)S(1)}, u32[]{:S(2)}, u32[]{:S(2)}) collective-permute-start(bf16[16,64,128]{2,1,0:T(8,128)(2,1)S(1)} %get-tuple-element.59.refs_0_), channel_id=1, source_target_pairs={{0,64},{32,96},{64,128},{96,160},{128,192},{160,224},{192,0},{224,... | collective-permute-start | bytes 786440 | tf_op jit(solution)/shard_map/ppermute | solution.py:480
  90.0 23.0 %all-to-all-start.1 = ((f32[256,1,128]{2,1,0:T(1,128)}), f32[256,1,128]{2,1,0:T(1,128)S(1)}, u32[]{:S(2)}, u32[]{:S(2)}) async-start(f32[256,1,128]{2,1,0:T(1,128)} %bitcast.5), calls=%async_computation.1 | async-start | bytes 262144 | tf_op jit(solution)/shard_map/all_to_all | solution.py:484
  100.4 13.9 %collective-permute-start.11 = (bf16[16,64,128]{2,1,0:T(8,128)(2,1)S(1)}, bf16[16,64,128]{2,1,0:T(8,128)(2,1)S(1)}, u32[]{:S(2)}, u32[]{:S(2)}) collective-permute-start(bf16[16,64,128]{2,1,0:T(8,128)(2,1)S(1)} %get-tuple-element.59.refs_0_), channel_id=1, source_target_pairs={{0,32},{32,0},{64,96},{96,64},{128,160},{160,128},{192,224},{224,1... | collective-permute-start | bytes 786440 | tf_op jit(solution)/shard_map/ppermute | solution.py:483
  113.0 2.0 %collective-permute-start.12 = (bf16[16,64,128]{2,1,0:T(8,128)(2,1)S(1)}, bf16[16,64,128]{2,1,0:T(8,128)(2,1)S(1)}, u32[]{:S(2)}, u32[]{:S(2)}) collective-permute-start(bf16[16,64,128]{2,1,0:T(8,128)(2,1)S(1)} %collective-permute-done.8.refs_1_), channel_id=1, source_target_pairs={{0,32},{32,0},{64,96},{96,64},{128,160},{160,128},{192,224},{224,1... | collective-permute-start | bytes 786440 | tf_op jit(solution)/shard_map/ppermute | solution.py:486
  113.8 1.5 %collective-permute-start.13 = (bf16[16,64,128]{2,1,0:T(8,128)(2,1)S(1)}, bf16[16,64,128]{2,1,0:T(8,128)(2,1)S(1)}, u32[]{:S(2)}, u32[]{:S(2)}) collective-permute-start(bf16[16,64,128]{2,1,0:T(8,128)(2,1)S(1)} %collective-permute-done.9.refs_2_), channel_id=1, source_target_pairs={{0,32},{32,0},{64,96},{96,64},{128,160},{160,128},{192,224},{224,1... | collective-permute-start | bytes 786440 | tf_op jit(solution)/shard_map/ppermute | solution.py:486
  113.9 1.8 %collective-permute-start.14 = (bf16[16,64,128]{2,1,0:T(8,128)(2,1)S(1)}, bf16[16,64,128]{2,1,0:T(8,128)(2,1)S(1)}, u32[]{:S(2)}, u32[]{:S(2)}) collective-permute-start(bf16[16,64,128]{2,1,0:T(8,128)(2,1)S(1)} %collective-permute-done.10.refs_3_), channel_id=1, source_target_pairs={{0,32},{32,0},{64,96},{96,64},{128,160},{160,128},{192,224},{224,1... | collective-permute-start | bytes 786440 | tf_op jit(solution)/shard_map/ppermute | solution.py:486

commit v4 on v3

--- a/solution.py
+++ b/solution.py
@@ -136,10 +136,9 @@
     )(route, slot, cond)
 
 
-def combine_kernel(recv, code, v, z_a, z_b, y_own):
-    g = lax.axis_index("gz")
-    d = lax.axis_index("xy")
-    v[...] = jnp.zeros_like(v)
+def lists_kernel(code, count, entries):
+    for j in range(16):
+        count[j] = 0
 
     def source(s, carry):
         word = code[s // 4, (s % 4) * 32 + 31]
@@ -148,21 +147,44 @@
 
             @pl.when(j >= 0)
             def _():
-                z0 = pl.multiple_of((j // 8) * 8, 8)
-                y0 = pl.multiple_of((j % 8) * 8, 8)
-                block = recv[s * CAP + k].astype(F32).reshape(8, 8, 128)
-                v[pl.ds(z0, 8), pl.ds(y0, 8), :] += block
+                n = count[j]
+                entries[j * 128 + n] = s * CAP + k
+                count[j] = n + 1
 
         return carry
 
-    lax.fori_loop(0, 32, source, 0, unroll=4)
+    lax.fori_loop(0, 32, source, 0)
+
+
+def lists(code):
+    return pl.pallas_call(
+        lists_kernel,
+        out_shape=(sds((16,), jnp.int32), sds((16 * 128,), jnp.int32)),
+        in_specs=[sspec()],
+        out_specs=(sspec(), sspec()),
+        compiler_params=params(),
+        name="lists",
+    )(code)
+
+
+def combine_kernel(recv, count, entries, v, z_a, z_b, y_own):
+    g = lax.axis_index("gz")
+    d = lax.axis_index("xy")
+    for j in range(16):
+
+        def record(i, acc):
+            return acc + recv[entries[j * 128 + i]].astype(F32)
+
+        block = lax.fori_loop(0, count[j], record, jnp.zeros((64, 128), F32))
+        z0, y0 = (j // 8) * 8, (j % 8) * 8
+        v[z0 : z0 + 8, y0 : y0 + 8, :] = block.reshape(8, 8, 128)
     z_hi, z_lo = edge_starts(g)
     z_a[...] = v[pl.ds(z_hi, 4)]
     z_b[...] = v[pl.ds(z_lo, 4)]
     y_own[0], y_own[1] = edge_pairs(v, d % 2 == 0)
 
 
-def combine(recv, code):
+def combine(recv, count, entries):
     return pl.pallas_call(
         combine_kernel,
         out_shape=(
@@ -171,11 +193,11 @@
             sds((4, 64, 128), F32),
             sds((2, 8, 8, 128), F32),
         ),
-        in_specs=[vspec(), sspec()],
+        in_specs=[vspec(), sspec(), sspec()],
         out_specs=(vspec(),) * 4,
         compiler_params=params(),
         name="combine",
-    )(recv, code)
+    )(recv, count, entries)
 
 
 def strips_kernel(y_own, r_a, r_b, y_c, y_d):
@@ -265,13 +287,6 @@
         ext[place, 72:80, :] = jnp.concatenate([hi * keep, zeros4], axis=0)
 
 
-SHIFTS = (2, 1, 0, -1, -2)
-
-
-def shifted(a):
-    return [pltpu.roll(a, sh % 80, 0) for sh in SHIFTS]
-
-
 def mix_xy(ext, sx, dx):
     weights = jnp.concatenate([band(S_TAPS), band(D_TAPS)], axis=1)
     twice = jnp.concatenate([weights, weights], axis=0)
@@ -287,11 +302,12 @@
     lax.fori_loop(0, 2, along_x, 0)
 
     def along_y(z, carry):
-        ss = shifted(sx[z])
-        tt = shifted(dx[z])
-        dx[z] = smooth5(tt)
-        sx[z] = deriv5(ss)
-        ext[z] = smooth5(ss)
+        ss = [sx[z, 2 + i : 74 + i, :] for i in range(5)]
+        tt = [dx[z, 2 + i : 74 + i, :] for i in range(5)]
+        yx, xy, yy = smooth5(tt), deriv5(ss), smooth5(ss)
+        dx[z, 4:76, :] = yx
+        sx[z, 4:76, :] = xy
+        ext[z, 4:76, :] = yy
         return carry
 
     lax.fori_loop(0, 24, along_y, 0, unroll=2)
@@ -333,7 +349,7 @@
     )(cond, r_a, r_b, q_c, q_d)
 
 
-def stencil_kernel(v, r_a, r_b, q_c, q_d, gm, out, total, ext, sx, dx, adj, mid_u, mid_t):
+def stencil_kernel(v, r_a, r_b, q_c, q_d, gm, out, total, ext, sx, dx, back):
     g = lax.axis_index("gz")
     d = lax.axis_index("xy")
     low_in = (g > 0).astype(F32)
@@ -348,6 +364,7 @@
         inside = jnp.where((y >= 0) | (d > 0), NORM, 0.0)
         inside = jnp.where((y < 64) | (d < 31), inside, 0.0)
         tile = pl.ds(y0, 8)
+        adj = []
         for z in range(20):
             scale = inside
             if z < 2:
@@ -359,39 +376,35 @@
             cx = my * vz - mz * vy
             cy = mz * vx - mx * vz
             cz = mx * vy - my * vx
-            adj[0, z, tile, :] = vy * cz - vz * cy
-            adj[1, z, tile, :] = vz * cx - vx * cz
-            adj[2, z, tile, :] = vx * cy - vy * cx
+            adj.append((vy * cz - vz * cy, vz * cx - vx * cz, vx * cy - vy * cx))
+            if z >= 4:
+                ax, ay, az = zip(*adj[z - 4 :])
+                back[0, z - 4, tile, :] = smooth5(ax)
+                back[1, z - 4, tile, :] = smooth5(ay)
+                back[2, z - 4, tile, :] = deriv5(az)
         return carry
 
     lax.fori_loop(0, 10, cross, 0)
-
-    def back_yz(z, carry):
-        p = smooth5([adj[0, z + i] for i in range(5)])
-        q = smooth5([adj[1, z + i] for i in range(5)])
-        r = deriv5([adj[2, z + i] for i in range(5)])
-        mid_u[z] = smooth5(shifted(p))[8:72]
-        mid_t[z] = (deriv5(shifted(q)) + smooth5(shifted(r)))[8:72]
-        return carry
-
-    lax.fori_loop(0, 16, back_yz, 0)
 
     w_s = band(S_TAPS)
     w_d = band(D_TAPS)
     w = jnp.concatenate([w_d, w_s], axis=0)
     total[0:8, :] = jnp.zeros((8, 128), F32)
 
-    def back_x(i, carry):
+    w = jnp.concatenate([w, w, w], axis=0)
+
+    def back_xy(i, carry):
         part = pl.ds(i * 8, 8)
-        us = split3(mid_u[part].reshape(512, 128))
-        ts = split3(mid_t[part].reshape(512, 128))
-        acc = sum(dot(jnp.concatenate([a, b], axis=1), w) for a, b in zip(us, ts))
-        acc = acc * NORM
+        p, q, r = [[back[j, part, 6 + k : 70 + k, :] for k in range(5)] for j in range(3)]
+        us = split3(smooth5(p).reshape(512, 128))
+        ts = split3((deriv5(q) + smooth5(r)).reshape(512, 128))
+        both = [x for pair in zip(us, ts) for x in pair]
+        acc = dot(jnp.concatenate(both, axis=1), w) * NORM
         out[part] = acc.reshape(8, 64, 128).astype(BF16)
         total[0:8, :] += jnp.sum((acc * acc).reshape(64, 8, 128), axis=0)
         return carry
 
-    lax.fori_loop(0, 2, back_x, 0, unroll=2)
+    lax.fori_loop(0, 2, back_xy, 0, unroll=2)
     total[...] = jnp.broadcast_to(jnp.sum(total[0:8, :], axis=0, keepdims=True), (256, 128))
 
 
@@ -405,9 +418,7 @@
             pltpu.VMEM((24, 80, 128), F32),
             pltpu.VMEM((24, 80, 128), F32),
             pltpu.VMEM((24, 80, 128), F32),
-            pltpu.VMEM((3, 20, 80, 128), F32),
-            pltpu.VMEM((16, 64, 128), F32),
-            pltpu.VMEM((16, 64, 128), F32),
+            pltpu.VMEM((3, 16, 80, 128), F32),
         ],
         compiler_params=params(),
         name="stencil",
@@ -415,7 +426,7 @@
 
 
 def scale_kernel(cells, sums, *refs):
-    pieces, out = refs[:-1], refs[-1]
+    pieces, out, held, sems = refs[:-3], refs[-3], refs[-2], refs[-1]
     g = lax.axis_index("gz")
     total = jnp.sum(sums[...], axis=0, keepdims=True)
     total = jnp.sum(total, axis=1, keepdims=True)
@@ -423,9 +434,15 @@
     scale = jnp.broadcast_to(scale, (64, 128))
     left, right, across = lax.rem(g + 6, 8), lax.rem(g + 2, 8), lax.rem(g + 4, 8)
     owners = (g, left, right, across, g ^ 1, left ^ 1, right ^ 1, across ^ 1)
-    for piece, owner in zip(pieces, owners):
+    copies = []
+    for k, (piece, owner) in enumerate(zip(pieces, owners)):
         for z in range(16):
-            out[owner * 16 + z] = (piece[z].astype(F32) * scale).astype(BF16)
+            held[k, z] = (piece[z].astype(F32) * scale).astype(BF16)
+        copy = pltpu.make_async_copy(held.at[k], out.at[pl.ds(owner * 16, 16)], sems.at[k])
+        copy.start()
+        copies.append(copy)
+    for copy in copies:
+        copy.wait()
 
 
 def scaled(cells, sums, pieces):
@@ -433,7 +450,8 @@
         functools.partial(scale_kernel, cells),
         out_shape=sds((128, 64, 128), BF16),
         in_specs=[vspec()] * (1 + len(pieces)),
-        out_specs=vspec(),
+        out_specs=pl.BlockSpec(memory_space=pl.ANY),
+        scratch_shapes=[pltpu.VMEM((8, 16, 64, 128), BF16), pltpu.SemaphoreType.DMA((8,))],
         compiler_params=params(),
         name="scale",
     )(sums, *pieces)
@@ -466,15 +484,16 @@
     m_c, m_d = strips(m_own, rc_a, rc_b)
     qm_c = lax.ppermute(m_c, "xy", y_even)
     qm_d = lax.ppermute(m_d, "xy", y_odd)
-    recv, code, qm_c, qm_d = lax.optimization_barrier((recv, code, qm_c, qm_d))
-    v, z_a, z_b, y_own = combine(recv.reshape(n_x * CAP, 64, 128), code)
+    count, entries = lists(code)
+    recv, count, entries, qm_c, qm_d = lax.optimization_barrier((recv, count, entries, qm_c, qm_d))
+    v, z_a, z_b, y_own = combine(recv.reshape(n_x * CAP, 64, 128), count, entries)
+    z_a, z_b, qm_c, qm_d = lax.optimization_barrier((z_a, z_b, qm_c, qm_d))
     r_b = lax.ppermute(z_b, "gz", z_odd)
     r_a = lax.ppermute(z_a, "gz", z_even)
+    gm = model(conductivity, rc_a, rc_b, qm_c, qm_d)
     y_c, y_d = strips(y_own, r_a, r_b)
-    y_c, y_d, qm_c, qm_d = lax.optimization_barrier((y_c, y_d, qm_c, qm_d))
     q_c = lax.ppermute(y_c, "xy", y_even)
     q_d = lax.ppermute(y_d, "xy", y_odd)
-    gm = model(conductivity, rc_a, rc_b, qm_c, qm_d)
     grad, total = stencil(v, r_a, r_b, q_c, q_d, gm)
     core = swap_even(n_g)
     before = lax.ppermute(grad, "gz", [(i, (i + 2) % n_g) for i in range(n_g)])

time: 117 us -> 114 us (0.974)
  starting transfers between devices: 43.9 us -> 41.5 us
  waiting for transfers between devices: 57.9 us -> 56.3 us
    pallas_call x0 -> x1, Pallas kernels: none -> 2.43 us  [lists(): pl.pallas_call(lists_kernel, out_shape=(sds((16,), jnp.int32), sds((16 *...]
    ppermute x1, waiting for transfers between devices: 1.82 us -> 0.01 us  [local(): qm_c = lax.ppermute(m_c, 'xy', y_even)]
    all_to_all x1, starting transfers between devices: 10.4 us -> 9.1 us  [local(): sums = lax.all_to_all(total, ('gz', 'xy'), 0, 0, tiled=True)]
  transfers between devices with their start and end apart: 17 -> 17, of which waited for: 10 -> 10; matrix products, arithmetic and copies ran while one was open for 0% -> 0% of each run, Pallas kernels for 3% -> 4%
where the time goes in v4:
time: 114 us
  waiting for transfers between devices  56.3 us (49%)
  starting transfers between devices  41.5 us (36%)
  Pallas kernels  15.9 us (14%)
    ppermute x1, waiting for transfers between devices, local(): qm_d = lax.ppermute(m_d, 'xy', y_odd)  33.9 us
    all_to_all x1, starting transfers between devices, local(): lax.all_to_all(send.reshape(n_x, CAP * 64, 128), 'xy', split_axis=0, conc...  12 us
    all_to_all x1, waiting for transfers between devices, local(): sums = lax.all_to_all(total, ('gz', 'xy'), 0, 0, tiled=True)  10.3 us
    all_to_all x1, starting transfers between devices, local(): sums = lax.all_to_all(total, ('gz', 'xy'), 0, 0, tiled=True)  9.1 us
    pallas_call x1, Pallas kernels, stencil(): pl.pallas_call(stencil_kernel, out_shape=(sds((16, 64, 128), BF16), sds((...  4.48 us
    ppermute x1, starting transfers between devices, local(): qm_d = lax.ppermute(m_d, 'xy', y_odd)  3.98 us
    ppermute x1, waiting for transfers between devices, local(): rc_b = lax.ppermute(c_b, 'gz', z_odd)  3.5 us
    ppermute x1, waiting for transfers between devices, local(): q_d = lax.ppermute(y_d, 'xy', y_odd)  3.42 us
  transfers between devices with their start and end apart: 17, of which 10 were waited for; matrix products, arithmetic and copies ran while one was open for 0% of the time, Pallas kernels for 4%

profile of v4, /device:TPU:1, one launch (start us, length us, event | category | flops | bytes accessed | tf_op | source)
XLA Modules:
  0.0 113.9 jit_solution(13349871850105648365)
XLA Ops:
  0.0 2.9 %pack.1 = bf16[128,64,128]{2,1,0:T(8,128)(2,1)} custom-call(f32[32,8,8,128]{3,2,1,0:T(8,128)} %vel_any.1, s32[32]{0:T(128)} %off.1, f32[32]{0:T(128)} %wt.1, s32[64,128]{1,0:T(8,128)} %bitcast.10), custom_call_target="tpu_custom_call" | custom-call | tf_op jit(solution)/shard_map/pack/pallas_call | solution.py:73
  2.9 12.0 %all-to-all-start = ((bf16[32,256,128]{2,1,0:T(8,128)(2,1)}), bf16[32,256,128]{2,1,0:T(8,128)(2,1)S(1)}, u32[]{:S(2)}, u32[]{:S(2)}) async-start(bf16[32,256,128]{2,1,0:T(8,128)(2,1)} %bitcast.13), calls=%async_computation | async-start | bytes 4194304 | tf_op jit(solution)/shard_map/all_to_all | solution.py:478
  15.0 0.7 prepare.1
  15.7 1.0 collective-permute-start
  16.6 1.2 %collective-permute-start.1 = (f32[4,64,128]{2,1,0:T(8,128)S(1)}, f32[4,64,128]{2,1,0:T(8,128)S(1)}, u32[]{:S(2)}, u32[]{:S(2)}) collective-permute-start(f32[4,64,128]{2,1,0:T(8,128)S(1)} %get-tuple-element.47), channel_id=1, source_target_pairs={{0,224},{32,64},{64,32},{96,128},{128,96},{160,192},{192,160},{224... | collective-permute-start | bytes 393224 | tf_op jit(solution)/shard_map/ppermute | solution.py:482
  17.8 3.5 %collective-permute-done.1.r_b = f32[4,64,128]{2,1,0:T(8,128)S(1)} collective-permute-done((f32[4,64,128]{2,1,0:T(8,128)S(1)}, f32[4,64,128]{2,1,0:T(8,128)S(1)}, u32[]{:S(2)}, u32[]{:S(2)}) %collective-permute-start.1) | collective-permute-done | bytes 131104 | tf_op jit(solution)/shard_map/ppermute | solution.py:482
  21.3 1.6 %collective-permute-start.2 = (f32[12,8,128]{2,1,0:T(8,128)S(1)}, f32[12,8,128]{2,1,0:T(8,128)S(1)}, u32[]{:S(2)}, u32[]{:S(2)}) collective-permute-start(f32[12,8,128]{2,1,0:T(8,128)S(1)} %get-tuple-element.48), channel_id=1, source_target_pairs={{0,1},{1,0},{2,3},{3,2},{4,5},{5,4},{6,7},{7,6},{8,9},{9,8},{10,11... | collective-permute-start | bytes 147464 | tf_op jit(solution)/shard_map/ppermute | solution.py:485
  22.9 4.0 %collective-permute-start.3 = (f32[12,8,128]{2,1,0:T(8,128)S(1)}, f32[12,8,128]{2,1,0:T(8,128)S(1)}, u32[]{:S(2)}, u32[]{:S(2)}) collective-permute-start(f32[12,8,128]{2,1,0:T(8,128)S(1)} %get-tuple-element.49), channel_id=1, source_target_pairs={{0,31},{1,2},{2,1},{3,4},{4,3},{5,6},{6,5},{7,8},{8,7},{9,10},{10,... | collective-permute-start | bytes 147464 | tf_op jit(solution)/shard_map/ppermute | solution.py:486
  26.9 2.4 %lists.1 = (s32[16]{0:T(128)S(1)}, s32[2048]{0:T(1024)S(1)}) custom-call(s32[8,128]{1,0:T(8,128)S(1)} %get-tuple-element.42.code), custom_call_target="tpu_custom_call" | custom-call | tf_op jit(solution)/shard_map/lists/pallas_call | solution.py:160
  29.4 33.9 %collective-permute-done.3.q_d = f32[12,8,128]{2,1,0:T(8,128)S(1)} collective-permute-done((f32[12,8,128]{2,1,0:T(8,128)S(1)}, f32[12,8,128]{2,1,0:T(8,128)S(1)}, u32[]{:S(2)}, u32[]{:S(2)}) %collective-permute-start.3) | collective-permute-done | bytes 49184 | tf_op jit(solution)/shard_map/ppermute | solution.py:486
  63.3 0.2 all-to-all-done
  63.4 1.9 %combine.1 = (f32[16,64,128]{2,1,0:T(8,128)S(1)}, f32[4,64,128]{2,1,0:T(8,128)S(1)}, f32[4,64,128]{2,1,0:T(8,128)S(1)}, f32[2,8,8,128]{3,2,1,0:T(8,128)S(1)}) custom-call(bf16[128,64,128]{2,1,0:T(8,128)(2,1)S(1)} %bitcast.8, s32[16]{0:T(128)S(1)} %get-tuple-element.51.count, s32[2048]{0:T(1024)S(1)} %get-tuple-element.52.entries), custom_call_target="tpu_custom_call" | custom-call | tf_op jit(solution)/shard_map/combine/pallas_call | solution.py:188
  65.3 2.7 %collective-permute-start.4 = (f32[4,64,128]{2,1,0:T(8,128)S(1)}, f32[4,64,128]{2,1,0:T(8,128)S(1)}, u32[]{:S(2)}, u32[]{:S(2)}) collective-permute-start(f32[4,64,128]{2,1,0:T(8,128)S(1)} %get-tuple-element.58), channel_id=1, source_target_pairs={{0,32},{32,0},{64,96},{96,64},{128,160},{160,128},{192,224},{224,1... | collective-permute-start | bytes 393224 | tf_op jit(solution)/shard_map/ppermute | solution.py:492
  68.0 1.3 %collective-permute-start.5 = (f32[4,64,128]{2,1,0:T(8,128)S(1)}, f32[4,64,128]{2,1,0:T(8,128)S(1)}, u32[]{:S(2)}, u32[]{:S(2)}) collective-permute-start(f32[4,64,128]{2,1,0:T(8,128)S(1)} %get-tuple-element.59), channel_id=1, source_target_pairs={{0,224},{32,64},{64,32},{96,128},{128,96},{160,192},{192,160},{224... | collective-permute-start | bytes 393224 | tf_op jit(solution)/shard_map/ppermute | solution.py:491
  69.3 3.4 %collective-permute-done.5.r_b = f32[4,64,128]{2,1,0:T(8,128)S(1)} collective-permute-done((f32[4,64,128]{2,1,0:T(8,128)S(1)}, f32[4,64,128]{2,1,0:T(8,128)S(1)}, u32[]{:S(2)}, u32[]{:S(2)}) %collective-permute-start.5) | collective-permute-done | bytes 131104 | tf_op jit(solution)/shard_map/ppermute | solution.py:491
  72.8 0.8 collective-permute-start.7
  73.7 1.9 %model.1.gm = f32[3,20,80,128]{3,2,1,0:T(8,128)S(1)} custom-call(f32[16,64,128]{2,1,0:T(8,128)S(1)} %copy-done, f32[4,64,128]{2,1,0:T(8,128)S(1)} %collective-permute-done.r_a, f32[4,64,128]{2,1,0:T(8,128)S(1)} %collective-permute-done.1.r_b, f32[12,8,128]{2,1,0:T(8,128)S(1)} %collective-permute-done.2.q_c, f32[12,8,128]{2,1,0:T(8,128)S(1)} %collective-permute-done.3.q_d), custom_call_target="tpu_custom_call" | custom-call | flops 200000000 | bytes 8000000 | tf_op jit(solution)/shard_map/model/pallas_call | solution.py:340
  75.6 0.2 collective-permute-done.6.q_c
  75.8 3.4 %collective-permute-done.7.q_d = f32[12,8,128]{2,1,0:T(8,128)S(1)} collective-permute-done((f32[12,8,128]{2,1,0:T(8,128)S(1)}, f32[12,8,128]{2,1,0:T(8,128)S(1)}, u32[]{:S(2)}, u32[]{:S(2)}) %collective-permute-start.7) | collective-permute-done | bytes 49184 | tf_op jit(solution)/shard_map/ppermute | solution.py:496
  79.2 4.5 %stencil.1 = (bf16[16,64,128]{2,1,0:T(8,128)(2,1)S(1)}, f32[256,128]{1,0:T(8,128)}) custom-call(f32[16,64,128]{2,1,0:T(8,128)S(1)} %get-tuple-element.53.v, f32[4,64,128]{2,1,0:T(8,128)S(1)} %collective-permute-done.4.r_a, f32[4,64,128]{2,1,0:T(8,128)S(1)} %collective-permute-done.5.r_b, f32[12,8,128]{2,1,0:T(8,128)S(1)} %collective-permute-done.6.q_c, ...), custom_call_target="tpu_custom_call" | custom-call | tf_op jit(solution)/shard_map/stencil/pallas_call | solution.py:412
  83.7 2.7 %collective-permute-start.10 = (bf16[16,64,128]{2,1,0:T(8,128)(2,1)S(1)}, bf16[16,64,128]{2,1,0:T(8,128)(2,1)S(1)}, u32[]{:S(2)}, u32[]{:S(2)}) collective-permute-start(bf16[16,64,128]{2,1,0:T(8,128)(2,1)S(1)} %get-tuple-element.65.refs_0_), channel_id=1, source_target_pairs={{0,128},{32,160},{64,192},{96,224},{128,0},{160,32},{192,64},{224,... | collective-permute-start | bytes 786440 | tf_op jit(solution)/shard_map/ppermute | solution.py:501
  86.3 1.0 collective-permute-start.9
  87.3 0.6 collective-permute-start.8
  87.9 9.1 %all-to-all-start.1 = ((f32[256,1,128]{2,1,0:T(1,128)}), f32[256,1,128]{2,1,0:T(1,128)S(1)}, u32[]{:S(2)}, u32[]{:S(2)}) async-start(f32[256,1,128]{2,1,0:T(1,128)} %bitcast.5), calls=%async_computation.1 | async-start | bytes 262144 | tf_op jit(solution)/shard_map/all_to_all | solution.py:503
  97.0 2.2 %collective-permute-start.11 = (bf16[16,64,128]{2,1,0:T(8,128)(2,1)S(1)}, bf16[16,64,128]{2,1,0:T(8,128)(2,1)S(1)}, u32[]{:S(2)}, u32[]{:S(2)}) collective-permute-start(bf16[16,64,128]{2,1,0:T(8,128)(2,1)S(1)} %get-tuple-element.65.refs_0_), channel_id=1, source_target_pairs={{0,32},{32,0},{64,96},{96,64},{128,160},{160,128},{192,224},{224,1... | collective-permute-start | bytes 786440 | tf_op jit(solution)/shard_map/ppermute | solution.py:502
  99.2 10.3 %all-to-all-done.1 = f32[256,1,128]{2,1,0:T(1,128)S(1)} async-done(((f32[256,1,128]{2,1,0:T(1,128)}), f32[256,1,128]{2,1,0:T(1,128)S(1)}, u32[]{:S(2)}, u32[]{:S(2)}) %all-to-all-start.1) | async-done | bytes 131104 | tf_op jit(solution)/shard_map/all_to_all | solution.py:503
  109.6 0.8 collective-permute-start.12
  110.5 0.4 collective-permute-start.14
  110.9 0.6 collective-permute-done.12.refs_5_
  111.6 0.4 collective-permute-done.13.refs_6_
  111.9 0.4 collective-permute-done.14.refs_7_
  112.3 1.5 %scale.1 = bf16[128,64,128]{2,1,0:T(8,128)(2,1)} custom-call(f32[256,128]{1,0:T(8,128)S(1)} %bitcast.9, bf16[16,64,128]{2,1,0:T(8,128)(2,1)S(1)} %get-tuple-element.65.refs_0_, bf16[16,64,128]{2,1,0:T(8,128)(2,1)S(1)} %collective-permute-done.8.refs_1_, bf16[16,64,128]{2,1,0:T(8,128)(2,1)S(1)} %collective-permute-done.9.refs_2_, ...), custom_call_target="tpu_custom_call" | custom-call | tf_op jit(solution)/shard_map/scale/pallas_call | solution.py:449
  (17 shorter events, 0.3 us)
Async XLA Ops:
  2.9 12.1 %copy-start = (f32[16,64,128]{2,1,0:T(8,128)S(1)}, f32[16,64,128]{2,1,0:T(8,128)}, u32[]{:S(2)}) copy-start(f32[16,64,128]{2,1,0:T(8,128)} %cond.1) | copy-start | bytes 1572868
  2.9 12.1 %copy-start.1 = (s32[8192,1]{0,1:T(1,128)S(1)}, s32[8192,1]{0,1:T(1,128)}, u32[]{:S(2)}) copy-start(s32[8192,1]{0,1:T(1,128)} %param.9) | copy-start | bytes 98308
  2.9 12.1 %copy-start.2 = (s32[8192]{0:T(1024)S(1)}, s32[8192]{0:T(1024)}, u32[]{:S(2)}) copy-start(s32[8192]{0:T(1024)} %param.10) | copy-start | bytes 98308
  2.9 60.5 %all-to-all-start = ((bf16[32,256,128]{2,1,0:T(8,128)(2,1)}), bf16[32,256,128]{2,1,0:T(8,128)(2,1)S(1)}, u32[]{:S(2)}, u32[]{:S(2)}) async-start(bf16[32,256,128]{2,1,0:T(8,128)(2,1)} %bitcast.13), calls=%async_computation | async-start | bytes 4194304 | tf_op jit(solution)/shard_map/all_to_all | solution.py:478
  15.7 2.1 %collective-permute-start = (f32[4,64,128]{2,1,0:T(8,128)S(1)}, f32[4,64,128]{2,1,0:T(8,128)S(1)}, u32[]{:S(2)}, u32[]{:S(2)}) collective-permute-start(f32[4,64,128]{2,1,0:T(8,128)S(1)} %get-tuple-element.46), channel_id=1, source_target_pairs={{0,32},{32,0},{64,96},{96,64},{128,160},{160,128},{192,224},{224,1... | collective-permute-start | bytes 393224 | tf_op jit(solution)/shard_map/ppermute | solution.py:483
  16.6 4.7 %collective-permute-start.1 = (f32[4,64,128]{2,1,0:T(8,128)S(1)}, f32[4,64,128]{2,1,0:T(8,128)S(1)}, u32[]{:S(2)}, u32[]{:S(2)}) collective-permute-start(f32[4,64,128]{2,1,0:T(8,128)S(1)} %get-tuple-element.47), channel_id=1, source_target_pairs={{0,224},{32,64},{64,32},{96,128},{128,96},{160,192},{192,160},{224... | collective-permute-start | bytes 393224 | tf_op jit(solution)/shard_map/ppermute | solution.py:482
  21.3 8.0 %collective-permute-start.2 = (f32[12,8,128]{2,1,0:T(8,128)S(1)}, f32[12,8,128]{2,1,0:T(8,128)S(1)}, u32[]{:S(2)}, u32[]{:S(2)}) collective-permute-start(f32[12,8,128]{2,1,0:T(8,128)S(1)} %get-tuple-element.48), channel_id=1, source_target_pairs={{0,1},{1,0},{2,3},{3,2},{4,5},{5,4},{6,7},{7,6},{8,9},{9,8},{10,11... | collective-permute-start | bytes 147464 | tf_op jit(solution)/shard_map/ppermute | solution.py:485
  22.9 40.3 %collective-permute-start.3 = (f32[12,8,128]{2,1,0:T(8,128)S(1)}, f32[12,8,128]{2,1,0:T(8,128)S(1)}, u32[]{:S(2)}, u32[]{:S(2)}) collective-permute-start(f32[12,8,128]{2,1,0:T(8,128)S(1)} %get-tuple-element.49), channel_id=1, source_target_pairs={{0,31},{1,2},{2,1},{3,4},{4,3},{5,6},{6,5},{7,8},{8,7},{9,10},{10,... | collective-permute-start | bytes 147464 | tf_op jit(solution)/shard_map/ppermute | solution.py:486
  65.3 4.0 %collective-permute-start.4 = (f32[4,64,128]{2,1,0:T(8,128)S(1)}, f32[4,64,128]{2,1,0:T(8,128)S(1)}, u32[]{:S(2)}, u32[]{:S(2)}) collective-permute-start(f32[4,64,128]{2,1,0:T(8,128)S(1)} %get-tuple-element.58), channel_id=1, source_target_pairs={{0,32},{32,0},{64,96},{96,64},{128,160},{160,128},{192,224},{224,1... | collective-permute-start | bytes 393224 | tf_op jit(solution)/shard_map/ppermute | solution.py:492
  68.0 4.7 %collective-permute-start.5 = (f32[4,64,128]{2,1,0:T(8,128)S(1)}, f32[4,64,128]{2,1,0:T(8,128)S(1)}, u32[]{:S(2)}, u32[]{:S(2)}) collective-permute-start(f32[4,64,128]{2,1,0:T(8,128)S(1)} %get-tuple-element.59), channel_id=1, source_target_pairs={{0,224},{32,64},{64,32},{96,128},{128,96},{160,192},{192,160},{224... | collective-permute-start | bytes 393224 | tf_op jit(solution)/shard_map/ppermute | solution.py:491
  72.7 3.0 %collective-permute-start.6 = (f32[12,8,128]{2,1,0:T(8,128)S(1)}, f32[12,8,128]{2,1,0:T(8,128)S(1)}, u32[]{:S(2)}, u32[]{:S(2)}) collective-permute-start(f32[12,8,128]{2,1,0:T(8,128)S(1)} %get-tuple-element.61), channel_id=1, source_target_pairs={{0,1},{1,0},{2,3},{3,2},{4,5},{5,4},{6,7},{7,6},{8,9},{9,8},{10,11... | collective-permute-start | bytes 147464 | tf_op jit(solution)/shard_map/ppermute | solution.py:495
  72.8 6.3 %collective-permute-start.7 = (f32[12,8,128]{2,1,0:T(8,128)S(1)}, f32[12,8,128]{2,1,0:T(8,128)S(1)}, u32[]{:S(2)}, u32[]{:S(2)}) collective-permute-start(f32[12,8,128]{2,1,0:T(8,128)S(1)} %get-tuple-element.62), channel_id=1, source_target_pairs={{0,31},{1,2},{2,1},{3,4},{4,3},{5,6},{6,5},{7,8},{8,7},{9,10},{10,... | collective-permute-start | bytes 147464 | tf_op jit(solution)/shard_map/ppermute | solution.py:496
  83.7 25.9 %collective-permute-start.10 = (bf16[16,64,128]{2,1,0:T(8,128)(2,1)S(1)}, bf16[16,64,128]{2,1,0:T(8,128)(2,1)S(1)}, u32[]{:S(2)}, u32[]{:S(2)}) collective-permute-start(bf16[16,64,128]{2,1,0:T(8,128)(2,1)S(1)} %get-tuple-element.65.refs_0_), channel_id=1, source_target_pairs={{0,128},{32,160},{64,192},{96,224},{128,0},{160,32},{192,64},{224,... | collective-permute-start | bytes 786440 | tf_op jit(solution)/shard_map/ppermute | solution.py:501
  86.3 23.3 %collective-permute-start.9 = (bf16[16,64,128]{2,1,0:T(8,128)(2,1)S(1)}, bf16[16,64,128]{2,1,0:T(8,128)(2,1)S(1)}, u32[]{:S(2)}, u32[]{:S(2)}) collective-permute-start(bf16[16,64,128]{2,1,0:T(8,128)(2,1)S(1)} %get-tuple-element.65.refs_0_), channel_id=1, source_target_pairs={{0,192},{32,224},{64,0},{96,32},{128,64},{160,96},{192,128},{224,1... | collective-permute-start | bytes 786440 | tf_op jit(solution)/shard_map/ppermute | solution.py:500
  87.3 22.3 %collective-permute-start.8 = (bf16[16,64,128]{2,1,0:T(8,128)(2,1)S(1)}, bf16[16,64,128]{2,1,0:T(8,128)(2,1)S(1)}, u32[]{:S(2)}, u32[]{:S(2)}) collective-permute-start(bf16[16,64,128]{2,1,0:T(8,128)(2,1)S(1)} %get-tuple-element.65.refs_0_), channel_id=1, source_target_pairs={{0,64},{32,96},{64,128},{96,160},{128,192},{160,224},{192,0},{224,... | collective-permute-start | bytes 786440 | tf_op jit(solution)/shard_map/ppermute | solution.py:499
  87.9 21.7 %all-to-all-start.1 = ((f32[256,1,128]{2,1,0:T(1,128)}), f32[256,1,128]{2,1,0:T(1,128)S(1)}, u32[]{:S(2)}, u32[]{:S(2)}) async-start(f32[256,1,128]{2,1,0:T(1,128)} %bitcast.5), calls=%async_computation.1 | async-start | bytes 262144 | tf_op jit(solution)/shard_map/all_to_all | solution.py:503
  97.0 13.9 %collective-permute-start.11 = (bf16[16,64,128]{2,1,0:T(8,128)(2,1)S(1)}, bf16[16,64,128]{2,1,0:T(8,128)(2,1)S(1)}, u32[]{:S(2)}, u32[]{:S(2)}) collective-permute-start(bf16[16,64,128]{2,1,0:T(8,128)(2,1)S(1)} %get-tuple-element.65.refs_0_), channel_id=1, source_target_pairs={{0,32},{32,0},{64,96},{96,64},{128,160},{160,128},{192,224},{224,1... | collective-permute-start | bytes 786440 | tf_op jit(solution)/shard_map/ppermute | solution.py:502
  109.6 2.0 %collective-permute-start.12 = (bf16[16,64,128]{2,1,0:T(8,128)(2,1)S(1)}, bf16[16,64,128]{2,1,0:T(8,128)(2,1)S(1)}, u32[]{:S(2)}, u32[]{:S(2)}) collective-permute-start(bf16[16,64,128]{2,1,0:T(8,128)(2,1)S(1)} %collective-permute-done.8.refs_1_), channel_id=1, source_target_pairs={{0,32},{32,0},{64,96},{96,64},{128,160},{160,128},{192,224},{224,1... | collective-permute-start | bytes 786440 | tf_op jit(solution)/shard_map/ppermute | solution.py:505
  110.4 1.5 %collective-permute-start.13 = (bf16[16,64,128]{2,1,0:T(8,128)(2,1)S(1)}, bf16[16,64,128]{2,1,0:T(8,128)(2,1)S(1)}, u32[]{:S(2)}, u32[]{:S(2)}) collective-permute-start(bf16[16,64,128]{2,1,0:T(8,128)(2,1)S(1)} %collective-permute-done.9.refs_2_), channel_id=1, source_target_pairs={{0,32},{32,0},{64,96},{96,64},{128,160},{160,128},{192,224},{224,1... | collective-permute-start | bytes 786440 | tf_op jit(solution)/shard_map/ppermute | solution.py:505
  110.5 1.8 %collective-permute-start.14 = (bf16[16,64,128]{2,1,0:T(8,128)(2,1)S(1)}, bf16[16,64,128]{2,1,0:T(8,128)(2,1)S(1)}, u32[]{:S(2)}, u32[]{:S(2)}) collective-permute-start(bf16[16,64,128]{2,1,0:T(8,128)(2,1)S(1)} %collective-permute-done.10.refs_3_), channel_id=1, source_target_pairs={{0,32},{32,0},{64,96},{96,64},{128,160},{160,128},{192,224},{224,1... | collective-permute-start | bytes 786440 | tf_op jit(solution)/shard_map/ppermute | solution.py:505

commit v5 on v4

--- a/solution.py
+++ b/solution.py
@@ -167,7 +167,7 @@
     )(code)
 
 
-def combine_kernel(recv, count, entries, v, z_a, z_b, y_own):
+def combine_kernel(recv, count, entries, v, z_a, z_b, y_c, y_d):
     g = lax.axis_index("gz")
     d = lax.axis_index("xy")
     for j in range(16):
@@ -181,7 +181,7 @@
     z_hi, z_lo = edge_starts(g)
     z_a[...] = v[pl.ds(z_hi, 4)]
     z_b[...] = v[pl.ds(z_lo, 4)]
-    y_own[0], y_own[1] = edge_pairs(v, d % 2 == 0)
+    y_c[...], y_d[...] = edge_pairs(v, d % 2 == 0)
 
 
 def combine(recv, count, entries):
@@ -191,10 +191,11 @@
             sds((16, 64, 128), F32),
             sds((4, 64, 128), F32),
             sds((4, 64, 128), F32),
-            sds((2, 8, 8, 128), F32),
+            sds((8, 8, 128), F32),
+            sds((8, 8, 128), F32),
         ),
         in_specs=[vspec(), sspec(), sspec()],
-        out_specs=(vspec(),) * 4,
+        out_specs=(vspec(),) * 5,
         compiler_params=params(),
         name="combine",
     )(recv, count, entries)
@@ -218,6 +219,24 @@
         compiler_params=params(),
         name="strips",
     )(y_own, r_a, r_b)
+
+
+def corners_kernel(r_a, r_b, k_c, k_d):
+    d = lax.axis_index("xy")
+    y_even = d % 2 == 0
+    for at, field in ((0, r_a), (2, r_b)):
+        k_c[at : at + 2], k_d[at : at + 2] = edge_pairs(field, y_even)
+
+
+def corners(r_a, r_b):
+    return pl.pallas_call(
+        corners_kernel,
+        out_shape=(sds((4, 8, 128), F32),) * 2,
+        in_specs=[vspec()] * 2,
+        out_specs=(vspec(),) * 2,
+        compiler_params=params(),
+        name="corners",
+    )(r_a, r_b)
 
 
 def split3(x):
@@ -255,7 +274,7 @@
     return jnp.dot(a, b, preferred_element_type=F32)
 
 
-def fill(ext, field, r_a, r_b, q_c, q_d):
+def fill(ext, field, r_a, r_b, q_c, q_d, k_c=None, k_d=None):
     g = lax.axis_index("gz")
     d = lax.axis_index("xy")
     even = g % 2 == 0
@@ -273,8 +292,10 @@
     ext[pl.ds(at_a, 4), 8:72, :] = r_a[...] * keep_a
     ext[pl.ds(at_b, 4), 8:72, :] = r_b[...] * keep_b
     for z in range(24):
-        c = q_c[z // 2]
-        e = q_d[z // 2]
+        if k_c is None or z < 16:
+            c, e = q_c[z // 2], q_d[z // 2]
+        else:
+            c, e = k_c[z // 2 - 8], k_d[z // 2 - 8]
         lo = jnp.where(y_even, e, c)[4 * (z % 2) : 4 * (z % 2) + 4] * left_in
         hi = jnp.where(y_even, c, e)[4 * (z % 2) : 4 * (z % 2) + 4] * right_in
         if z < 16:
@@ -292,14 +313,14 @@
     twice = jnp.concatenate([weights, weights], axis=0)
 
     def along_x(i, carry):
-        part = pl.ds(i * 12, 12)
-        h, m, l = split3(ext[part].reshape(12 * 80, 128))
+        part = pl.ds(i * 6, 6)
+        h, m, l = split3(ext[part].reshape(6 * 80, 128))
         both = dot(jnp.concatenate([h, m], axis=1), twice) + dot(l, weights)
-        sx[part] = both[:, 0:128].reshape(12, 80, 128)
-        dx[part] = both[:, 128:256].reshape(12, 80, 128)
+        sx[part] = both[:, 0:128].reshape(6, 80, 128)
+        dx[part] = both[:, 128:256].reshape(6, 80, 128)
         return carry
 
-    lax.fori_loop(0, 2, along_x, 0)
+    lax.fori_loop(0, 4, along_x, 0, unroll=4)
 
     def along_y(z, carry):
         ss = [sx[z, 2 + i : 74 + i, :] for i in range(5)]
@@ -310,7 +331,7 @@
         ext[z, 4:76, :] = yy
         return carry
 
-    lax.fori_loop(0, 24, along_y, 0, unroll=2)
+    lax.fori_loop(0, 24, along_y, 0, unroll=4)
 
 
 def grad_tile(ext, sx, dx, z, tile):
@@ -349,12 +370,12 @@
     )(cond, r_a, r_b, q_c, q_d)
 
 
-def stencil_kernel(v, r_a, r_b, q_c, q_d, gm, out, total, ext, sx, dx, back):
+def stencil_kernel(v, r_a, r_b, q_c, q_d, k_c, k_d, gm, out, total, ext, sx, dx, back):
     g = lax.axis_index("gz")
     d = lax.axis_index("xy")
     low_in = (g > 0).astype(F32)
     high_in = (g < 7).astype(F32)
-    fill(ext, v, r_a, r_b, q_c, q_d)
+    fill(ext, v, r_a, r_b, q_c, q_d, k_c, k_d)
     mix_xy(ext, sx, dx)
     row = lax.broadcasted_iota(jnp.int32, (8, 128), 0)
 
@@ -389,30 +410,24 @@
     w_s = band(S_TAPS)
     w_d = band(D_TAPS)
     w = jnp.concatenate([w_d, w_s], axis=0)
-    total[0:8, :] = jnp.zeros((8, 128), F32)
 
     w = jnp.concatenate([w, w, w], axis=0)
 
-    def back_xy(i, carry):
-        part = pl.ds(i * 8, 8)
-        p, q, r = [[back[j, part, 6 + k : 70 + k, :] for k in range(5)] for j in range(3)]
-        us = split3(smooth5(p).reshape(512, 128))
-        ts = split3((deriv5(q) + smooth5(r)).reshape(512, 128))
-        both = [x for pair in zip(us, ts) for x in pair]
-        acc = dot(jnp.concatenate(both, axis=1), w) * NORM
-        out[part] = acc.reshape(8, 64, 128).astype(BF16)
-        total[0:8, :] += jnp.sum((acc * acc).reshape(64, 8, 128), axis=0)
-        return carry
-
-    lax.fori_loop(0, 2, back_xy, 0, unroll=2)
-    total[...] = jnp.broadcast_to(jnp.sum(total[0:8, :], axis=0, keepdims=True), (256, 128))
-
-
-def stencil(v, r_a, r_b, q_c, q_d, gm):
+    p, q, r = [[back[j, :, 6 + k : 70 + k, :] for k in range(5)] for j in range(3)]
+    us = split3(smooth5(p).reshape(1024, 128))
+    ts = split3((deriv5(q) + smooth5(r)).reshape(1024, 128))
+    both = [x for pair in zip(us, ts) for x in pair]
+    acc = dot(jnp.concatenate(both, axis=1), w) * NORM
+    out[...] = acc.reshape(16, 64, 128).astype(BF16)
+    squares = jnp.sum((acc * acc).reshape(128, 8, 128), axis=0)
+    total[...] = jnp.broadcast_to(jnp.sum(squares, axis=0, keepdims=True), (256, 128))
+
+
+def stencil(v, r_a, r_b, q_c, q_d, k_c, k_d, gm):
     return pl.pallas_call(
         stencil_kernel,
         out_shape=(sds((16, 64, 128), BF16), sds((256, 128), F32)),
-        in_specs=[vspec()] * 6,
+        in_specs=[vspec()] * 8,
         out_specs=(vspec(),) * 2,
         scratch_shapes=[
             pltpu.VMEM((24, 80, 128), F32),
@@ -422,7 +437,7 @@
         ],
         compiler_params=params(),
         name="stencil",
-    )(v, r_a, r_b, q_c, q_d, gm)
+    )(v, r_a, r_b, q_c, q_d, k_c, k_d, gm)
 
 
 def scale_kernel(cells, sums, *refs):
@@ -486,15 +501,17 @@
     qm_d = lax.ppermute(m_d, "xy", y_odd)
     count, entries = lists(code)
     recv, count, entries, qm_c, qm_d = lax.optimization_barrier((recv, count, entries, qm_c, qm_d))
-    v, z_a, z_b, y_own = combine(recv.reshape(n_x * CAP, 64, 128), count, entries)
-    z_a, z_b, qm_c, qm_d = lax.optimization_barrier((z_a, z_b, qm_c, qm_d))
+    v, z_a, z_b, y_c, y_d = combine(recv.reshape(n_x * CAP, 64, 128), count, entries)
+    z_a, z_b, y_c, y_d, qm_c, qm_d = lax.optimization_barrier((z_a, z_b, y_c, y_d, qm_c, qm_d))
     r_b = lax.ppermute(z_b, "gz", z_odd)
     r_a = lax.ppermute(z_a, "gz", z_even)
-    gm = model(conductivity, rc_a, rc_b, qm_c, qm_d)
-    y_c, y_d = strips(y_own, r_a, r_b)
     q_c = lax.ppermute(y_c, "xy", y_even)
     q_d = lax.ppermute(y_d, "xy", y_odd)
-    grad, total = stencil(v, r_a, r_b, q_c, q_d, gm)
+    gm = model(conductivity, rc_a, rc_b, qm_c, qm_d)
+    k_c, k_d = corners(r_a, r_b)
+    k_c = lax.ppermute(k_c, "xy", y_even)
+    k_d = lax.ppermute(k_d, "xy", y_odd)
+    grad, total = stencil(v, r_a, r_b, q_c, q_d, k_c, k_d, gm)
     core = swap_even(n_g)
     before = lax.ppermute(grad, "gz", [(i, (i + 2) % n_g) for i in range(n_g)])
     after = lax.ppermute(grad, "gz", [(i, (i - 2) % n_g) for i in range(n_g)])

time: 114 us -> 114 us (level)
  starting transfers between devices: 41.5 us -> 43.7 us
  waiting for transfers between devices: 56.3 us -> 54.7 us
    ppermute x1, waiting for transfers between devices: 3.42 us -> 0.01 us  [local(): q_d = lax.ppermute(y_d, 'xy', y_odd)]
    ppermute x0 -> x2, waiting for transfers between devices: none -> 2.74 us  [the longest x1 2.74 us: local(): k_d = lax.ppermute(k_d, 'xy', y_odd)]
    ppermute x0 -> x2, starting transfers between devices: none -> 1.58 us  [the longest x1 1.48 us: local(): k_d = lax.ppermute(k_d, 'xy', y_odd)]
  transfers between devices with their start and end apart: 17 -> 19, of which waited for: 10 -> 9; matrix products, arithmetic and copies ran while one was open for 0% -> 0% of each run, Pallas kernels for 4% -> 4%
where the time goes in v5:
time: 114 us
  waiting for transfers between devices  54.7 us (48%)
  starting transfers between devices  43.7 us (38%)
  Pallas kernels  15.3 us (13%)
    ppermute x1, waiting for transfers between devices, local(): qm_d = lax.ppermute(m_d, 'xy', y_odd)  33.9 us
    all_to_all x1, starting transfers between devices, local(): lax.all_to_all(send.reshape(n_x, CAP * 64, 128), 'xy', split_axis=0, conc...  12 us
    all_to_all x1, waiting for transfers between devices, local(): sums = lax.all_to_all(total, ('gz', 'xy'), 0, 0, tiled=True)  10.3 us
    all_to_all x1, starting transfers between devices, local(): sums = lax.all_to_all(total, ('gz', 'xy'), 0, 0, tiled=True)  9.89 us
    pallas_call x1, Pallas kernels, stencil(): pl.pallas_call(stencil_kernel, out_shape=(sds((16, 64, 128), BF16), sds((...  4.12 us
    ppermute x1, starting transfers between devices, local(): qm_d = lax.ppermute(m_d, 'xy', y_odd)  3.98 us
    ppermute x1, waiting for transfers between devices, local(): rc_b = lax.ppermute(c_b, 'gz', z_odd)  3.5 us
    pallas_call x1, Pallas kernels, pack(): pl.pallas_call(pack_kernel, out_shape=sds((32 * CAP, 64, 128), BF16), in_...  2.87 us
  transfers between devices with their start and end apart: 19, of which 9 were waited for; matrix products, arithmetic and copies ran while one was open for 0% of the time, Pallas kernels for 4%

profile of v5, /device:TPU:1, one launch (start us, length us, event | category | flops | bytes accessed | tf_op | source)
XLA Modules:
  0.0 114.1 jit_solution(13883998761367711082)
XLA Ops:
  0.0 2.9 %pack.1 = bf16[128,64,128]{2,1,0:T(8,128)(2,1)} custom-call(f32[32,8,8,128]{3,2,1,0:T(8,128)} %vel_any.1, s32[32]{0:T(128)} %off.1, f32[32]{0:T(128)} %wt.1, s32[64,128]{1,0:T(8,128)} %bitcast.10), custom_call_target="tpu_custom_call" | custom-call | tf_op jit(solution)/shard_map/pack/pallas_call | solution.py:73
  2.9 12.0 %all-to-all-start = ((bf16[32,256,128]{2,1,0:T(8,128)(2,1)}), bf16[32,256,128]{2,1,0:T(8,128)(2,1)S(1)}, u32[]{:S(2)}, u32[]{:S(2)}) async-start(bf16[32,256,128]{2,1,0:T(8,128)(2,1)} %bitcast.13), calls=%async_computation | async-start | bytes 4194304 | tf_op jit(solution)/shard_map/all_to_all | solution.py:493
  15.0 0.7 prepare.1
  15.7 1.0 collective-permute-start
  16.6 1.2 %collective-permute-start.1 = (f32[4,64,128]{2,1,0:T(8,128)S(1)}, f32[4,64,128]{2,1,0:T(8,128)S(1)}, u32[]{:S(2)}, u32[]{:S(2)}) collective-permute-start(f32[4,64,128]{2,1,0:T(8,128)S(1)} %get-tuple-element.50), channel_id=1, source_target_pairs={{0,224},{32,64},{64,32},{96,128},{128,96},{160,192},{192,160},{224... | collective-permute-start | bytes 393224 | tf_op jit(solution)/shard_map/ppermute | solution.py:497
  17.8 3.5 %collective-permute-done.1.r_b = f32[4,64,128]{2,1,0:T(8,128)S(1)} collective-permute-done((f32[4,64,128]{2,1,0:T(8,128)S(1)}, f32[4,64,128]{2,1,0:T(8,128)S(1)}, u32[]{:S(2)}, u32[]{:S(2)}) %collective-permute-start.1) | collective-permute-done | bytes 131104 | tf_op jit(solution)/shard_map/ppermute | solution.py:497
  21.3 1.6 %collective-permute-start.2 = (f32[12,8,128]{2,1,0:T(8,128)S(1)}, f32[12,8,128]{2,1,0:T(8,128)S(1)}, u32[]{:S(2)}, u32[]{:S(2)}) collective-permute-start(f32[12,8,128]{2,1,0:T(8,128)S(1)} %get-tuple-element.51), channel_id=1, source_target_pairs={{0,1},{1,0},{2,3},{3,2},{4,5},{5,4},{6,7},{7,6},{8,9},{9,8},{10,11... | collective-permute-start | bytes 147464 | tf_op jit(solution)/shard_map/ppermute | solution.py:500
  22.9 4.0 %collective-permute-start.3 = (f32[12,8,128]{2,1,0:T(8,128)S(1)}, f32[12,8,128]{2,1,0:T(8,128)S(1)}, u32[]{:S(2)}, u32[]{:S(2)}) collective-permute-start(f32[12,8,128]{2,1,0:T(8,128)S(1)} %get-tuple-element.52), channel_id=1, source_target_pairs={{0,31},{1,2},{2,1},{3,4},{4,3},{5,6},{6,5},{7,8},{8,7},{9,10},{10,... | collective-permute-start | bytes 147464 | tf_op jit(solution)/shard_map/ppermute | solution.py:501
  26.9 2.4 %lists.1 = (s32[16]{0:T(128)S(1)}, s32[2048]{0:T(1024)S(1)}) custom-call(s32[8,128]{1,0:T(8,128)S(1)} %get-tuple-element.45.code), custom_call_target="tpu_custom_call" | custom-call | tf_op jit(solution)/shard_map/lists/pallas_call | solution.py:160
  29.4 33.9 %collective-permute-done.3.q_d = f32[12,8,128]{2,1,0:T(8,128)S(1)} collective-permute-done((f32[12,8,128]{2,1,0:T(8,128)S(1)}, f32[12,8,128]{2,1,0:T(8,128)S(1)}, u32[]{:S(2)}, u32[]{:S(2)}) %collective-permute-start.3) | collective-permute-done | bytes 49184 | tf_op jit(solution)/shard_map/ppermute | solution.py:501
  63.3 0.2 all-to-all-done
  63.4 1.9 %combine.1 = (f32[16,64,128]{2,1,0:T(8,128)S(1)}, f32[4,64,128]{2,1,0:T(8,128)S(1)}, f32[4,64,128]{2,1,0:T(8,128)S(1)}, f32[8,8,128]{2,1,0:T(8,128)S(1)}, f32[8,8,128]{2,1,0:T(8,128)S(1)}) custom-call(bf16[128,64,128]{2,1,0:T(8,128)(2,1)S(1)} %bitcast.8, s32[16]{0:T(128)S(1)} %get-tuple-element.54.count, s32[2048]{0:T(1024)S(1)} %get-tuple-element.55.entries), custom_call_target="tpu_custom_call" | custom-call | tf_op jit(solution)/shard_map/combine/pallas_call | solution.py:188
  65.3 2.7 %collective-permute-start.4 = (f32[4,64,128]{2,1,0:T(8,128)S(1)}, f32[4,64,128]{2,1,0:T(8,128)S(1)}, u32[]{:S(2)}, u32[]{:S(2)}) collective-permute-start(f32[4,64,128]{2,1,0:T(8,128)S(1)} %get-tuple-element.63), channel_id=1, source_target_pairs={{0,32},{32,0},{64,96},{96,64},{128,160},{160,128},{192,224},{224,1... | collective-permute-start | bytes 393224 | tf_op jit(solution)/shard_map/ppermute | solution.py:507
  68.0 1.3 %collective-permute-start.5 = (f32[4,64,128]{2,1,0:T(8,128)S(1)}, f32[4,64,128]{2,1,0:T(8,128)S(1)}, u32[]{:S(2)}, u32[]{:S(2)}) collective-permute-start(f32[4,64,128]{2,1,0:T(8,128)S(1)} %get-tuple-element.64), channel_id=1, source_target_pairs={{0,224},{32,64},{64,32},{96,128},{128,96},{160,192},{192,160},{224... | collective-permute-start | bytes 393224 | tf_op jit(solution)/shard_map/ppermute | solution.py:506
  69.3 0.7 collective-permute-start.7
  70.0 2.7 %collective-permute-done.5.r_b = f32[4,64,128]{2,1,0:T(8,128)S(1)} collective-permute-done((f32[4,64,128]{2,1,0:T(8,128)S(1)}, f32[4,64,128]{2,1,0:T(8,128)S(1)}, u32[]{:S(2)}, u32[]{:S(2)}) %collective-permute-start.5) | collective-permute-done | bytes 131104 | tf_op jit(solution)/shard_map/ppermute | solution.py:506
  72.8 1.5 %collective-permute-start.9 = (f32[4,8,128]{2,1,0:T(8,128)S(1)}, f32[4,8,128]{2,1,0:T(8,128)S(1)}, u32[]{:S(2)}, u32[]{:S(2)}) collective-permute-start(f32[4,8,128]{2,1,0:T(8,128)S(1)} %get-tuple-element.68), channel_id=1, source_target_pairs={{0,31},{1,2},{2,1},{3,4},{4,3},{5,6},{6,5},{7,8},{8,7},{9,10},{10,... | collective-permute-start | bytes 49160 | tf_op jit(solution)/shard_map/ppermute | solution.py:513
  74.3 1.7 %model.1.gm = f32[3,20,80,128]{3,2,1,0:T(8,128)S(1)} custom-call(f32[16,64,128]{2,1,0:T(8,128)S(1)} %copy-done, f32[4,64,128]{2,1,0:T(8,128)S(1)} %collective-permute-done.r_a, f32[4,64,128]{2,1,0:T(8,128)S(1)} %collective-permute-done.1.r_b, f32[12,8,128]{2,1,0:T(8,128)S(1)} %collective-permute-done.2.q_c, f32[12,8,128]{2,1,0:T(8,128)S(1)} %collective-permute-done.3.q_d), custom_call_target="tpu_custom_call" | custom-call | flops 200000000 | bytes 8000000 | tf_op jit(solution)/shard_map/model/pallas_call | solution.py:361
  76.1 2.7 %collective-permute-done.9.k_d = f32[4,8,128]{2,1,0:T(8,128)S(1)} collective-permute-done((f32[4,8,128]{2,1,0:T(8,128)S(1)}, f32[4,8,128]{2,1,0:T(8,128)S(1)}, u32[]{:S(2)}, u32[]{:S(2)}) %collective-permute-start.9) | collective-permute-done | bytes 16416 | tf_op jit(solution)/shard_map/ppermute | solution.py:513
  78.8 4.1 %stencil.1 = (bf16[16,64,128]{2,1,0:T(8,128)(2,1)S(1)}, f32[256,128]{1,0:T(8,128)}) custom-call(f32[16,64,128]{2,1,0:T(8,128)S(1)} %get-tuple-element.56.v, f32[4,64,128]{2,1,0:T(8,128)S(1)} %collective-permute-done.4.r_a, f32[4,64,128]{2,1,0:T(8,128)S(1)} %collective-permute-done.5.r_b, f32[8,8,128]{2,1,0:T(8,128)S(1)} %collective-permute-done.6.q_c, ...), custom_call_target="tpu_custom_call" | custom-call | tf_op jit(solution)/shard_map/stencil/pallas_call | solution.py:427
  82.9 2.6 %collective-permute-start.12 = (bf16[16,64,128]{2,1,0:T(8,128)(2,1)S(1)}, bf16[16,64,128]{2,1,0:T(8,128)(2,1)S(1)}, u32[]{:S(2)}, u32[]{:S(2)}) collective-permute-start(bf16[16,64,128]{2,1,0:T(8,128)(2,1)S(1)} %get-tuple-element.71.refs_0_), channel_id=1, source_target_pairs={{0,128},{32,160},{64,192},{96,224},{128,0},{160,32},{192,64},{224,... | collective-permute-start | bytes 786440 | tf_op jit(solution)/shard_map/ppermute | solution.py:518
  85.6 1.0 collective-permute-start.11
  86.6 0.6 collective-permute-start.10
  87.2 9.9 %all-to-all-start.1 = ((f32[256,1,128]{2,1,0:T(1,128)}), f32[256,1,128]{2,1,0:T(1,128)S(1)}, u32[]{:S(2)}, u32[]{:S(2)}) async-start(f32[256,1,128]{2,1,0:T(1,128)} %bitcast.5), calls=%async_computation.1 | async-start | bytes 262144 | tf_op jit(solution)/shard_map/all_to_all | solution.py:520
  97.1 2.2 %collective-permute-start.13 = (bf16[16,64,128]{2,1,0:T(8,128)(2,1)S(1)}, bf16[16,64,128]{2,1,0:T(8,128)(2,1)S(1)}, u32[]{:S(2)}, u32[]{:S(2)}) collective-permute-start(bf16[16,64,128]{2,1,0:T(8,128)(2,1)S(1)} %get-tuple-element.71.refs_0_), channel_id=1, source_target_pairs={{0,32},{32,0},{64,96},{96,64},{128,160},{160,128},{192,224},{224,1... | collective-permute-start | bytes 786440 | tf_op jit(solution)/shard_map/ppermute | solution.py:519
  99.3 10.3 %all-to-all-done.1 = f32[256,1,128]{2,1,0:T(1,128)S(1)} async-done(((f32[256,1,128]{2,1,0:T(1,128)}), f32[256,1,128]{2,1,0:T(1,128)S(1)}, u32[]{:S(2)}, u32[]{:S(2)}) %all-to-all-start.1) | async-done | bytes 131104 | tf_op jit(solution)/shard_map/all_to_all | solution.py:520
  109.7 0.8 collective-permute-start.14
  110.6 0.4 collective-permute-start.16
  111.0 0.6 collective-permute-done.14.refs_5_
  111.7 0.4 collective-permute-done.15.refs_6_
  112.0 0.4 collective-permute-done.16.refs_7_
  112.4 1.5 %scale.1 = bf16[128,64,128]{2,1,0:T(8,128)(2,1)} custom-call(f32[256,128]{1,0:T(8,128)S(1)} %bitcast.9, bf16[16,64,128]{2,1,0:T(8,128)(2,1)S(1)} %get-tuple-element.71.refs_0_, bf16[16,64,128]{2,1,0:T(8,128)(2,1)S(1)} %collective-permute-done.10.refs_1_, bf16[16,64,128]{2,1,0:T(8,128)(2,1)S(1)} %collective-permute-done.11.refs_2_, ...), custom_call_target="tpu_custom_call" | custom-call | tf_op jit(solution)/shard_map/scale/pallas_call | solution.py:464
  (21 shorter events, 0.3 us)
Async XLA Ops:
  2.9 12.1 %copy-start = (f32[16,64,128]{2,1,0:T(8,128)S(1)}, f32[16,64,128]{2,1,0:T(8,128)}, u32[]{:S(2)}) copy-start(f32[16,64,128]{2,1,0:T(8,128)} %cond.1) | copy-start | bytes 1572868
  2.9 12.1 %copy-start.1 = (s32[8192,1]{0,1:T(1,128)S(1)}, s32[8192,1]{0,1:T(1,128)}, u32[]{:S(2)}) copy-start(s32[8192,1]{0,1:T(1,128)} %param.9) | copy-start | bytes 98308
  2.9 12.1 %copy-start.2 = (s32[8192]{0:T(1024)S(1)}, s32[8192]{0:T(1024)}, u32[]{:S(2)}) copy-start(s32[8192]{0:T(1024)} %param.10) | copy-start | bytes 98308
  2.9 60.5 %all-to-all-start = ((bf16[32,256,128]{2,1,0:T(8,128)(2,1)}), bf16[32,256,128]{2,1,0:T(8,128)(2,1)S(1)}, u32[]{:S(2)}, u32[]{:S(2)}) async-start(bf16[32,256,128]{2,1,0:T(8,128)(2,1)} %bitcast.13), calls=%async_computation | async-start | bytes 4194304 | tf_op jit(solution)/shard_map/all_to_all | solution.py:493
  15.7 2.1 %collective-permute-start = (f32[4,64,128]{2,1,0:T(8,128)S(1)}, f32[4,64,128]{2,1,0:T(8,128)S(1)}, u32[]{:S(2)}, u32[]{:S(2)}) collective-permute-start(f32[4,64,128]{2,1,0:T(8,128)S(1)} %get-tuple-element.49), channel_id=1, source_target_pairs={{0,32},{32,0},{64,96},{96,64},{128,160},{160,128},{192,224},{224,1... | collective-permute-start | bytes 393224 | tf_op jit(solution)/shard_map/ppermute | solution.py:498
  16.6 4.7 %collective-permute-start.1 = (f32[4,64,128]{2,1,0:T(8,128)S(1)}, f32[4,64,128]{2,1,0:T(8,128)S(1)}, u32[]{:S(2)}, u32[]{:S(2)}) collective-permute-start(f32[4,64,128]{2,1,0:T(8,128)S(1)} %get-tuple-element.50), channel_id=1, source_target_pairs={{0,224},{32,64},{64,32},{96,128},{128,96},{160,192},{192,160},{224... | collective-permute-start | bytes 393224 | tf_op jit(solution)/shard_map/ppermute | solution.py:497
  21.3 8.0 %collective-permute-start.2 = (f32[12,8,128]{2,1,0:T(8,128)S(1)}, f32[12,8,128]{2,1,0:T(8,128)S(1)}, u32[]{:S(2)}, u32[]{:S(2)}) collective-permute-start(f32[12,8,128]{2,1,0:T(8,128)S(1)} %get-tuple-element.51), channel_id=1, source_target_pairs={{0,1},{1,0},{2,3},{3,2},{4,5},{5,4},{6,7},{7,6},{8,9},{9,8},{10,11... | collective-permute-start | bytes 147464 | tf_op jit(solution)/shard_map/ppermute | solution.py:500
  22.9 40.3 %collective-permute-start.3 = (f32[12,8,128]{2,1,0:T(8,128)S(1)}, f32[12,8,128]{2,1,0:T(8,128)S(1)}, u32[]{:S(2)}, u32[]{:S(2)}) collective-permute-start(f32[12,8,128]{2,1,0:T(8,128)S(1)} %get-tuple-element.52), channel_id=1, source_target_pairs={{0,31},{1,2},{2,1},{3,4},{4,3},{5,6},{6,5},{7,8},{8,7},{9,10},{10,... | collective-permute-start | bytes 147464 | tf_op jit(solution)/shard_map/ppermute | solution.py:501
  65.3 4.7 %collective-permute-start.4 = (f32[4,64,128]{2,1,0:T(8,128)S(1)}, f32[4,64,128]{2,1,0:T(8,128)S(1)}, u32[]{:S(2)}, u32[]{:S(2)}) collective-permute-start(f32[4,64,128]{2,1,0:T(8,128)S(1)} %get-tuple-element.63), channel_id=1, source_target_pairs={{0,32},{32,0},{64,96},{96,64},{128,160},{160,128},{192,224},{224,1... | collective-permute-start | bytes 393224 | tf_op jit(solution)/shard_map/ppermute | solution.py:507
  68.0 4.7 %collective-permute-start.5 = (f32[4,64,128]{2,1,0:T(8,128)S(1)}, f32[4,64,128]{2,1,0:T(8,128)S(1)}, u32[]{:S(2)}, u32[]{:S(2)}) collective-permute-start(f32[4,64,128]{2,1,0:T(8,128)S(1)} %get-tuple-element.64), channel_id=1, source_target_pairs={{0,224},{32,64},{64,32},{96,128},{128,96},{160,192},{192,160},{224... | collective-permute-start | bytes 393224 | tf_op jit(solution)/shard_map/ppermute | solution.py:506
  69.3 6.7 %collective-permute-start.6 = (f32[8,8,128]{2,1,0:T(8,128)S(1)}, f32[8,8,128]{2,1,0:T(8,128)S(1)}, u32[]{:S(2)}, u32[]{:S(2)}) collective-permute-start(f32[8,8,128]{2,1,0:T(8,128)S(1)} %get-tuple-element.65), channel_id=1, source_target_pairs={{0,1},{1,0},{2,3},{3,2},{4,5},{5,4},{6,7},{7,6},{8,9},{9,8},{10,11... | collective-permute-start | bytes 98312 | tf_op jit(solution)/shard_map/ppermute | solution.py:508
  69.3 6.8 %collective-permute-start.7 = (f32[8,8,128]{2,1,0:T(8,128)S(1)}, f32[8,8,128]{2,1,0:T(8,128)S(1)}, u32[]{:S(2)}, u32[]{:S(2)}) collective-permute-start(f32[8,8,128]{2,1,0:T(8,128)S(1)} %get-tuple-element.66), channel_id=1, source_target_pairs={{0,31},{1,2},{2,1},{3,4},{4,3},{5,6},{6,5},{7,8},{8,7},{9,10},{10,... | collective-permute-start | bytes 98312 | tf_op jit(solution)/shard_map/ppermute | solution.py:509
  72.7 3.4 %collective-permute-start.8 = (f32[4,8,128]{2,1,0:T(8,128)S(1)}, f32[4,8,128]{2,1,0:T(8,128)S(1)}, u32[]{:S(2)}, u32[]{:S(2)}) collective-permute-start(f32[4,8,128]{2,1,0:T(8,128)S(1)} %get-tuple-element.67), channel_id=1, source_target_pairs={{0,1},{1,0},{2,3},{3,2},{4,5},{5,4},{6,7},{7,6},{8,9},{9,8},{10,11... | collective-permute-start | bytes 49160 | tf_op jit(solution)/shard_map/ppermute | solution.py:512
  72.8 6.0 %collective-permute-start.9 = (f32[4,8,128]{2,1,0:T(8,128)S(1)}, f32[4,8,128]{2,1,0:T(8,128)S(1)}, u32[]{:S(2)}, u32[]{:S(2)}) collective-permute-start(f32[4,8,128]{2,1,0:T(8,128)S(1)} %get-tuple-element.68), channel_id=1, source_target_pairs={{0,31},{1,2},{2,1},{3,4},{4,3},{5,6},{6,5},{7,8},{8,7},{9,10},{10,... | collective-permute-start | bytes 49160 | tf_op jit(solution)/shard_map/ppermute | solution.py:513
  82.9 26.7 %collective-permute-start.12 = (bf16[16,64,128]{2,1,0:T(8,128)(2,1)S(1)}, bf16[16,64,128]{2,1,0:T(8,128)(2,1)S(1)}, u32[]{:S(2)}, u32[]{:S(2)}) collective-permute-start(bf16[16,64,128]{2,1,0:T(8,128)(2,1)S(1)} %get-tuple-element.71.refs_0_), channel_id=1, source_target_pairs={{0,128},{32,160},{64,192},{96,224},{128,0},{160,32},{192,64},{224,... | collective-permute-start | bytes 786440 | tf_op jit(solution)/shard_map/ppermute | solution.py:518
  85.6 24.1 %collective-permute-start.11 = (bf16[16,64,128]{2,1,0:T(8,128)(2,1)S(1)}, bf16[16,64,128]{2,1,0:T(8,128)(2,1)S(1)}, u32[]{:S(2)}, u32[]{:S(2)}) collective-permute-start(bf16[16,64,128]{2,1,0:T(8,128)(2,1)S(1)} %get-tuple-element.71.refs_0_), channel_id=1, source_target_pairs={{0,192},{32,224},{64,0},{96,32},{128,64},{160,96},{192,128},{224,1... | collective-permute-start | bytes 786440 | tf_op jit(solution)/shard_map/ppermute | solution.py:517
  86.6 23.1 %collective-permute-start.10 = (bf16[16,64,128]{2,1,0:T(8,128)(2,1)S(1)}, bf16[16,64,128]{2,1,0:T(8,128)(2,1)S(1)}, u32[]{:S(2)}, u32[]{:S(2)}) collective-permute-start(bf16[16,64,128]{2,1,0:T(8,128)(2,1)S(1)} %get-tuple-element.71.refs_0_), channel_id=1, source_target_pairs={{0,64},{32,96},{64,128},{96,160},{128,192},{160,224},{192,0},{224,... | collective-permute-start | bytes 786440 | tf_op jit(solution)/shard_map/ppermute | solution.py:516
  87.2 22.5 %all-to-all-start.1 = ((f32[256,1,128]{2,1,0:T(1,128)}), f32[256,1,128]{2,1,0:T(1,128)S(1)}, u32[]{:S(2)}, u32[]{:S(2)}) async-start(f32[256,1,128]{2,1,0:T(1,128)} %bitcast.5), calls=%async_computation.1 | async-start | bytes 262144 | tf_op jit(solution)/shard_map/all_to_all | solution.py:520
  97.1 13.9 %collective-permute-start.13 = (bf16[16,64,128]{2,1,0:T(8,128)(2,1)S(1)}, bf16[16,64,128]{2,1,0:T(8,128)(2,1)S(1)}, u32[]{:S(2)}, u32[]{:S(2)}) collective-permute-start(bf16[16,64,128]{2,1,0:T(8,128)(2,1)S(1)} %get-tuple-element.71.refs_0_), channel_id=1, source_target_pairs={{0,32},{32,0},{64,96},{96,64},{128,160},{160,128},{192,224},{224,1... | collective-permute-start | bytes 786440 | tf_op jit(solution)/shard_map/ppermute | solution.py:519
  109.7 2.0 %collective-permute-start.14 = (bf16[16,64,128]{2,1,0:T(8,128)(2,1)S(1)}, bf16[16,64,128]{2,1,0:T(8,128)(2,1)S(1)}, u32[]{:S(2)}, u32[]{:S(2)}) collective-permute-start(bf16[16,64,128]{2,1,0:T(8,128)(2,1)S(1)} %collective-permute-done.10.refs_1_), channel_id=1, source_target_pairs={{0,32},{32,0},{64,96},{96,64},{128,160},{160,128},{192,224},{224,1... | collective-permute-start | bytes 786440 | tf_op jit(solution)/shard_map/ppermute | solution.py:522
  110.5 1.5 %collective-permute-start.15 = (bf16[16,64,128]{2,1,0:T(8,128)(2,1)S(1)}, bf16[16,64,128]{2,1,0:T(8,128)(2,1)S(1)}, u32[]{:S(2)}, u32[]{:S(2)}) collective-permute-start(bf16[16,64,128]{2,1,0:T(8,128)(2,1)S(1)} %collective-permute-done.11.refs_2_), channel_id=1, source_target_pairs={{0,32},{32,0},{64,96},{96,64},{128,160},{160,128},{192,224},{224,1... | collective-permute-start | bytes 786440 | tf_op jit(solution)/shard_map/ppermute | solution.py:522
  110.6 1.8 %collective-permute-start.16 = (bf16[16,64,128]{2,1,0:T(8,128)(2,1)S(1)}, bf16[16,64,128]{2,1,0:T(8,128)(2,1)S(1)}, u32[]{:S(2)}, u32[]{:S(2)}) collective-permute-start(bf16[16,64,128]{2,1,0:T(8,128)(2,1)S(1)} %collective-permute-done.12.refs_3_), channel_id=1, source_target_pairs={{0,32},{32,0},{64,96},{96,64},{128,160},{160,128},{192,224},{224,1... | collective-permute-start | bytes 786440 | tf_op jit(solution)/shard_map/ppermute | solution.py:522

commit v6 on v5

--- a/solution.py
+++ b/solution.py
@@ -515,8 +515,9 @@
     core = swap_even(n_g)
     before = lax.ppermute(grad, "gz", [(i, (i + 2) % n_g) for i in range(n_g)])
     after = lax.ppermute(grad, "gz", [(i, (i - 2) % n_g) for i in range(n_g)])
-    across = lax.ppermute(grad, "gz", [(i, (i + 4) % n_g) for i in range(n_g)])
     twin = lax.ppermute(grad, "gz", core)
+    again, twin = lax.optimization_barrier((grad, twin))
+    across = lax.ppermute(again, "gz", [(i, (i + 4) % n_g) for i in range(n_g)])
     sums = lax.all_to_all(total, ("gz", "xy"), 0, 0, tiled=True)
     before, after, across, sums = lax.optimization_barrier((before, after, across, sums))
     others = [lax.ppermute(piece, "gz", core) for piece in (before, after, across)]

time: 114 us -> 113 us (level)
  blocking collectives: 0 us -> 21.5 us
  waiting for transfers between devices: 54.7 us -> 43.5 us
  starting transfers between devices: 43.7 us -> 34.5 us
  Pallas kernels: 15.3 us -> 13.7 us
    all_to_all x0 -> x1, blocking collectives: none -> 21.5 us  [local(): sums = lax.all_to_all(total, ('gz', 'xy'), 0, 0, tiled=True)]
    all_to_all x1 -> x0, waiting for transfers between devices: 10.3 us -> none  [local(): sums = lax.all_to_all(total, ('gz', 'xy'), 0, 0, tiled=True)]
    all_to_all x1 -> x0, starting transfers between devices: 9.89 us -> none  [local(): sums = lax.all_to_all(total, ('gz', 'xy'), 0, 0, tiled=True)]
    ppermute x1, starting transfers between devices: 2.64 us -> 0.8 us  [local(): across = lax.ppermute(again, 'gz', [(i, (i + 4) % n_g) for i in range(n_g)])]
    ppermute x1, starting transfers between devices: 2.23 us -> 3.4 us  [local(): twin = lax.ppermute(grad, 'gz', core)]
  transfers between devices with their start and end apart: 19 -> 18, of which waited for: 9 -> 8; matrix products, arithmetic and copies ran while one was open for 0% -> 0% of each run, Pallas kernels for 4% -> 4%
where the time goes in v6:
time: 113 us; the launch traced here: 114 us
  waiting for transfers between devices  43.5 us (38%)
  starting transfers between devices  34.5 us (31%)
  blocking collectives  21.5 us (19%)
  Pallas kernels  13.7 us (12%)
    ppermute x1, waiting for transfers between devices, local(): qm_d = lax.ppermute(m_d, 'xy', y_odd)  33.9 us
    all_to_all x1, blocking collectives, local(): sums = lax.all_to_all(total, ('gz', 'xy'), 0, 0, tiled=True)  21.5 us
    all_to_all x1, starting transfers between devices, local(): lax.all_to_all(send.reshape(n_x, CAP * 64, 128), 'xy', split_axis=0, conc...  12 us
    ppermute x1, starting transfers between devices, local(): qm_d = lax.ppermute(m_d, 'xy', y_odd)  3.98 us
    ppermute x1, waiting for transfers between devices, local(): rc_b = lax.ppermute(c_b, 'gz', z_odd)  3.5 us
    pallas_call x1, Pallas kernels, stencil(): pl.pallas_call(stencil_kernel, out_shape=(sds((16, 64, 128), BF16), sds((...  3.46 us
    ppermute x1, starting transfers between devices, local(): twin = lax.ppermute(grad, 'gz', core)  3.4 us
    pallas_call x1, Pallas kernels, pack(): pl.pallas_call(pack_kernel, out_shape=sds((32 * CAP, 64, 128), BF16), in_...  2.87 us
  transfers between devices with their start and end apart: 18, of which 8 were waited for; matrix products, arithmetic and copies ran while one was open for 0% of the time, Pallas kernels for 4%

profile of v6, /device:TPU:1, one launch (start us, length us, event | category | flops | bytes accessed | tf_op | source)
XLA Modules:
  0.0 113.5 jit_solution(2501713498667337937)
XLA Ops:
  0.0 2.9 %pack.1 = bf16[128,64,128]{2,1,0:T(8,128)(2,1)} custom-call(f32[32,8,8,128]{3,2,1,0:T(8,128)} %vel_any.1, s32[32]{0:T(128)} %off.1, f32[32]{0:T(128)} %wt.1, s32[64,128]{1,0:T(8,128)} %bitcast.10), custom_call_target="tpu_custom_call" | custom-call | tf_op jit(solution)/shard_map/pack/pallas_call | solution.py:73
  2.9 12.0 %all-to-all-start = ((bf16[32,256,128]{2,1,0:T(8,128)(2,1)}), bf16[32,256,128]{2,1,0:T(8,128)(2,1)S(1)}, u32[]{:S(2)}, u32[]{:S(2)}) async-start(bf16[32,256,128]{2,1,0:T(8,128)(2,1)} %bitcast.14), calls=%async_computation | async-start | bytes 4194304 | tf_op jit(solution)/shard_map/all_to_all | solution.py:493
  15.0 0.7 prepare.1
  15.7 1.0 collective-permute-start
  16.6 1.2 %collective-permute-start.1 = (f32[4,64,128]{2,1,0:T(8,128)S(1)}, f32[4,64,128]{2,1,0:T(8,128)S(1)}, u32[]{:S(2)}, u32[]{:S(2)}) collective-permute-start(f32[4,64,128]{2,1,0:T(8,128)S(1)} %get-tuple-element.52), channel_id=1, source_target_pairs={{0,224},{32,64},{64,32},{96,128},{128,96},{160,192},{192,160},{224... | collective-permute-start | bytes 393224 | tf_op jit(solution)/shard_map/ppermute | solution.py:497
  17.8 3.5 %collective-permute-done.1.r_b = f32[4,64,128]{2,1,0:T(8,128)S(1)} collective-permute-done((f32[4,64,128]{2,1,0:T(8,128)S(1)}, f32[4,64,128]{2,1,0:T(8,128)S(1)}, u32[]{:S(2)}, u32[]{:S(2)}) %collective-permute-start.1) | collective-permute-done | bytes 131104 | tf_op jit(solution)/shard_map/ppermute | solution.py:497
  21.3 1.6 %collective-permute-start.2 = (f32[12,8,128]{2,1,0:T(8,128)S(1)}, f32[12,8,128]{2,1,0:T(8,128)S(1)}, u32[]{:S(2)}, u32[]{:S(2)}) collective-permute-start(f32[12,8,128]{2,1,0:T(8,128)S(1)} %get-tuple-element.53), channel_id=1, source_target_pairs={{0,1},{1,0},{2,3},{3,2},{4,5},{5,4},{6,7},{7,6},{8,9},{9,8},{10,11... | collective-permute-start | bytes 147464 | tf_op jit(solution)/shard_map/ppermute | solution.py:500
  22.9 4.0 %collective-permute-start.3 = (f32[12,8,128]{2,1,0:T(8,128)S(1)}, f32[12,8,128]{2,1,0:T(8,128)S(1)}, u32[]{:S(2)}, u32[]{:S(2)}) collective-permute-start(f32[12,8,128]{2,1,0:T(8,128)S(1)} %get-tuple-element.54), channel_id=1, source_target_pairs={{0,31},{1,2},{2,1},{3,4},{4,3},{5,6},{6,5},{7,8},{8,7},{9,10},{10,... | collective-permute-start | bytes 147464 | tf_op jit(solution)/shard_map/ppermute | solution.py:501
  26.9 2.4 %lists.1 = (s32[16]{0:T(128)S(1)}, s32[2048]{0:T(1024)S(1)}) custom-call(s32[8,128]{1,0:T(8,128)S(1)} %get-tuple-element.47.code), custom_call_target="tpu_custom_call" | custom-call | tf_op jit(solution)/shard_map/lists/pallas_call | solution.py:160
  29.4 33.9 %collective-permute-done.3.q_d = f32[12,8,128]{2,1,0:T(8,128)S(1)} collective-permute-done((f32[12,8,128]{2,1,0:T(8,128)S(1)}, f32[12,8,128]{2,1,0:T(8,128)S(1)}, u32[]{:S(2)}, u32[]{:S(2)}) %collective-permute-start.3) | collective-permute-done | bytes 49184 | tf_op jit(solution)/shard_map/ppermute | solution.py:501
  63.4 1.0 combine.1
  64.4 2.7 %collective-permute-start.4 = (f32[4,64,128]{2,1,0:T(8,128)S(1)}, f32[4,64,128]{2,1,0:T(8,128)S(1)}, u32[]{:S(2)}, u32[]{:S(2)}) collective-permute-start(f32[4,64,128]{2,1,0:T(8,128)S(1)} %get-tuple-element.65), channel_id=1, source_target_pairs={{0,32},{32,0},{64,96},{96,64},{128,160},{160,128},{192,224},{224,1... | collective-permute-start | bytes 393224 | tf_op jit(solution)/shard_map/ppermute | solution.py:507
  67.1 1.3 %collective-permute-start.5 = (f32[4,64,128]{2,1,0:T(8,128)S(1)}, f32[4,64,128]{2,1,0:T(8,128)S(1)}, u32[]{:S(2)}, u32[]{:S(2)}) collective-permute-start(f32[4,64,128]{2,1,0:T(8,128)S(1)} %get-tuple-element.66), channel_id=1, source_target_pairs={{0,224},{32,64},{64,32},{96,128},{128,96},{160,192},{192,160},{224... | collective-permute-start | bytes 393224 | tf_op jit(solution)/shard_map/ppermute | solution.py:506
  68.4 0.5 collective-permute-start.6
  69.0 1.0 collective-permute-start.7
  70.0 1.8 %collective-permute-done.5.r_b = f32[4,64,128]{2,1,0:T(8,128)S(1)} collective-permute-done((f32[4,64,128]{2,1,0:T(8,128)S(1)}, f32[4,64,128]{2,1,0:T(8,128)S(1)}, u32[]{:S(2)}, u32[]{:S(2)}) %collective-permute-start.5) | collective-permute-done | bytes 131104 | tf_op jit(solution)/shard_map/ppermute | solution.py:506
  71.8 0.7 collective-permute-start.8
  72.5 1.4 %collective-permute-start.9 = (f32[4,8,128]{2,1,0:T(8,128)S(1)}, f32[4,8,128]{2,1,0:T(8,128)S(1)}, u32[]{:S(2)}, u32[]{:S(2)}) collective-permute-start(f32[4,8,128]{2,1,0:T(8,128)S(1)} %get-tuple-element.70), channel_id=1, source_target_pairs={{0,31},{1,2},{2,1},{3,4},{4,3},{5,6},{6,5},{7,8},{8,7},{9,10},{10,... | collective-permute-start | bytes 49160 | tf_op jit(solution)/shard_map/ppermute | solution.py:513
  74.0 1.7 %model.1.gm = f32[3,20,80,128]{3,2,1,0:T(8,128)S(1)} custom-call(f32[16,64,128]{2,1,0:T(8,128)S(1)} %copy-done, f32[4,64,128]{2,1,0:T(8,128)S(1)} %collective-permute-done.r_a, f32[4,64,128]{2,1,0:T(8,128)S(1)} %collective-permute-done.1.r_b, f32[12,8,128]{2,1,0:T(8,128)S(1)} %collective-permute-done.2.q_c, f32[12,8,128]{2,1,0:T(8,128)S(1)} %collective-permute-done.3.q_d), custom_call_target="tpu_custom_call" | custom-call | flops 200000000 | bytes 8000000 | tf_op jit(solution)/shard_map/model/pallas_call | solution.py:361
  75.8 2.7 %collective-permute-done.9.k_d = f32[4,8,128]{2,1,0:T(8,128)S(1)} collective-permute-done((f32[4,8,128]{2,1,0:T(8,128)S(1)}, f32[4,8,128]{2,1,0:T(8,128)S(1)}, u32[]{:S(2)}, u32[]{:S(2)}) %collective-permute-start.9) | collective-permute-done | bytes 16416 | tf_op jit(solution)/shard_map/ppermute | solution.py:513
  78.4 3.5 %stencil.1 = (bf16[16,64,128]{2,1,0:T(8,128)(2,1)S(1)}, f32[256,128]{1,0:T(8,128)S(1)}) custom-call(f32[16,64,128]{2,1,0:T(8,128)S(1)} %get-tuple-element.58.v, f32[4,64,128]{2,1,0:T(8,128)S(1)} %collective-permute-done.4.r_a, f32[4,64,128]{2,1,0:T(8,128)S(1)} %collective-permute-done.5.r_b, f32[8,8,128]{2,1,0:T(8,128)S(1)} %collective-permute-done.6.q_c, ...), custom_call_target="tpu_custom_call" | custom-call | tf_op jit(solution)/shard_map/stencil/pallas_call | solution.py:427
  81.9 3.4 %collective-permute-start.12 = (bf16[16,64,128]{2,1,0:T(8,128)(2,1)S(1)}, bf16[16,64,128]{2,1,0:T(8,128)(2,1)S(1)}, u32[]{:S(2)}, u32[]{:S(2)}) collective-permute-start(bf16[16,64,128]{2,1,0:T(8,128)(2,1)S(1)} %get-tuple-element.74.refs_0_), channel_id=1, source_target_pairs={{0,32},{32,0},{64,96},{96,64},{128,160},{160,128},{192,224},{224,1... | collective-permute-start | bytes 786440 | tf_op jit(solution)/shard_map/ppermute | solution.py:518
  85.3 0.6 collective-permute-start.11
  86.0 0.8 collective-permute-start.10
  86.8 0.8 collective-permute-start.13
  87.6 21.5 %all_to_all.17 = f32[256,1,128]{2,1,0:T(1,128)S(1)} all-to-all(f32[256,1,128]{2,1,0:T(1,128)S(1)} %bitcast.12), channel_id=1, replica_groups=mesh['gz'=8,'xy'=32] {'gz','xy'}, dimensions={0} | all-to-all | bytes 262144 | tf_op jit(solution)/shard_map/all_to_all | solution.py:521
  109.1 0.8 collective-permute-start.14
  110.0 0.4 collective-permute-start.16
  110.4 0.7 collective-permute-done.14.refs_5_
  111.1 0.4 collective-permute-done.15.refs_6_
  111.5 0.4 collective-permute-done.16.refs_7_
  111.8 1.5 %scale.1 = bf16[128,64,128]{2,1,0:T(8,128)(2,1)} custom-call(f32[256,128]{1,0:T(8,128)S(1)} %bitcast.9, bf16[16,64,128]{2,1,0:T(8,128)(2,1)S(1)} %get-tuple-element.74.refs_0_, bf16[16,64,128]{2,1,0:T(8,128)(2,1)S(1)} %collective-permute-done.10.refs_1_, bf16[16,64,128]{2,1,0:T(8,128)(2,1)S(1)} %collective-permute-done.11.refs_2_, ...), custom_call_target="tpu_custom_call" | custom-call | tf_op jit(solution)/shard_map/scale/pallas_call | solution.py:464
  (20 shorter events, 0.3 us)
Async XLA Ops:
  2.9 12.1 %copy-start = (f32[16,64,128]{2,1,0:T(8,128)S(1)}, f32[16,64,128]{2,1,0:T(8,128)}, u32[]{:S(2)}) copy-start(f32[16,64,128]{2,1,0:T(8,128)} %cond.1) | copy-start | bytes 1572868
  2.9 12.1 %copy-start.1 = (s32[8192,1]{0,1:T(1,128)S(1)}, s32[8192,1]{0,1:T(1,128)}, u32[]{:S(2)}) copy-start(s32[8192,1]{0,1:T(1,128)} %param.9) | copy-start | bytes 98308
  2.9 12.1 %copy-start.2 = (s32[8192]{0:T(1024)S(1)}, s32[8192]{0:T(1024)}, u32[]{:S(2)}) copy-start(s32[8192]{0:T(1024)} %param.10) | copy-start | bytes 98308
  2.9 60.5 %all-to-all-start = ((bf16[32,256,128]{2,1,0:T(8,128)(2,1)}), bf16[32,256,128]{2,1,0:T(8,128)(2,1)S(1)}, u32[]{:S(2)}, u32[]{:S(2)}) async-start(bf16[32,256,128]{2,1,0:T(8,128)(2,1)} %bitcast.14), calls=%async_computation | async-start | bytes 4194304 | tf_op jit(solution)/shard_map/all_to_all | solution.py:493
  15.7 2.1 %collective-permute-start = (f32[4,64,128]{2,1,0:T(8,128)S(1)}, f32[4,64,128]{2,1,0:T(8,128)S(1)}, u32[]{:S(2)}, u32[]{:S(2)}) collective-permute-start(f32[4,64,128]{2,1,0:T(8,128)S(1)} %get-tuple-element.51), channel_id=1, source_target_pairs={{0,32},{32,0},{64,96},{96,64},{128,160},{160,128},{192,224},{224,1... | collective-permute-start | bytes 393224 | tf_op jit(solution)/shard_map/ppermute | solution.py:498
  16.6 4.7 %collective-permute-start.1 = (f32[4,64,128]{2,1,0:T(8,128)S(1)}, f32[4,64,128]{2,1,0:T(8,128)S(1)}, u32[]{:S(2)}, u32[]{:S(2)}) collective-permute-start(f32[4,64,128]{2,1,0:T(8,128)S(1)} %get-tuple-element.52), channel_id=1, source_target_pairs={{0,224},{32,64},{64,32},{96,128},{128,96},{160,192},{192,160},{224... | collective-permute-start | bytes 393224 | tf_op jit(solution)/shard_map/ppermute | solution.py:497
  21.3 8.0 %collective-permute-start.2 = (f32[12,8,128]{2,1,0:T(8,128)S(1)}, f32[12,8,128]{2,1,0:T(8,128)S(1)}, u32[]{:S(2)}, u32[]{:S(2)}) collective-permute-start(f32[12,8,128]{2,1,0:T(8,128)S(1)} %get-tuple-element.53), channel_id=1, source_target_pairs={{0,1},{1,0},{2,3},{3,2},{4,5},{5,4},{6,7},{7,6},{8,9},{9,8},{10,11... | collective-permute-start | bytes 147464 | tf_op jit(solution)/shard_map/ppermute | solution.py:500
  22.9 40.3 %collective-permute-start.3 = (f32[12,8,128]{2,1,0:T(8,128)S(1)}, f32[12,8,128]{2,1,0:T(8,128)S(1)}, u32[]{:S(2)}, u32[]{:S(2)}) collective-permute-start(f32[12,8,128]{2,1,0:T(8,128)S(1)} %get-tuple-element.54), channel_id=1, source_target_pairs={{0,31},{1,2},{2,1},{3,4},{4,3},{5,6},{6,5},{7,8},{8,7},{9,10},{10,... | collective-permute-start | bytes 147464 | tf_op jit(solution)/shard_map/ppermute | solution.py:501
  64.4 5.6 %collective-permute-start.4 = (f32[4,64,128]{2,1,0:T(8,128)S(1)}, f32[4,64,128]{2,1,0:T(8,128)S(1)}, u32[]{:S(2)}, u32[]{:S(2)}) collective-permute-start(f32[4,64,128]{2,1,0:T(8,128)S(1)} %get-tuple-element.65), channel_id=1, source_target_pairs={{0,32},{32,0},{64,96},{96,64},{128,160},{160,128},{192,224},{224,1... | collective-permute-start | bytes 393224 | tf_op jit(solution)/shard_map/ppermute | solution.py:507
  67.1 4.7 %collective-permute-start.5 = (f32[4,64,128]{2,1,0:T(8,128)S(1)}, f32[4,64,128]{2,1,0:T(8,128)S(1)}, u32[]{:S(2)}, u32[]{:S(2)}) collective-permute-start(f32[4,64,128]{2,1,0:T(8,128)S(1)} %get-tuple-element.66), channel_id=1, source_target_pairs={{0,224},{32,64},{64,32},{96,128},{128,96},{160,192},{192,160},{224... | collective-permute-start | bytes 393224 | tf_op jit(solution)/shard_map/ppermute | solution.py:506
  68.4 7.3 %collective-permute-start.6 = (f32[8,8,128]{2,1,0:T(8,128)S(1)}, f32[8,8,128]{2,1,0:T(8,128)S(1)}, u32[]{:S(2)}, u32[]{:S(2)}) collective-permute-start(f32[8,8,128]{2,1,0:T(8,128)S(1)} %get-tuple-element.67), channel_id=1, source_target_pairs={{0,1},{1,0},{2,3},{3,2},{4,5},{5,4},{6,7},{7,6},{8,9},{9,8},{10,11... | collective-permute-start | bytes 98312 | tf_op jit(solution)/shard_map/ppermute | solution.py:508
  69.0 6.8 %collective-permute-start.7 = (f32[8,8,128]{2,1,0:T(8,128)S(1)}, f32[8,8,128]{2,1,0:T(8,128)S(1)}, u32[]{:S(2)}, u32[]{:S(2)}) collective-permute-start(f32[8,8,128]{2,1,0:T(8,128)S(1)} %get-tuple-element.68), channel_id=1, source_target_pairs={{0,31},{1,2},{2,1},{3,4},{4,3},{5,6},{6,5},{7,8},{8,7},{9,10},{10,... | collective-permute-start | bytes 98312 | tf_op jit(solution)/shard_map/ppermute | solution.py:509
  71.8 3.9 %collective-permute-start.8 = (f32[4,8,128]{2,1,0:T(8,128)S(1)}, f32[4,8,128]{2,1,0:T(8,128)S(1)}, u32[]{:S(2)}, u32[]{:S(2)}) collective-permute-start(f32[4,8,128]{2,1,0:T(8,128)S(1)} %get-tuple-element.69), channel_id=1, source_target_pairs={{0,1},{1,0},{2,3},{3,2},{4,5},{5,4},{6,7},{7,6},{8,9},{9,8},{10,11... | collective-permute-start | bytes 49160 | tf_op jit(solution)/shard_map/ppermute | solution.py:512
  72.5 5.9 %collective-permute-start.9 = (f32[4,8,128]{2,1,0:T(8,128)S(1)}, f32[4,8,128]{2,1,0:T(8,128)S(1)}, u32[]{:S(2)}, u32[]{:S(2)}) collective-permute-start(f32[4,8,128]{2,1,0:T(8,128)S(1)} %get-tuple-element.70), channel_id=1, source_target_pairs={{0,31},{1,2},{2,1},{3,4},{4,3},{5,6},{6,5},{7,8},{8,7},{9,10},{10,... | collective-permute-start | bytes 49160 | tf_op jit(solution)/shard_map/ppermute | solution.py:513
  81.9 4.9 %collective-permute-start.12 = (bf16[16,64,128]{2,1,0:T(8,128)(2,1)S(1)}, bf16[16,64,128]{2,1,0:T(8,128)(2,1)S(1)}, u32[]{:S(2)}, u32[]{:S(2)}) collective-permute-start(bf16[16,64,128]{2,1,0:T(8,128)(2,1)S(1)} %get-tuple-element.74.refs_0_), channel_id=1, source_target_pairs={{0,32},{32,0},{64,96},{96,64},{128,160},{160,128},{192,224},{224,1... | collective-permute-start | bytes 786440 | tf_op jit(solution)/shard_map/ppermute | solution.py:518
  85.3 23.8 %collective-permute-start.11 = (bf16[16,64,128]{2,1,0:T(8,128)(2,1)S(1)}, bf16[16,64,128]{2,1,0:T(8,128)(2,1)S(1)}, u32[]{:S(2)}, u32[]{:S(2)}) collective-permute-start(bf16[16,64,128]{2,1,0:T(8,128)(2,1)S(1)} %get-tuple-element.74.refs_0_), channel_id=1, source_target_pairs={{0,192},{32,224},{64,0},{96,32},{128,64},{160,96},{192,128},{224,1... | collective-permute-start | bytes 786440 | tf_op jit(solution)/shard_map/ppermute | solution.py:517
  86.0 23.1 %collective-permute-start.10 = (bf16[16,64,128]{2,1,0:T(8,128)(2,1)S(1)}, bf16[16,64,128]{2,1,0:T(8,128)(2,1)S(1)}, u32[]{:S(2)}, u32[]{:S(2)}) collective-permute-start(bf16[16,64,128]{2,1,0:T(8,128)(2,1)S(1)} %get-tuple-element.74.refs_0_), channel_id=1, source_target_pairs={{0,64},{32,96},{64,128},{96,160},{128,192},{160,224},{192,0},{224,... | collective-permute-start | bytes 786440 | tf_op jit(solution)/shard_map/ppermute | solution.py:516
  86.8 22.3 %collective-permute-start.13 = (bf16[16,64,128]{2,1,0:T(8,128)(2,1)S(1)}, bf16[16,64,128]{2,1,0:T(8,128)(2,1)S(1)}, u32[]{:S(2)}, u32[]{:S(2)}) collective-permute-start(bf16[16,64,128]{2,1,0:T(8,128)(2,1)S(1)} %get-tuple-element.74.refs_0_), channel_id=1, source_target_pairs={{0,128},{32,160},{64,192},{96,224},{128,0},{160,32},{192,64},{224,... | collective-permute-start | bytes 786440 | tf_op jit(solution)/shard_map/ppermute | solution.py:520
  109.1 2.0 %collective-permute-start.14 = (bf16[16,64,128]{2,1,0:T(8,128)(2,1)S(1)}, bf16[16,64,128]{2,1,0:T(8,128)(2,1)S(1)}, u32[]{:S(2)}, u32[]{:S(2)}) collective-permute-start(bf16[16,64,128]{2,1,0:T(8,128)(2,1)S(1)} %collective-permute-done.10.refs_1_), channel_id=1, source_target_pairs={{0,32},{32,0},{64,96},{96,64},{128,160},{160,128},{192,224},{224,1... | collective-permute-start | bytes 786440 | tf_op jit(solution)/shard_map/ppermute | solution.py:523
  109.9 1.5 %collective-permute-start.15 = (bf16[16,64,128]{2,1,0:T(8,128)(2,1)S(1)}, bf16[16,64,128]{2,1,0:T(8,128)(2,1)S(1)}, u32[]{:S(2)}, u32[]{:S(2)}) collective-permute-start(bf16[16,64,128]{2,1,0:T(8,128)(2,1)S(1)} %collective-permute-done.11.refs_2_), channel_id=1, source_target_pairs={{0,32},{32,0},{64,96},{96,64},{128,160},{160,128},{192,224},{224,1... | collective-permute-start | bytes 786440 | tf_op jit(solution)/shard_map/ppermute | solution.py:523
  110.0 1.8 %collective-permute-start.16 = (bf16[16,64,128]{2,1,0:T(8,128)(2,1)S(1)}, bf16[16,64,128]{2,1,0:T(8,128)(2,1)S(1)}, u32[]{:S(2)}, u32[]{:S(2)}) collective-permute-start(bf16[16,64,128]{2,1,0:T(8,128)(2,1)S(1)} %collective-permute-done.13.refs_3_), channel_id=1, source_target_pairs={{0,32},{32,0},{64,96},{96,64},{128,160},{160,128},{192,224},{224,1... | collective-permute-start | bytes 786440 | tf_op jit(solution)/shard_map/ppermute | solution.py:523

commit v7 on v6

--- a/solution.py
+++ b/solution.py
@@ -440,15 +440,19 @@
     )(v, r_a, r_b, q_c, q_d, k_c, k_d, gm)
 
 
-def scale_kernel(cells, sums, *refs):
+def scale_kernel(cells, later, sums, *refs):
     pieces, out, held, sems = refs[:-3], refs[-3], refs[-2], refs[-1]
+    if later:
+        pieces = pieces[1:]
     g = lax.axis_index("gz")
     total = jnp.sum(sums[...], axis=0, keepdims=True)
     total = jnp.sum(total, axis=1, keepdims=True)
     scale = 1.0 / jnp.sqrt(total / cells + 1e-06)
     scale = jnp.broadcast_to(scale, (64, 128))
     left, right, across = lax.rem(g + 6, 8), lax.rem(g + 2, 8), lax.rem(g + 4, 8)
-    owners = (g, left, right, across, g ^ 1, left ^ 1, right ^ 1, across ^ 1)
+    owners = (g, left, right, across, g ^ 1)
+    if later:
+        owners = (left ^ 1, right ^ 1, across ^ 1)
     copies = []
     for k, (piece, owner) in enumerate(zip(pieces, owners)):
         for z in range(16):
@@ -460,16 +464,21 @@
         copy.wait()
 
 
-def scaled(cells, sums, pieces):
-    return pl.pallas_call(
-        functools.partial(scale_kernel, cells),
+def scaled(cells, sums, pieces, begun=None):
+    anywhere = pl.BlockSpec(memory_space=pl.ANY)
+    later = begun is not None
+    n = len(pieces)
+    return pl.pallas_call(
+        functools.partial(scale_kernel, cells, later),
         out_shape=sds((128, 64, 128), BF16),
-        in_specs=[vspec()] * (1 + len(pieces)),
-        out_specs=pl.BlockSpec(memory_space=pl.ANY),
-        scratch_shapes=[pltpu.VMEM((8, 16, 64, 128), BF16), pltpu.SemaphoreType.DMA((8,))],
-        compiler_params=params(),
+        in_specs=[vspec()] + [anywhere] * later + [vspec()] * n,
+        out_specs=anywhere,
+        scratch_shapes=[pltpu.VMEM((n, 16, 64, 128), BF16), pltpu.SemaphoreType.DMA((n,))],
+        input_output_aliases={1: 0} if later else {},
+        compiler_params=params(),
+        cost_estimate=pl.CostEstimate(flops=n * 262144, bytes_accessed=n * 524288, transcendentals=0),
         name="scale",
-    )(sums, *pieces)
+    )(sums, *([begun] if later else []), *pieces)
 
 
 def swap_odd(count):
@@ -521,9 +530,9 @@
     sums = lax.all_to_all(total, ("gz", "xy"), 0, 0, tiled=True)
     before, after, across, sums = lax.optimization_barrier((before, after, across, sums))
     others = [lax.ppermute(piece, "gz", core) for piece in (before, after, across)]
-    pieces = [grad, before, after, across, twin] + others
     cells = float(n_g * n_x * 16 * 64 * 128)
-    return scaled(cells, sums, pieces)
+    begun = scaled(cells, sums, [grad, before, after, across, twin])
+    return scaled(cells, sums, others, begun)
 
 
 def solution(mesh):

time: 113 us -> 112 us (level)
  waiting for transfers between devices: 43.5 us -> 42.2 us
    ppermute x3, waiting for transfers between devices: 1.4 us -> 0.12 us  [local(): lax.ppermute(piece, 'gz', core)]
    pallas_call x1 -> x2, Pallas kernels: 1.55 us -> 2.33 us  [scaled(): pl.pallas_call(functools.partial(scale_kernel, cells, later), out_shape=s...]
  transfers between devices with their start and end apart: 18 -> 18, of which waited for: 8 -> 6; matrix products, arithmetic and copies ran while one was open for 0% -> 0% of each run, Pallas kernels for 4% -> 5%
where the time goes in v7:
time: 112 us
  waiting for transfers between devices  42.2 us (38%)
  starting transfers between devices  34.5 us (31%)
  blocking collectives  20.6 us (18%)
  Pallas kernels  14.5 us (13%)
    ppermute x1, waiting for transfers between devices, local(): qm_d = lax.ppermute(m_d, 'xy', y_odd)  33.9 us
    all_to_all x1, blocking collectives, local(): sums = lax.all_to_all(total, ('gz', 'xy'), 0, 0, tiled=True)  20.6 us
    all_to_all x1, starting transfers between devices, local(): lax.all_to_all(send.reshape(n_x, CAP * 64, 128), 'xy', split_axis=0, conc...  12 us
    ppermute x1, starting transfers between devices, local(): qm_d = lax.ppermute(m_d, 'xy', y_odd)  3.98 us
    ppermute x1, waiting for transfers between devices, local(): rc_b = lax.ppermute(c_b, 'gz', z_odd)  3.5 us
    pallas_call x1, Pallas kernels, stencil(): pl.pallas_call(stencil_kernel, out_shape=(sds((16, 64, 128), BF16), sds((...  3.46 us
    ppermute x1, starting transfers between devices, local(): twin = lax.ppermute(grad, 'gz', core)  3.39 us
    pallas_call x1, Pallas kernels, pack(): pl.pallas_call(pack_kernel, out_shape=sds((32 * CAP, 64, 128), BF16), in_...  2.87 us
  transfers between devices with their start and end apart: 18, of which 6 were waited for; matrix products, arithmetic and copies ran while one was open for 0% of the time, Pallas kernels for 5%

profile of v7, /device:TPU:1, one launch (start us, length us, event | category | flops | bytes accessed | tf_op | source)
XLA Modules:
  0.0 112.2 jit_solution(6065091308582214983)
XLA Ops:
  0.0 2.9 %pack.1 = bf16[128,64,128]{2,1,0:T(8,128)(2,1)} custom-call(f32[32,8,8,128]{3,2,1,0:T(8,128)} %vel_any.1, s32[32]{0:T(128)} %off.1, f32[32]{0:T(128)} %wt.1, s32[64,128]{1,0:T(8,128)} %bitcast.11), custom_call_target="tpu_custom_call" | custom-call | tf_op jit(solution)/shard_map/pack/pallas_call | solution.py:73
  2.9 12.0 %all-to-all-start = ((bf16[32,256,128]{2,1,0:T(8,128)(2,1)}), bf16[32,256,128]{2,1,0:T(8,128)(2,1)S(1)}, u32[]{:S(2)}, u32[]{:S(2)}) async-start(bf16[32,256,128]{2,1,0:T(8,128)(2,1)} %bitcast.15), calls=%async_computation | async-start | bytes 4194304 | tf_op jit(solution)/shard_map/all_to_all | solution.py:502
  15.0 0.7 prepare.1
  15.7 1.0 collective-permute-start
  16.6 1.2 %collective-permute-start.1 = (f32[4,64,128]{2,1,0:T(8,128)S(1)}, f32[4,64,128]{2,1,0:T(8,128)S(1)}, u32[]{:S(2)}, u32[]{:S(2)}) collective-permute-start(f32[4,64,128]{2,1,0:T(8,128)S(1)} %get-tuple-element.52), channel_id=1, source_target_pairs={{0,224},{32,64},{64,32},{96,128},{128,96},{160,192},{192,160},{224... | collective-permute-start | bytes 393224 | tf_op jit(solution)/shard_map/ppermute | solution.py:506
  17.8 3.5 %collective-permute-done.1.r_b = f32[4,64,128]{2,1,0:T(8,128)S(1)} collective-permute-done((f32[4,64,128]{2,1,0:T(8,128)S(1)}, f32[4,64,128]{2,1,0:T(8,128)S(1)}, u32[]{:S(2)}, u32[]{:S(2)}) %collective-permute-start.1) | collective-permute-done | bytes 131104 | tf_op jit(solution)/shard_map/ppermute | solution.py:506
  21.3 1.6 %collective-permute-start.2 = (f32[12,8,128]{2,1,0:T(8,128)S(1)}, f32[12,8,128]{2,1,0:T(8,128)S(1)}, u32[]{:S(2)}, u32[]{:S(2)}) collective-permute-start(f32[12,8,128]{2,1,0:T(8,128)S(1)} %get-tuple-element.53), channel_id=1, source_target_pairs={{0,1},{1,0},{2,3},{3,2},{4,5},{5,4},{6,7},{7,6},{8,9},{9,8},{10,11... | collective-permute-start | bytes 147464 | tf_op jit(solution)/shard_map/ppermute | solution.py:509
  22.9 4.0 %collective-permute-start.3 = (f32[12,8,128]{2,1,0:T(8,128)S(1)}, f32[12,8,128]{2,1,0:T(8,128)S(1)}, u32[]{:S(2)}, u32[]{:S(2)}) collective-permute-start(f32[12,8,128]{2,1,0:T(8,128)S(1)} %get-tuple-element.54), channel_id=1, source_target_pairs={{0,31},{1,2},{2,1},{3,4},{4,3},{5,6},{6,5},{7,8},{8,7},{9,10},{10,... | collective-permute-start | bytes 147464 | tf_op jit(solution)/shard_map/ppermute | solution.py:510
  26.9 2.4 %lists.1 = (s32[16]{0:T(128)S(1)}, s32[2048]{0:T(1024)S(1)}) custom-call(s32[8,128]{1,0:T(8,128)S(1)} %get-tuple-element.47.code), custom_call_target="tpu_custom_call" | custom-call | tf_op jit(solution)/shard_map/lists/pallas_call | solution.py:160
  29.4 33.9 %collective-permute-done.3.q_d = f32[12,8,128]{2,1,0:T(8,128)S(1)} collective-permute-done((f32[12,8,128]{2,1,0:T(8,128)S(1)}, f32[12,8,128]{2,1,0:T(8,128)S(1)}, u32[]{:S(2)}, u32[]{:S(2)}) %collective-permute-start.3) | collective-permute-done | bytes 49184 | tf_op jit(solution)/shard_map/ppermute | solution.py:510
  63.3 0.2 all-to-all-done
  63.4 1.0 combine.1
  64.4 2.7 %collective-permute-start.4 = (f32[4,64,128]{2,1,0:T(8,128)S(1)}, f32[4,64,128]{2,1,0:T(8,128)S(1)}, u32[]{:S(2)}, u32[]{:S(2)}) collective-permute-start(f32[4,64,128]{2,1,0:T(8,128)S(1)} %get-tuple-element.65), channel_id=1, source_target_pairs={{0,32},{32,0},{64,96},{96,64},{128,160},{160,128},{192,224},{224,1... | collective-permute-start | bytes 393224 | tf_op jit(solution)/shard_map/ppermute | solution.py:516
  67.1 1.3 %collective-permute-start.5 = (f32[4,64,128]{2,1,0:T(8,128)S(1)}, f32[4,64,128]{2,1,0:T(8,128)S(1)}, u32[]{:S(2)}, u32[]{:S(2)}) collective-permute-start(f32[4,64,128]{2,1,0:T(8,128)S(1)} %get-tuple-element.66), channel_id=1, source_target_pairs={{0,224},{32,64},{64,32},{96,128},{128,96},{160,192},{192,160},{224... | collective-permute-start | bytes 393224 | tf_op jit(solution)/shard_map/ppermute | solution.py:515
  68.4 0.6 collective-permute-start.6
  69.0 1.0 collective-permute-start.7
  70.0 1.9 %collective-permute-done.5.r_b = f32[4,64,128]{2,1,0:T(8,128)S(1)} collective-permute-done((f32[4,64,128]{2,1,0:T(8,128)S(1)}, f32[4,64,128]{2,1,0:T(8,128)S(1)}, u32[]{:S(2)}, u32[]{:S(2)}) %collective-permute-start.5) | collective-permute-done | bytes 131104 | tf_op jit(solution)/shard_map/ppermute | solution.py:515
  71.8 0.7 collective-permute-start.8
  72.5 1.5 %collective-permute-start.9 = (f32[4,8,128]{2,1,0:T(8,128)S(1)}, f32[4,8,128]{2,1,0:T(8,128)S(1)}, u32[]{:S(2)}, u32[]{:S(2)}) collective-permute-start(f32[4,8,128]{2,1,0:T(8,128)S(1)} %get-tuple-element.70), channel_id=1, source_target_pairs={{0,31},{1,2},{2,1},{3,4},{4,3},{5,6},{6,5},{7,8},{8,7},{9,10},{10,... | collective-permute-start | bytes 49160 | tf_op jit(solution)/shard_map/ppermute | solution.py:522
  74.0 1.7 %model.1.gm = f32[3,20,80,128]{3,2,1,0:T(8,128)S(1)} custom-call(f32[16,64,128]{2,1,0:T(8,128)S(1)} %copy-done, f32[4,64,128]{2,1,0:T(8,128)S(1)} %collective-permute-done.r_a, f32[4,64,128]{2,1,0:T(8,128)S(1)} %collective-permute-done.1.r_b, f32[12,8,128]{2,1,0:T(8,128)S(1)} %collective-permute-done.2.q_c, f32[12,8,128]{2,1,0:T(8,128)S(1)} %collective-permute-done.3.q_d), custom_call_target="tpu_custom_call" | custom-call | flops 200000000 | bytes 8000000 | tf_op jit(solution)/shard_map/model/pallas_call | solution.py:361
  75.8 2.7 %collective-permute-done.9.k_d = f32[4,8,128]{2,1,0:T(8,128)S(1)} collective-permute-done((f32[4,8,128]{2,1,0:T(8,128)S(1)}, f32[4,8,128]{2,1,0:T(8,128)S(1)}, u32[]{:S(2)}, u32[]{:S(2)}) %collective-permute-start.9) | collective-permute-done | bytes 16416 | tf_op jit(solution)/shard_map/ppermute | solution.py:522
  78.4 3.5 %stencil.1 = (bf16[16,64,128]{2,1,0:T(8,128)(2,1)S(1)}, f32[256,128]{1,0:T(8,128)S(1)}) custom-call(f32[16,64,128]{2,1,0:T(8,128)S(1)} %get-tuple-element.58.v, f32[4,64,128]{2,1,0:T(8,128)S(1)} %collective-permute-done.4.r_a, f32[4,64,128]{2,1,0:T(8,128)S(1)} %collective-permute-done.5.r_b, f32[8,8,128]{2,1,0:T(8,128)S(1)} %collective-permute-done.6.q_c, ...), custom_call_target="tpu_custom_call" | custom-call | tf_op jit(solution)/shard_map/stencil/pallas_call | solution.py:427
  81.9 3.4 %collective-permute-start.12 = (bf16[16,64,128]{2,1,0:T(8,128)(2,1)S(1)}, bf16[16,64,128]{2,1,0:T(8,128)(2,1)S(1)}, u32[]{:S(2)}, u32[]{:S(2)}) collective-permute-start(bf16[16,64,128]{2,1,0:T(8,128)(2,1)S(1)} %get-tuple-element.74.refs_0_), channel_id=1, source_target_pairs={{0,32},{32,0},{64,96},{96,64},{128,160},{160,128},{192,224},{224,1... | collective-permute-start | bytes 786440 | tf_op jit(solution)/shard_map/ppermute | solution.py:527
  85.3 0.7 collective-permute-start.11
  86.0 0.8 collective-permute-start.10
  86.8 0.8 collective-permute-start.13
  87.6 20.6 %all_to_all.17 = f32[256,1,128]{2,1,0:T(1,128)S(1)} all-to-all(f32[256,1,128]{2,1,0:T(1,128)S(1)} %bitcast.13), channel_id=1, replica_groups=mesh['gz'=8,'xy'=32] {'gz','xy'}, dimensions={0} | all-to-all | bytes 262144 | tf_op jit(solution)/shard_map/all_to_all | solution.py:530
  108.2 0.8 collective-permute-start.14
  109.2 0.4 collective-permute-start.16
  109.6 1.3 %scale.2.refs_0_ = bf16[128,64,128]{2,1,0:T(8,128)(2,1)} custom-call(f32[256,128]{1,0:T(8,128)S(1)} %bitcast.9, bf16[16,64,128]{2,1,0:T(8,128)(2,1)S(1)} %get-tuple-element.74.refs_0_, bf16[16,64,128]{2,1,0:T(8,128)(2,1)S(1)} %collective-permute-done.10.refs_1_, bf16[16,64,128]{2,1,0:T(8,128)(2,1)S(1)} %collective-permute-done.11.refs_2_, ...), custom_call_target="tpu_custom_call" | custom-call | flops 1310720 | bytes 2621440 | tf_op jit(solution)/shard_map/scale/pallas_call | solution.py:471
  110.9 0.1 collective-permute-done.16.refs_3_
  111.0 1.1 scale.3
  (21 shorter events, 0.2 us)
Async XLA Ops:
  2.9 12.1 %copy-start = (f32[16,64,128]{2,1,0:T(8,128)S(1)}, f32[16,64,128]{2,1,0:T(8,128)}, u32[]{:S(2)}) copy-start(f32[16,64,128]{2,1,0:T(8,128)} %cond.1) | copy-start | bytes 1572868
  2.9 12.1 %copy-start.1 = (s32[8192,1]{0,1:T(1,128)S(1)}, s32[8192,1]{0,1:T(1,128)}, u32[]{:S(2)}) copy-start(s32[8192,1]{0,1:T(1,128)} %param.9) | copy-start | bytes 98308
  2.9 12.1 %copy-start.2 = (s32[8192]{0:T(1024)S(1)}, s32[8192]{0:T(1024)}, u32[]{:S(2)}) copy-start(s32[8192]{0:T(1024)} %param.10) | copy-start | bytes 98308
  2.9 60.5 %all-to-all-start = ((bf16[32,256,128]{2,1,0:T(8,128)(2,1)}), bf16[32,256,128]{2,1,0:T(8,128)(2,1)S(1)}, u32[]{:S(2)}, u32[]{:S(2)}) async-start(bf16[32,256,128]{2,1,0:T(8,128)(2,1)} %bitcast.15), calls=%async_computation | async-start | bytes 4194304 | tf_op jit(solution)/shard_map/all_to_all | solution.py:502
  15.7 2.1 %collective-permute-start = (f32[4,64,128]{2,1,0:T(8,128)S(1)}, f32[4,64,128]{2,1,0:T(8,128)S(1)}, u32[]{:S(2)}, u32[]{:S(2)}) collective-permute-start(f32[4,64,128]{2,1,0:T(8,128)S(1)} %get-tuple-element.51), channel_id=1, source_target_pairs={{0,32},{32,0},{64,96},{96,64},{128,160},{160,128},{192,224},{224,1... | collective-permute-start | bytes 393224 | tf_op jit(solution)/shard_map/ppermute | solution.py:507
  16.6 4.7 %collective-permute-start.1 = (f32[4,64,128]{2,1,0:T(8,128)S(1)}, f32[4,64,128]{2,1,0:T(8,128)S(1)}, u32[]{:S(2)}, u32[]{:S(2)}) collective-permute-start(f32[4,64,128]{2,1,0:T(8,128)S(1)} %get-tuple-element.52), channel_id=1, source_target_pairs={{0,224},{32,64},{64,32},{96,128},{128,96},{160,192},{192,160},{224... | collective-permute-start | bytes 393224 | tf_op jit(solution)/shard_map/ppermute | solution.py:506
  21.3 8.0 %collective-permute-start.2 = (f32[12,8,128]{2,1,0:T(8,128)S(1)}, f32[12,8,128]{2,1,0:T(8,128)S(1)}, u32[]{:S(2)}, u32[]{:S(2)}) collective-permute-start(f32[12,8,128]{2,1,0:T(8,128)S(1)} %get-tuple-element.53), channel_id=1, source_target_pairs={{0,1},{1,0},{2,3},{3,2},{4,5},{5,4},{6,7},{7,6},{8,9},{9,8},{10,11... | collective-permute-start | bytes 147464 | tf_op jit(solution)/shard_map/ppermute | solution.py:509
  22.9 40.3 %collective-permute-start.3 = (f32[12,8,128]{2,1,0:T(8,128)S(1)}, f32[12,8,128]{2,1,0:T(8,128)S(1)}, u32[]{:S(2)}, u32[]{:S(2)}) collective-permute-start(f32[12,8,128]{2,1,0:T(8,128)S(1)} %get-tuple-element.54), channel_id=1, source_target_pairs={{0,31},{1,2},{2,1},{3,4},{4,3},{5,6},{6,5},{7,8},{8,7},{9,10},{10,... | collective-permute-start | bytes 147464 | tf_op jit(solution)/shard_map/ppermute | solution.py:510
  64.4 5.6 %collective-permute-start.4 = (f32[4,64,128]{2,1,0:T(8,128)S(1)}, f32[4,64,128]{2,1,0:T(8,128)S(1)}, u32[]{:S(2)}, u32[]{:S(2)}) collective-permute-start(f32[4,64,128]{2,1,0:T(8,128)S(1)} %get-tuple-element.65), channel_id=1, source_target_pairs={{0,32},{32,0},{64,96},{96,64},{128,160},{160,128},{192,224},{224,1... | collective-permute-start | bytes 393224 | tf_op jit(solution)/shard_map/ppermute | solution.py:516
  67.1 4.7 %collective-permute-start.5 = (f32[4,64,128]{2,1,0:T(8,128)S(1)}, f32[4,64,128]{2,1,0:T(8,128)S(1)}, u32[]{:S(2)}, u32[]{:S(2)}) collective-permute-start(f32[4,64,128]{2,1,0:T(8,128)S(1)} %get-tuple-element.66), channel_id=1, source_target_pairs={{0,224},{32,64},{64,32},{96,128},{128,96},{160,192},{192,160},{224... | collective-permute-start | bytes 393224 | tf_op jit(solution)/shard_map/ppermute | solution.py:515
  68.4 7.3 %collective-permute-start.6 = (f32[8,8,128]{2,1,0:T(8,128)S(1)}, f32[8,8,128]{2,1,0:T(8,128)S(1)}, u32[]{:S(2)}, u32[]{:S(2)}) collective-permute-start(f32[8,8,128]{2,1,0:T(8,128)S(1)} %get-tuple-element.67), channel_id=1, source_target_pairs={{0,1},{1,0},{2,3},{3,2},{4,5},{5,4},{6,7},{7,6},{8,9},{9,8},{10,11... | collective-permute-start | bytes 98312 | tf_op jit(solution)/shard_map/ppermute | solution.py:517
  69.0 6.8 %collective-permute-start.7 = (f32[8,8,128]{2,1,0:T(8,128)S(1)}, f32[8,8,128]{2,1,0:T(8,128)S(1)}, u32[]{:S(2)}, u32[]{:S(2)}) collective-permute-start(f32[8,8,128]{2,1,0:T(8,128)S(1)} %get-tuple-element.68), channel_id=1, source_target_pairs={{0,31},{1,2},{2,1},{3,4},{4,3},{5,6},{6,5},{7,8},{8,7},{9,10},{10,... | collective-permute-start | bytes 98312 | tf_op jit(solution)/shard_map/ppermute | solution.py:518
  71.8 3.9 %collective-permute-start.8 = (f32[4,8,128]{2,1,0:T(8,128)S(1)}, f32[4,8,128]{2,1,0:T(8,128)S(1)}, u32[]{:S(2)}, u32[]{:S(2)}) collective-permute-start(f32[4,8,128]{2,1,0:T(8,128)S(1)} %get-tuple-element.69), channel_id=1, source_target_pairs={{0,1},{1,0},{2,3},{3,2},{4,5},{5,4},{6,7},{7,6},{8,9},{9,8},{10,11... | collective-permute-start | bytes 49160 | tf_op jit(solution)/shard_map/ppermute | solution.py:521
  72.5 5.9 %collective-permute-start.9 = (f32[4,8,128]{2,1,0:T(8,128)S(1)}, f32[4,8,128]{2,1,0:T(8,128)S(1)}, u32[]{:S(2)}, u32[]{:S(2)}) collective-permute-start(f32[4,8,128]{2,1,0:T(8,128)S(1)} %get-tuple-element.70), channel_id=1, source_target_pairs={{0,31},{1,2},{2,1},{3,4},{4,3},{5,6},{6,5},{7,8},{8,7},{9,10},{10,... | collective-permute-start | bytes 49160 | tf_op jit(solution)/shard_map/ppermute | solution.py:522
  81.9 4.9 %collective-permute-start.12 = (bf16[16,64,128]{2,1,0:T(8,128)(2,1)S(1)}, bf16[16,64,128]{2,1,0:T(8,128)(2,1)S(1)}, u32[]{:S(2)}, u32[]{:S(2)}) collective-permute-start(bf16[16,64,128]{2,1,0:T(8,128)(2,1)S(1)} %get-tuple-element.74.refs_0_), channel_id=1, source_target_pairs={{0,32},{32,0},{64,96},{96,64},{128,160},{160,128},{192,224},{224,1... | collective-permute-start | bytes 786440 | tf_op jit(solution)/shard_map/ppermute | solution.py:527
  85.3 22.9 %collective-permute-start.11 = (bf16[16,64,128]{2,1,0:T(8,128)(2,1)S(1)}, bf16[16,64,128]{2,1,0:T(8,128)(2,1)S(1)}, u32[]{:S(2)}, u32[]{:S(2)}) collective-permute-start(bf16[16,64,128]{2,1,0:T(8,128)(2,1)S(1)} %get-tuple-element.74.refs_0_), channel_id=1, source_target_pairs={{0,192},{32,224},{64,0},{96,32},{128,64},{160,96},{192,128},{224,1... | collective-permute-start | bytes 786440 | tf_op jit(solution)/shard_map/ppermute | solution.py:526
  86.0 22.2 %collective-permute-start.10 = (bf16[16,64,128]{2,1,0:T(8,128)(2,1)S(1)}, bf16[16,64,128]{2,1,0:T(8,128)(2,1)S(1)}, u32[]{:S(2)}, u32[]{:S(2)}) collective-permute-start(bf16[16,64,128]{2,1,0:T(8,128)(2,1)S(1)} %get-tuple-element.74.refs_0_), channel_id=1, source_target_pairs={{0,64},{32,96},{64,128},{96,160},{128,192},{160,224},{192,0},{224,... | collective-permute-start | bytes 786440 | tf_op jit(solution)/shard_map/ppermute | solution.py:525
  86.8 21.5 %collective-permute-start.13 = (bf16[16,64,128]{2,1,0:T(8,128)(2,1)S(1)}, bf16[16,64,128]{2,1,0:T(8,128)(2,1)S(1)}, u32[]{:S(2)}, u32[]{:S(2)}) collective-permute-start(bf16[16,64,128]{2,1,0:T(8,128)(2,1)S(1)} %get-tuple-element.74.refs_0_), channel_id=1, source_target_pairs={{0,128},{32,160},{64,192},{96,224},{128,0},{160,32},{192,64},{224,... | collective-permute-start | bytes 786440 | tf_op jit(solution)/shard_map/ppermute | solution.py:529
  108.2 2.6 %collective-permute-start.14 = (bf16[16,64,128]{2,1,0:T(8,128)(2,1)S(1)}, bf16[16,64,128]{2,1,0:T(8,128)(2,1)S(1)}, u32[]{:S(2)}, u32[]{:S(2)}) collective-permute-start(bf16[16,64,128]{2,1,0:T(8,128)(2,1)S(1)} %collective-permute-done.10.refs_1_), channel_id=1, source_target_pairs={{0,32},{32,0},{64,96},{96,64},{128,160},{160,128},{192,224},{224,1... | collective-permute-start | bytes 786440 | tf_op jit(solution)/shard_map/ppermute | solution.py:532
  109.1 1.8 %collective-permute-start.15 = (bf16[16,64,128]{2,1,0:T(8,128)(2,1)S(1)}, bf16[16,64,128]{2,1,0:T(8,128)(2,1)S(1)}, u32[]{:S(2)}, u32[]{:S(2)}) collective-permute-start(bf16[16,64,128]{2,1,0:T(8,128)(2,1)S(1)} %collective-permute-done.11.refs_2_), channel_id=1, source_target_pairs={{0,32},{32,0},{64,96},{96,64},{128,160},{160,128},{192,224},{224,1... | collective-permute-start | bytes 786440 | tf_op jit(solution)/shard_map/ppermute | solution.py:532
  109.2 1.8 %collective-permute-start.16 = (bf16[16,64,128]{2,1,0:T(8,128)(2,1)S(1)}, bf16[16,64,128]{2,1,0:T(8,128)(2,1)S(1)}, u32[]{:S(2)}, u32[]{:S(2)}) collective-permute-start(bf16[16,64,128]{2,1,0:T(8,128)(2,1)S(1)} %collective-permute-done.13.refs_3_), channel_id=1, source_target_pairs={{0,32},{32,0},{64,96},{96,64},{128,160},{160,128},{192,224},{224,1... | collective-permute-start | bytes 786440 | tf_op jit(solution)/shard_map/ppermute | solution.py:532
